TPU v7x, 128 devices: a whole 4x4x4 slice. The times are simulated.
128 devices in a mesh: blk: 16 (over y, z_hi, core), uly: 8 (over z_lo, x).
Axes of the slice: x: 4, y: 4, z: 4 (z_hi: 2, z_lo: 2; z = z_hi * 2 + z_lo), core: 2. Of those that a mesh axis runs over, the one named last changes fastest.
Arguments:
- queries: bfloat16 [16384, 8192], P(('blk', 'uly')), may hold values from -4 to 4, as said below
- key_rows: bfloat16 [16384, 1024], P(('blk', 'uly')), may hold values from -4 to 4, as said below
- value_rows: bfloat16 [16384, 1024], P(('blk', 'uly')), may hold values from -6 to 6
- grad_out: bfloat16 [16384, 8192], P(('blk', 'uly')), may hold values from -6 to 6
- attn_out: bfloat16 [16384, 8192], P(('blk', 'uly')), may hold values from -1.796875 to 1.796875
- log_norm: float32 [16384, 64], P(('blk', 'uly')), may hold values from 5.5 to 8.5
- doc_ids: int32 [16384], replicated, may hold values from 0 to 7, never falling along the last dimension, each value on 1 to 16128 neighbouring positions
Outputs:
- grad_queries: bfloat16 [16384, 8192], P(('blk', 'uly'))
- grad_keys: bfloat16 [16384, 1024], P(('blk', 'uly'))
- grad_values: bfloat16 [16384, 1024], P(('blk', 'uly'))
Inputs may be any that keep to these rules, and one draw needn't show every extreme that they name: `queries`: entries of order one. `key_rows`: entries of order one. `doc_ids`: document numbers never fall along positions; a document holds 1 to 16128 positions.
All inputs are finite; a program needn't handle non-finite values.
Results may differ from a plain program's by a relative error of at most 0.0051.
Values may be sent and summed in bfloat16 or wider, within the bound.
No kernel may reach another device: no remote copies, remote signals or barrier semaphores. Data moves between devices by JAX's collectives and lax.ppermute only.
A program may use at most 192 MiB of HBM per device.

v0:
```python
import jax
import jax.numpy as jnp
from jax import lax
from jax.sharding import PartitionSpec as P

HD = 128
STEPS = 4


def from_behind(value, axis, steps):
    count = lax.axis_size(axis)
    pairs = [(source, (source + steps) % count) for source in range(count)]
    return lax.ppermute(value, axis, pairs)


def take_half(array, half_index, half_len, axis_pos):
    return lax.dynamic_slice_in_dim(array, half_index * half_len, half_len, axis_pos)


def add_half(running, half_index, half_len, update, axis_pos):
    start_row = half_index * half_len
    current = lax.dynamic_slice_in_dim(running, start_row, half_len, axis_pos)
    return lax.dynamic_update_slice_in_dim(running, current + update, start_row, axis_pos)


def block_layout(group_index, half_index, group_count, half_len, doc_ids):
    first_row = jnp.where(
        half_index == 0, group_index * half_len, (2 * group_count - 1 - group_index) * half_len
    )
    positions = first_row + jnp.arange(half_len, dtype=jnp.int32)
    return (positions, lax.dynamic_slice_in_dim(doc_ids, first_row, half_len))


def tile_grads(query_tile, grad_tile, norm_tile, delta_tile, key_tile, value_tile, allowed):
    softmax_scale = HD ** (-0.5)
    scores = (
        jnp.einsum("qcgh,kch->cgqk", query_tile, key_tile, preferred_element_type=jnp.float32)
        * softmax_scale
    )
    norm_t = jnp.transpose(norm_tile, (1, 2, 0))[..., None]
    delta_t = jnp.transpose(delta_tile, (1, 2, 0))[..., None]
    attn_prob = jnp.where(allowed, jnp.exp(scores - norm_t), 0.0)
    prob_low = attn_prob.astype(jnp.bfloat16)
    value_part = jnp.einsum(
        "cgqk,qcgh->kch", prob_low, grad_tile, preferred_element_type=jnp.float32
    )
    grad_prob = jnp.einsum(
        "qcgh,kch->cgqk", grad_tile, value_tile, preferred_element_type=jnp.float32
    )
    score_low = (attn_prob * (grad_prob - delta_t)).astype(jnp.bfloat16)
    query_part = softmax_scale * jnp.einsum(
        "cgqk,kch->qcgh", score_low, key_tile, preferred_element_type=jnp.float32
    )
    key_part = softmax_scale * jnp.einsum(
        "cgqk,qcgh->kch", score_low, query_tile, preferred_element_type=jnp.float32
    )
    return (query_part, key_part, value_part)


def move_pair(pair_acc, offset):
    return from_behind(pair_acc, "blk", offset)


def local(queries, key_rows, value_rows, grad_out, attn_out, log_norm, doc_ids):
    uly_count = lax.axis_size("uly")
    blk_count = lax.axis_size("blk")
    tok_rows = queries.shape[0]
    head_count = log_norm.shape[1]
    kv_count = key_rows.shape[1] // HD
    head_dev = head_count // uly_count
    kv_dev = kv_count // uly_count
    group_size = head_count // kv_count
    group_rows = tok_rows * uly_count
    half_len = group_rows // 2
    delta = jnp.sum(
        grad_out.reshape(tok_rows, head_count, HD).astype(jnp.float32)
        * attn_out.reshape(tok_rows, head_count, HD).astype(jnp.float32),
        axis=-1,
    )
    query_x, grad_x, key_x, value_x = (
        lax.all_to_all(
            queries.reshape(tok_rows, uly_count, head_dev * HD),
            "uly",
            split_axis=1,
            concat_axis=0,
            tiled=True,
        ),
        lax.all_to_all(
            grad_out.reshape(tok_rows, uly_count, head_dev * HD),
            "uly",
            split_axis=1,
            concat_axis=0,
            tiled=True,
        ),
        lax.all_to_all(
            key_rows.reshape(tok_rows, uly_count, kv_dev * HD),
            "uly",
            split_axis=1,
            concat_axis=0,
            tiled=True,
        ),
        lax.all_to_all(
            value_rows.reshape(tok_rows, uly_count, kv_dev * HD),
            "uly",
            split_axis=1,
            concat_axis=0,
            tiled=True,
        ),
    )
    norm_x, delta_x = (
        lax.all_to_all(
            log_norm.reshape(tok_rows, uly_count, head_dev),
            "uly",
            split_axis=1,
            concat_axis=0,
            tiled=True,
        ),
        lax.all_to_all(
            delta.reshape(tok_rows, uly_count, head_dev),
            "uly",
            split_axis=1,
            concat_axis=0,
            tiled=True,
        ),
    )
    query_x = query_x.reshape(group_rows, kv_dev, group_size, HD)
    grad_x = grad_x.reshape(group_rows, kv_dev, group_size, HD)
    visiting = jnp.stack([key_x, value_x])
    group_index = lax.axis_index("blk")
    grad_query = jnp.zeros((group_rows, kv_dev, group_size, HD), jnp.float32)
    zero_pair = jnp.zeros((2, group_rows, kv_dev, HD), jnp.float32)
    riding = zero_pair
    for visit_step in range(STEPS):
        key_group = (group_index - visit_step) % blk_count
        if visit_step == 0:
            tile_list = [(0, 0), (1, 0), (1, 1)]
        else:
            second = jnp.where(group_index >= visit_step, 0, 1).astype(jnp.int32)
            tile_list = [(1, 0), (second, second)]
        for query_half, key_half in tile_list:
            tile_grad_query = grad_query
            pair_acc = riding
            query_spots, query_docs = block_layout(
                group_index, query_half, blk_count, half_len, doc_ids
            )
            key_spots, key_docs = block_layout(key_group, key_half, blk_count, half_len, doc_ids)
            allowed = (query_spots[:, None] >= key_spots[None, :]) & (
                query_docs[:, None] == key_docs[None, :]
            )
            results = tile_grads(
                take_half(query_x, query_half, half_len, 0),
                take_half(grad_x, query_half, half_len, 0),
                take_half(norm_x, query_half, half_len, 0),
                take_half(delta_x, query_half, half_len, 0),
                take_half(visiting[0], key_half, half_len, 0),
                take_half(visiting[1], key_half, half_len, 0),
                allowed,
            )
            tile_grad_query = add_half(tile_grad_query, query_half, half_len, results[0], 0)
            pair_acc = add_half(
                pair_acc, key_half, half_len, jnp.stack([results[1], results[2]]), 1
            )
            grad_query = tile_grad_query
            riding = pair_acc
        if visit_step + 1 < STEPS:
            visiting = from_behind(visiting, "blk", 1)
            riding = move_pair(riding, 1)
    owned = move_pair(riding, 1 - STEPS)
    grad_pair = owned.astype(jnp.bfloat16)
    back_query, back_key, back_value = (
        lax.all_to_all(
            grad_query.astype(jnp.bfloat16).reshape(group_rows, 1, head_dev * HD),
            "uly",
            split_axis=0,
            concat_axis=1,
            tiled=True,
        ),
        lax.all_to_all(grad_pair[0], "uly", split_axis=0, concat_axis=1, tiled=True),
        lax.all_to_all(grad_pair[1], "uly", split_axis=0, concat_axis=1, tiled=True),
    )
    return (
        back_query.reshape(tok_rows, head_count * HD),
        back_key.reshape(tok_rows, kv_count * HD),
        back_value.reshape(tok_rows, kv_count * HD),
    )


def solution(mesh):
    return jax.shard_map(
        local,
        mesh=mesh,
        in_specs=(
            P(("blk", "uly"), None),
            P(("blk", "uly"), None),
            P(("blk", "uly"), None),
            P(("blk", "uly"), None),
            P(("blk", "uly"), None),
            P(("blk", "uly"), None),
            P(),
        ),
        out_specs=(P(("blk", "uly"), None), P(("blk", "uly"), None), P(("blk", "uly"), None)),
        check_vma=False,
    )
```

profile of v0, /device:TPU:90, one launch (start us, length us, event | category | flops | bytes accessed | tf_op | source)
XLA Modules:
  0.0 363.7 jit_solution(2889035350331000404)
XLA Ops:
  0.6 6.0 %all-to-all-start.2 = ((f32[128,8,8]{0,2,1:T(8,128)}), f32[128,8,8]{0,2,1:T(8,128)S(1)}, u32[]{:S(2)}, u32[]{:S(2)}) async-start(f32[128,8,8]{0,2,1:T(8,128)} %bitcast.935), calls=%async_computation.2 | async-start | bytes 65536 | tf_op jit(solution)/shard_map/all_to_all | solution.py:111
  7.4 4.7 %multiply_bitcast_fusion = f32[16,8,64,128]{3,1,2,0:T(8,128)} fusion(bf16[128,8192]{1,0:T(8,128)(2,1)} %param.11, bf16[128,8192]{1,0:T(8,128)(2,1)} %param.10), kind=kLoop, calls=%fused_computation.82 | loop fusion | flops 3145728 | bytes 8388608
  12.2 4.9 %copy.559 = f32[16,8,64,128]{3,2,1,0:T(8,128)} copy(f32[16,8,64,128]{3,1,2,0:T(8,128)} %multiply_bitcast_fusion) | data formatting | bytes 8388608
  21.3 5.7 %all-to-all-start.5 = ((f32[128,8,8]{0,2,1:T(8,128)}), f32[128,8,8]{0,2,1:T(8,128)S(1)}, u32[]{:S(2)}, u32[]{:S(2)}) async-start(f32[128,8,8]{0,2,1:T(8,128)} %bitcast.22), calls=%async_computation.5 | async-start | bytes 65536 | tf_op jit(solution)/shard_map/all_to_all | solution.py:118
  27.0 4.9 %all-to-all-done.5 = f32[128,8,8]{0,2,1:T(8,128)S(1)} async-done(((f32[128,8,8]{0,2,1:T(8,128)}), f32[128,8,8]{0,2,1:T(8,128)S(1)}, u32[]{:S(2)}, u32[]{:S(2)}) %all-to-all-start.5) | async-done | bytes 32800 | tf_op jit(solution)/shard_map/all_to_all | solution.py:118
  31.9 4.7 %all-to-all-start = ((bf16[128,8,128]{2,0,1:T(8,128)(2,1)}), bf16[128,8,128]{2,0,1:T(8,128)(2,1)S(1)}, u32[]{:S(2)}, u32[]{:S(2)}) async-start(bf16[128,8,128]{2,0,1:T(8,128)(2,1)} %copy_bitcast_fusion.3), calls=%async_computation | async-start | bytes 524288 | tf_op jit(solution)/shard_map/all_to_all | solution.py:95
  37.3 5.4 %all-to-all-done = bf16[128,8,128]{2,0,1:T(8,128)(2,1)S(1)} async-done(((bf16[128,8,128]{2,0,1:T(8,128)(2,1)}), bf16[128,8,128]{2,0,1:T(8,128)(2,1)S(1)}, u32[]{:S(2)}, u32[]{:S(2)}) %all-to-all-start) | async-done | bytes 262176 | tf_op jit(solution)/shard_map/all_to_all | solution.py:95
  42.7 4.5 %all-to-all-start.3 = ((bf16[128,8,128]{2,0,1:T(8,128)(2,1)}), bf16[128,8,128]{2,0,1:T(8,128)(2,1)S(1)}, u32[]{:S(2)}, u32[]{:S(2)}) async-start(bf16[128,8,128]{2,0,1:T(8,128)(2,1)} %copy_bitcast_fusion.2), calls=%async_computation.3 | async-start | bytes 524288 | tf_op jit(solution)/shard_map/all_to_all | solution.py:102
  53.4 4.7 %all-to-all-start.4 = ((bf16[128,8,1024]{2,0,1:T(8,128)(2,1)}), bf16[128,8,1024]{2,0,1:T(8,128)(2,1)S(1)}, u32[]{:S(2)}, u32[]{:S(2)}) async-start(bf16[128,8,1024]{2,0,1:T(8,128)(2,1)} %bitcast.885), calls=%async_computation.4 | async-start | bytes 4194304 | tf_op jit(solution)/shard_map/all_to_all | solution.py:88
  65.9 17.7 %collective-permute-done = bf16[2,1024,1,128]{3,1,2,0:T(8,128)(2,1)S(1)} collective-permute-done((bf16[2,1024,1,128]{3,1,2,0:T(8,128)(2,1)S(1)}, bf16[2,1024,1,128]{3,1,2,0:T(8,128)(2,1)S(1)}, u32[]{:S(2)}, u32[]{:S(2)}) %collective-permute-start) | collective-permute-done | bytes 524320 | tf_op jit(solution)/shard_map/ppermute | solution.py:13
  85.1 8.6 %all-to-all-start.1 = ((bf16[128,8,1024]{2,0,1:T(8,128)(2,1)}), bf16[128,8,1024]{2,0,1:T(8,128)(2,1)}, u32[]{:S(2)}, u32[]{:S(2)}) async-start(bf16[128,8,1024]{2,0,1:T(8,128)(2,1)} %bitcast.884), calls=%async_computation.1 | async-start | bytes 4194304 | tf_op jit(solution)/shard_map/all_to_all | solution.py:81
  95.6 14.6 %collective-permute-done.1 = bf16[2,1024,1,128]{3,1,2,0:T(8,128)(2,1)} collective-permute-done((bf16[2,1024,1,128]{3,1,2,0:T(8,128)(2,1)S(1)}, bf16[2,1024,1,128]{3,1,2,0:T(8,128)(2,1)}, u32[]{:S(2)}, u32[]{:S(2)}) %collective-permute-start.1) | collective-permute-done | bytes 524320 | tf_op jit(solution)/shard_map/ppermute | solution.py:13
  113.4 8.4 %collective-permute-done.2 = bf16[2,1024,1,128]{3,1,2,0:T(8,128)(2,1)S(1)} collective-permute-done((bf16[2,1024,1,128]{3,1,2,0:T(8,128)(2,1)}, bf16[2,1024,1,128]{3,1,2,0:T(8,128)(2,1)S(1)}, u32[]{:S(2)}, u32[]{:S(2)}) %collective-permute-start.2) | collective-permute-done | bytes 524320 | tf_op jit(solution)/shard_map/ppermute | solution.py:13
  171.4 4.0 %fusion.59 = bf16[8,512,512]{1,2,0:T(8,128)(2,1)S(1)} fusion(f32[512,512,8]{1,0,2:T(8,128)S(1)} %fusion.188, f32[8,512]{1,0:T(8,128)S(1)} %copy-done.60, f32[8,512]{1,0:T(8,128)S(1)} %copy-done.59, pred[512,512]{0,1:T(8,128)(4,1)S(1)} %copy-done.32, bf16[2,1024,1,128]{3,1,2,0:T(8,128)(2,1)} %collective-permute-done.1, bf16[512,8,128]{2,1,0:T(8,128)(2,1)S(1)} %bitcast.918), kind=kOutput, calls=%fused_computation.77 | convolution fusion | flops 549453824 | bytes 14057472 | tf_op jit(solution)/shard_map/qcgh,kch->cgqk/dot_general | solution.py:47
  195.8 4.6 %fusion.154 = f32[512,512,8]{1,0,2:T(8,128)} fusion(bf16[512,1,8,128]{3,2,0,1:T(8,128)(2,1)S(1)} %copy-done.16, bf16[1,1024,1,128]{3,1,2,0:T(8,128)(2,1)S(1)} %copy-done.23, s32[]{:T(128)S(6)} %select_n.180), kind=kOutput, calls=%fused_computation.167 | convolution fusion | flops 536870912 | bytes 9568260 | tf_op jit(solution)/shard_map/qcgh,kch->cgqk/dot_general | solution.py:37
  200.4 8.6 %fusion.58 = bf16[8,512,512]{1,2,0:T(8,128)(2,1)} fusion(f32[512,512,8]{1,0,2:T(8,128)} %fusion.154, f32[8,512]{1,0:T(8,128)S(1)} %copy-done.58, f32[8,512]{1,0:T(8,128)S(1)} %copy-done.55, pred[512,512]{0,1:T(8,128)(4,1)S(1)} %copy-done.42, bf16[512,1,8,128]{3,2,0,1:T(8,128)(2,1)S(1)} %copy-done.29, bf16[1,1024,1,128]{3,1,2,0:T(8,128)(2,1)S(1)} %copy-done.50, ...), kind=kOutput, calls=%fused_computation.76 | convolution fusion | flops 549453824 | bytes 14057476 | tf_op jit(solution)/shard_map/qcgh,kch->cgqk/dot_general | solution.py:47
  209.0 4.1 %fusion.95 = f32[1024,1,8,128]{3,0,2,1:T(8,128)S(1)} fusion(f32[1024,1,8,128]{3,0,2,1:T(8,128)S(1)} %get-tuple-element.66, f32[512,1,8,128]{3,0,2,1:T(8,128)S(1)} %get-tuple-element.67, bf16[8,512,512]{1,2,0:T(8,128)(2,1)} %copy-done.12, bf16[2,1024,1,128]{3,1,2,0:T(8,128)(2,1)S(1)} %copy-done.18), kind=kOutput, calls=%fused_computation.114 | convolution fusion | flops 537919488 | bytes 8519680 | tf_op jit(solution)/shard_map/cgqk,kch->qcgh/dot_general | solution.py:51
  218.4 6.3 %fusion.91 = f32[1024,1,8,128]{3,0,2,1:T(8,128)S(1)} fusion(f32[1024,1,8,128]{3,0,2,1:T(8,128)S(1)} %fusion.94, bf16[8,512,512]{1,2,0:T(8,128)(2,1)} %copy-done.11, bf16[2,1024,1,128]{3,1,2,0:T(8,128)(2,1)} %collective-permute-done.1), kind=kOutput, calls=%fused_computation.106 | convolution fusion | flops 537919488 | bytes 8519680 | tf_op jit(solution)/shard_map/cgqk,kch->qcgh/dot_general | solution.py:51
  230.2 3.6 %fusion.90 = f32[1024,1,8,128]{3,0,2,1:T(8,128)S(1)} fusion(f32[1024,1,8,128]{3,0,2,1:T(8,128)S(1)} %fusion.93, bf16[8,512,512]{1,2,0:T(8,128)(2,1)S(1)} %copy-done.8, bf16[2,1024,1,128]{3,1,2,0:T(8,128)(2,1)} %copy-done.19), kind=kOutput, calls=%fused_computation.104 | convolution fusion | flops 537919488 | bytes 8519680 | tf_op jit(solution)/shard_map/cgqk,kch->qcgh/dot_general | solution.py:51
  239.4 3.9 %reduce = bf16[1024,1024]{0,1:T(8,128)(2,1)S(1)} reduce(bf16[1024,1,1024]{0,2,1:T(8,128)(2,1)} %bitcast.886, bf16[]{:T(256)} %broadcast.265), dimensions={1}, to_apply=%copy.442.reduce_sub_computation | reduce | bytes 4194306 | tf_op jit(solution)/shard_map/reshape | solution.py:172
  245.8 6.3 %reshape.667 = bf16[8,2,65536]{2,1,0:T(2,128)(2,1)} reshape(bf16[1024,1024]{1,0:T(8,128)(2,1)} %copy.654) | data formatting | bytes 4194304
  252.1 7.8 %all-to-all-start.6 = ((bf16[8,2,65536]{2,1,0:T(2,128)(2,1)}), bf16[8,2,65536]{2,1,0:T(2,128)(2,1)S(1)}, u32[]{:S(2)}, u32[]{:S(2)}) async-start(bf16[8,2,65536]{2,1,0:T(2,128)(2,1)} %reshape.667), calls=%async_computation.6 | async-start | bytes 4194304 | tf_op jit(solution)/shard_map/all_to_all | solution.py:171
  259.9 3.8 %fusion.107 = f32[1,512,1,128]{3,1,2,0:T(8,128)S(1)} fusion(bf16[8,512,512]{1,2,0:T(8,128)(2,1)} %fusion.58, bf16[512,8,128]{2,1,0:T(8,128)(2,1)} %bitcast.893), kind=kOutput, calls=%fused_computation.138 | convolution fusion | flops 536936448 | bytes 5505024 | tf_op jit(solution)/shard_map/cgqk,qcgh->kch/dot_general | solution.py:54
  263.8 5.1 %fusion.126 = f32[1,512,1,128]{3,1,2,0:T(8,128)S(1)} fusion(f32[512,512,8]{1,0,2:T(8,128)} %fusion.154, f32[8,512]{1,0:T(8,128)S(1)} %copy-done.55, pred[512,512]{0,1:T(8,128)(4,1)S(1)} %copy-done.43, bf16[512,8,128]{2,1,0:T(8,128)(2,1)S(1)} %bitcast.927), kind=kOutput, calls=%fused_computation.149 | convolution fusion | flops 545259520 | bytes 9977856 | tf_op jit(solution)/shard_map/cgqk,qcgh->kch/dot_general | solution.py:44
  276.9 18.3 %collective-permute-done.4 = f32[2,1024,1,128]{3,1,2,0:T(8,128)S(1)} collective-permute-done((f32[2,1024,1,128]{3,1,2,0:T(8,128)}, f32[2,1024,1,128]{3,1,2,0:T(8,128)S(1)}, u32[]{:S(2)}, u32[]{:S(2)}) %collective-permute-start.4) | collective-permute-done | bytes 1048608 | tf_op jit(solution)/shard_map/ppermute | solution.py:13
  298.4 12.8 %collective-permute-done.5 = f32[2,1024,1,128]{3,1,2,0:T(8,128)S(1)} collective-permute-done((f32[2,1024,1,128]{3,1,2,0:T(8,128)S(1)}, f32[2,1024,1,128]{3,1,2,0:T(8,128)S(1)}, u32[]{:S(2)}, u32[]{:S(2)}) %collective-permute-start.5) | collective-permute-done | bytes 1048608 | tf_op jit(solution)/shard_map/ppermute | solution.py:13
  311.5 17.5 %collective-permute-done.6 = bf16[2,1024,1,128]{3,1,2,0:T(8,128)(2,1)S(1)} collective-permute-done((bf16[2,1024,1,128]{3,1,2,0:T(8,128)(2,1)S(1)}, bf16[2,1024,1,128]{3,1,2,0:T(8,128)(2,1)S(1)}, u32[]{:S(2)}, u32[]{:S(2)}) %collective-permute-start.6) | collective-permute-done | bytes 524320 | tf_op jit(solution)/shard_map/ppermute | solution.py:13
  330.6 4.4 %all-to-all-start.7 = ((bf16[8,2,8192]{2,1,0:T(2,128)(2,1)}), bf16[8,2,8192]{2,1,0:T(2,128)(2,1)S(1)}, u32[]{:S(2)}, u32[]{:S(2)}) async-start(bf16[8,2,8192]{2,1,0:T(2,128)(2,1)} %reshape.669), calls=%async_computation.7 | async-start | bytes 524288 | tf_op jit(solution)/shard_map/all_to_all | solution.py:178
  336.6 5.6 %all-to-all-done.7 = bf16[8,2,8192]{2,1,0:T(2,128)(2,1)S(1)} async-done(((bf16[8,2,8192]{2,1,0:T(2,128)(2,1)}), bf16[8,2,8192]{2,1,0:T(2,128)(2,1)S(1)}, u32[]{:S(2)}, u32[]{:S(2)}) %all-to-all-start.7) | async-done | bytes 262176 | tf_op jit(solution)/shard_map/all_to_all | solution.py:178
  342.2 4.5 %all-to-all-start.8 = ((bf16[8,2,8192]{2,1,0:T(2,128)(2,1)}), bf16[8,2,8192]{2,1,0:T(2,128)(2,1)S(1)}, u32[]{:S(2)}, u32[]{:S(2)}) async-start(bf16[8,2,8192]{2,1,0:T(2,128)(2,1)} %reshape.671), calls=%async_computation.8 | async-start | bytes 524288 | tf_op jit(solution)/shard_map/all_to_all | solution.py:179
  346.7 4.4 %reshape.668 = bf16[1024,1,1024]{2,1,0:T(2,128)(2,1)} reshape(bf16[8,2,65536]{2,1,0:T(2,128)(2,1)S(1)} %all-to-all-done.6) | data formatting | bytes 4194304
  356.4 4.1 %copy.478 = bf16[128,8192]{1,0:T(8,128)(2,1)} copy(bf16[128,8192]{0,1:T(8,128)(2,1)} %bitcast.887) | data formatting | bytes 4194304
  (255 shorter events, 136.7 us)
Async XLA Ops:
  0.6 20.7 %all-to-all-start.2 = ((f32[128,8,8]{0,2,1:T(8,128)}), f32[128,8,8]{0,2,1:T(8,128)S(1)}, u32[]{:S(2)}, u32[]{:S(2)}) async-start(f32[128,8,8]{0,2,1:T(8,128)} %bitcast.935), calls=%async_computation.2 | async-start | bytes 65536 | tf_op jit(solution)/shard_map/all_to_all | solution.py:111
  17.1 19.5 %copy-start.37 = (bf16[128,1024]{1,0:T(8,128)(2,1)S(1)}, bf16[128,1024]{1,0:T(8,128)(2,1)}, u32[]{:S(2)}) copy-start(bf16[128,1024]{1,0:T(8,128)(2,1)} %param.9) | copy-start | bytes 786436
  17.1 33.3 %copy-start.4 = (bf16[128,8192]{1,0:T(8,128)(2,1)S(1)}, bf16[128,8192]{1,0:T(8,128)(2,1)}, u32[]{:S(2)}) copy-start(bf16[128,8192]{1,0:T(8,128)(2,1)} %param.10) | copy-start | bytes 6291460
  21.3 10.6 %all-to-all-start.5 = ((f32[128,8,8]{0,2,1:T(8,128)}), f32[128,8,8]{0,2,1:T(8,128)S(1)}, u32[]{:S(2)}, u32[]{:S(2)}) async-start(f32[128,8,8]{0,2,1:T(8,128)} %bitcast.22), calls=%async_computation.5 | async-start | bytes 65536 | tf_op jit(solution)/shard_map/all_to_all | solution.py:118
  31.9 10.8 %all-to-all-start = ((bf16[128,8,128]{2,0,1:T(8,128)(2,1)}), bf16[128,8,128]{2,0,1:T(8,128)(2,1)S(1)}, u32[]{:S(2)}, u32[]{:S(2)}) async-start(bf16[128,8,128]{2,0,1:T(8,128)(2,1)} %copy_bitcast_fusion.3), calls=%async_computation | async-start | bytes 524288 | tf_op jit(solution)/shard_map/all_to_all | solution.py:95
  42.7 10.6 %all-to-all-start.3 = ((bf16[128,8,128]{2,0,1:T(8,128)(2,1)}), bf16[128,8,128]{2,0,1:T(8,128)(2,1)S(1)}, u32[]{:S(2)}, u32[]{:S(2)}) async-start(bf16[128,8,128]{2,0,1:T(8,128)(2,1)} %copy_bitcast_fusion.2), calls=%async_computation.3 | async-start | bytes 524288 | tf_op jit(solution)/shard_map/all_to_all | solution.py:102
  53.4 31.7 %all-to-all-start.4 = ((bf16[128,8,1024]{2,0,1:T(8,128)(2,1)}), bf16[128,8,1024]{2,0,1:T(8,128)(2,1)S(1)}, u32[]{:S(2)}, u32[]{:S(2)}) async-start(bf16[128,8,1024]{2,0,1:T(8,128)(2,1)} %bitcast.885), calls=%async_computation.4 | async-start | bytes 4194304 | tf_op jit(solution)/shard_map/all_to_all | solution.py:88
  63.6 20.0 %collective-permute-start = (bf16[2,1024,1,128]{3,1,2,0:T(8,128)(2,1)S(1)}, bf16[2,1024,1,128]{3,1,2,0:T(8,128)(2,1)S(1)}, u32[]{:S(2)}, u32[]{:S(2)}) collective-permute-start(bf16[2,1024,1,128]{3,1,2,0:T(8,128)(2,1)S(1)} %pad_maximum_fusion.1), channel_id=1, source_target_pairs={{0,8},{8,16},{16,24},{24,32},{32,40},{40,48},{48,56},{56,64},{64,7... | collective-permute-start | bytes 1572872 | tf_op jit(solution)/shard_map/ppermute | solution.py:13
  83.6 39.1 %copy-start.17 = (bf16[2,1024,1,128]{3,1,2,0:T(8,128)(2,1)}, bf16[2,1024,1,128]{3,1,2,0:T(8,128)(2,1)S(1)}, u32[]{:S(2)}) copy-start(bf16[2,1024,1,128]{3,1,2,0:T(8,128)(2,1)S(1)} %collective-permute-done) | copy-start | bytes 1572868
  83.6 26.6 %collective-permute-start.1 = (bf16[2,1024,1,128]{3,1,2,0:T(8,128)(2,1)S(1)}, bf16[2,1024,1,128]{3,1,2,0:T(8,128)(2,1)}, u32[]{:S(2)}, u32[]{:S(2)}) collective-permute-start(bf16[2,1024,1,128]{3,1,2,0:T(8,128)(2,1)S(1)} %collective-permute-done), channel_id=1, source_target_pairs={{0,8},{8,16},{16,24},{24,32},{32,40},{40,48},{48,56},{56,64},{64,7... | collective-permute-start | bytes 1572872 | tf_op jit(solution)/shard_map/ppermute | solution.py:13
  85.1 39.1 %all-to-all-start.1 = ((bf16[128,8,1024]{2,0,1:T(8,128)(2,1)}), bf16[128,8,1024]{2,0,1:T(8,128)(2,1)}, u32[]{:S(2)}, u32[]{:S(2)}) async-start(bf16[128,8,1024]{2,0,1:T(8,128)(2,1)} %bitcast.884), calls=%async_computation.1 | async-start | bytes 4194304 | tf_op jit(solution)/shard_map/all_to_all | solution.py:81
  110.2 11.6 %collective-permute-start.2 = (bf16[2,1024,1,128]{3,1,2,0:T(8,128)(2,1)}, bf16[2,1024,1,128]{3,1,2,0:T(8,128)(2,1)S(1)}, u32[]{:S(2)}, u32[]{:S(2)}) collective-permute-start(bf16[2,1024,1,128]{3,1,2,0:T(8,128)(2,1)} %collective-permute-done.1), channel_id=1, source_target_pairs={{0,8},{8,16},{16,24},{24,32},{32,40},{40,48},{48,56},{56,64},{64,7... | collective-permute-start | bytes 1572872 | tf_op jit(solution)/shard_map/ppermute | solution.py:13
  190.6 78.4 %collective-permute-start.3 = (f32[2,1024,1,128]{3,1,2,0:T(8,128)}, f32[2,1024,1,128]{3,1,2,0:T(8,128)}, u32[]{:S(2)}, u32[]{:S(2)}) collective-permute-start(f32[2,1024,1,128]{3,1,2,0:T(8,128)} %fusion.170), channel_id=1, source_target_pairs={{0,8},{8,16},{16,24},{24,32},{32,40},{40,48},{48,56},{56,64},{64,7... | collective-permute-start | bytes 3145736 | tf_op jit(solution)/shard_map/ppermute | solution.py:13
  193.5 33.3 %copy-start.2 = (f32[512,512,8]{1,0,2:T(8,128)}, f32[512,512,8]{1,0,2:T(8,128)S(1)}, u32[]{:S(2)}) copy-start(f32[512,512,8]{1,0,2:T(8,128)S(1)} %fusion.148) | copy-start | bytes 25165828
  194.8 20.3 %copy-start.3 = (f32[512,512,8]{1,0,2:T(8,128)}, f32[512,512,8]{1,0,2:T(8,128)S(1)}, u32[]{:S(2)}) copy-start(f32[512,512,8]{1,0,2:T(8,128)S(1)} %fusion.151) | copy-start | bytes 25165828
  252.1 11.6 %copy-start.43 = (pred[512,512]{0,1:T(8,128)(4,1)S(1)}, pred[512,512]{0,1:T(8,128)(4,1)}, u32[]{:S(2)}) copy-start(pred[512,512]{0,1:T(8,128)(4,1)} %compare_and_fusion.4) | copy-start | bytes 786436
  252.1 78.5 %all-to-all-start.6 = ((bf16[8,2,65536]{2,1,0:T(2,128)(2,1)}), bf16[8,2,65536]{2,1,0:T(2,128)(2,1)S(1)}, u32[]{:S(2)}, u32[]{:S(2)}) async-start(bf16[8,2,65536]{2,1,0:T(2,128)(2,1)} %reshape.667), calls=%async_computation.6 | async-start | bytes 4194304 | tf_op jit(solution)/shard_map/all_to_all | solution.py:171
  263.7 11.4 %slice-start.2 = ((s8[8388608]{0:T(1024)(128)(4,1)}), s8[4194304]{0:T(1024)(128)(4,1)S(1)}, s32[]{:S(2)}) async-start(s8[8388608]{0:T(1024)(128)(4,1)} %bitcast.882), calls=%async_computation.11 | async-start | bytes 8388608
  273.6 21.5 %collective-permute-start.4 = (f32[2,1024,1,128]{3,1,2,0:T(8,128)}, f32[2,1024,1,128]{3,1,2,0:T(8,128)S(1)}, u32[]{:S(2)}, u32[]{:S(2)}) collective-permute-start(f32[2,1024,1,128]{3,1,2,0:T(8,128)} %fusion.172), channel_id=1, source_target_pairs={{0,8},{8,16},{16,24},{24,32},{32,40},{40,48},{48,56},{56,64},{64,7... | collective-permute-start | bytes 3145736 | tf_op jit(solution)/shard_map/ppermute | solution.py:13
  275.1 21.6 %slice-start = ((s8[8388608]{0:T(1024)(128)(4,1)}), s8[4194304]{0:T(1024)(128)(4,1)S(1)}, s32[]{:S(2)}) async-start(s8[8388608]{0:T(1024)(128)(4,1)} %bitcast.880), calls=%async_computation.9 | async-start | bytes 8388608
  275.2 20.0 %copy-start.48 = (f32[1,512,1,128]{3,1,2,0:T(8,128)S(1)}, f32[1,512,1,128]{3,1,2,0:T(8,128)}, u32[]{:S(2)}) copy-start(f32[1,512,1,128]{3,1,2,0:T(8,128)} %fusion.123) | copy-start | bytes 786436
  275.2 19.9 %copy-start.49 = (f32[1,512,1,128]{3,1,2,0:T(8,128)S(1)}, f32[1,512,1,128]{3,1,2,0:T(8,128)}, u32[]{:S(2)}) copy-start(f32[1,512,1,128]{3,1,2,0:T(8,128)} %fusion.109) | copy-start | bytes 786436
  275.2 20.2 %copy-start.6 = (bf16[8,512,512]{1,2,0:T(8,128)(2,1)S(1)}, bf16[8,512,512]{1,2,0:T(8,128)(2,1)}, u32[]{:S(2)}) copy-start(bf16[8,512,512]{1,2,0:T(8,128)(2,1)} %copy-done.5) | copy-start | bytes 12582916
  275.2 21.5 %slice-start.1 = ((s8[8388608]{0:T(1024)(128)(4,1)}), s8[4194304]{0:T(1024)(128)(4,1)S(1)}, s32[]{:S(2)}) async-start(s8[8388608]{0:T(1024)(128)(4,1)} %bitcast.880), calls=%async_computation.10 | async-start | bytes 8388608
  276.9 19.9 %copy-start.26 = (bf16[512,1,8,128]{3,2,0,1:T(8,128)(2,1)S(1)}, bf16[512,1,8,128]{3,2,0,1:T(8,128)(2,1)}, u32[]{:S(2)}) copy-start(bf16[512,1,8,128]{3,2,0,1:T(8,128)(2,1)} %get-tuple-element.15) | copy-start | bytes 3145732
  276.9 19.9 %copy-start.39 = (pred[512,512]{0,1:T(8,128)(4,1)S(1)}, pred[512,512]{0,1:T(8,128)(4,1)}, u32[]{:S(2)}) copy-start(pred[512,512]{0,1:T(8,128)(4,1)} %compare_and_fusion) | copy-start | bytes 786436
  295.4 15.8 %collective-permute-start.5 = (f32[2,1024,1,128]{3,1,2,0:T(8,128)S(1)}, f32[2,1024,1,128]{3,1,2,0:T(8,128)S(1)}, u32[]{:S(2)}, u32[]{:S(2)}) collective-permute-start(f32[2,1024,1,128]{3,1,2,0:T(8,128)S(1)} %fusion.173), channel_id=1, source_target_pairs={{0,8},{8,16},{16,24},{24,32},{32,40},{40,48},{48,56},{56,64},{64,7... | collective-permute-start | bytes 3145736 | tf_op jit(solution)/shard_map/ppermute | solution.py:13
  296.7 14.4 %copy-start.44 = (f32[1,512,1,128]{3,1,2,0:T(8,128)S(1)}, f32[1,512,1,128]{3,1,2,0:T(8,128)}, u32[]{:S(2)}) copy-start(f32[1,512,1,128]{3,1,2,0:T(8,128)} %fusion.117) | copy-start | bytes 786436
  296.8 14.4 %copy-start.46 = (f32[1,512,1,128]{3,1,2,0:T(8,128)S(1)}, f32[1,512,1,128]{3,1,2,0:T(8,128)}, u32[]{:S(2)}) copy-start(f32[1,512,1,128]{3,1,2,0:T(8,128)} %fusion.108) | copy-start | bytes 786436
  311.4 17.6 %collective-permute-start.6 = (bf16[2,1024,1,128]{3,1,2,0:T(8,128)(2,1)S(1)}, bf16[2,1024,1,128]{3,1,2,0:T(8,128)(2,1)S(1)}, u32[]{:S(2)}, u32[]{:S(2)}) collective-permute-start(bf16[2,1024,1,128]{3,1,2,0:T(8,128)(2,1)S(1)} %convert), channel_id=1, source_target_pairs={{0,104},{8,112},{16,120},{24,0},{32,8},{40,16},{48,24},{56,32},{64... | collective-permute-start | bytes 1572872 | tf_op jit(solution)/shard_map/ppermute | solution.py:13
  330.6 11.6 %all-to-all-start.7 = ((bf16[8,2,8192]{2,1,0:T(2,128)(2,1)}), bf16[8,2,8192]{2,1,0:T(2,128)(2,1)S(1)}, u32[]{:S(2)}, u32[]{:S(2)}) async-start(bf16[8,2,8192]{2,1,0:T(2,128)(2,1)} %reshape.669), calls=%async_computation.7 | async-start | bytes 524288 | tf_op jit(solution)/shard_map/all_to_all | solution.py:178
  342.2 19.7 %all-to-all-start.8 = ((bf16[8,2,8192]{2,1,0:T(2,128)(2,1)}), bf16[8,2,8192]{2,1,0:T(2,128)(2,1)S(1)}, u32[]{:S(2)}, u32[]{:S(2)}) async-start(bf16[8,2,8192]{2,1,0:T(2,128)(2,1)} %reshape.671), calls=%async_computation.8 | async-start | bytes 524288 | tf_op jit(solution)/shard_map/all_to_all | solution.py:179
  (51 other events, 170.5 us)
where the time goes:
time: 370 us; the launch traced here: 364 us
  matrix products  112 us (30%)
  waiting for transfers between devices  108 us (29%)
  local copies, waits for them, and re-layouts  61.1 us (17%)
  starting transfers between devices  51.8 us (14%)
  other arithmetic  28.7 us (8%)
    ppermute x7, waiting for transfers between devices, from_behind(): return lax.ppermute(value, axis, pairs)  89.3 us
    dot_general x9, matrix products, tile_grads(): jnp.einsum('qcgh,kch->cgqk', grad_tile, value_tile, preferred_element_typ...  35.6 us
    unnamed x154, local copies, waits for them, and re-layouts  35.3 us
    dot_general x9, matrix products, tile_grads(): jnp.einsum('cgqk,kch->qcgh', score_low, key_tile, preferred_element_type=...  23.9 us
    dot_general x9, matrix products, tile_grads(): jnp.einsum('cgqk,qcgh->kch', prob_low, grad_tile, preferred_element_type=...  20.4 us
    dot_general x9, matrix products, tile_grads(): jnp.einsum('cgqk,qcgh->kch', score_low, query_tile, preferred_element_typ...  16.2 us
    dot_general x9, matrix products, tile_grads(): jnp.einsum('qcgh,kch->cgqk', query_tile, key_tile, preferred_element_type...  15.6 us
    all_to_all x1, starting transfers between devices, local(): lax.all_to_all(queries.reshape(tok_rows, uly_count, head_dev * HD), 'uly'...  8.59 us
  transfers between devices with their start and end apart: 16, of which 11 were waited for; matrix products, arithmetic and copies ran while one was open for 37% of the time, Pallas kernels for 0%

commit v1 on v0

v1 whole, which is shorter than its diff:
```python
import functools
import math

import jax
import jax.numpy as jnp
from jax import lax
from jax.experimental import pallas as pl
from jax.experimental.pallas import tpu as pltpu
from jax.sharding import PartitionSpec as P

HD = 128
STEPS = 4
DOCS = 8
TOK = 128
HEADS_DEV = 8
HALF = 512
CHUNKS = (4, 4)
PARTS = 3
FAR = 32768.0
SCALE = HD ** (-0.5)
EXP2_SCALE = SCALE * math.log2(math.e)
NORM_SCALE = HD ** 0.5
BF = jnp.bfloat16
F32 = jnp.float32
VMEM_LIMIT = 60 * 1024 * 1024

NN = (((1,), (0,)), ((), ()))
NT = (((1,), (1,)), ((), ()))


def dot(a, b, dims=NN):
    return lax.dot_general(a, b, dims, preferred_element_type=F32)


def three_parts(x, first, second):
    high = x.astype(BF).astype(F32)
    rest = x - high
    mid = rest.astype(BF).astype(F32)
    low = rest - mid
    return jnp.where(first, high, jnp.where(second, mid, low))


def pack_kernel(q_ref, do_ref, o_ref, k_ref, v_ref, ln_ref, doc_ref, kvs_ref, *qd_refs):
    u = pl.program_id(0)
    lane = lax.broadcasted_iota(jnp.int32, (TOK, 128), 1)
    ln_lane = lax.broadcasted_iota(jnp.int32, (TOK, ln_ref.shape[1]), 1)
    norm = ln_ref[...] * NORM_SCALE
    block = jnp.zeros((TOK, 128), F32)
    for h in range(HEADS_DEV):
        cols = slice(h * HD, (h + 1) * HD)
        delta = jnp.sum(
            do_ref[:, cols].astype(F32) * o_ref[:, cols].astype(F32), axis=1, keepdims=True
        )
        norm_h = jnp.sum(
            jnp.where(ln_lane == u * HEADS_DEV + h, norm, 0.0), axis=1, keepdims=True
        )
        mine = lane % HEADS_DEV == h
        block = jnp.where(mine & (lane < 24), norm_h, block)
        block = jnp.where(mine & (lane >= 24) & (lane < 48), delta, block)
    part = (lane // HEADS_DEV) % PARTS
    block = three_parts(block, part == 0, part == 1)
    kvs_ref[0, 0] = k_ref[...].T
    kvs_ref[0, 1] = v_ref[...].T
    kvs_ref[0, 2] = jnp.where(lane < 48, block, doc_ref[...]).astype(BF)
    h = 0
    for ref in qd_refs:
        count = ref.shape[1] // 2
        for i in range(count):
            cols = slice(h * HD, (h + 1) * HD)
            ref[0, i] = q_ref[:, cols]
            ref[0, count + i] = do_ref[:, cols]
            h += 1


def pack(queries, grad_out, attn_out, key_rows, value_rows, log_norm, doc_block):
    width = HEADS_DEV * HD
    wide = pl.BlockSpec((TOK, width), lambda u: (0, u))
    thin = pl.BlockSpec((TOK, HD), lambda u: (0, u))
    shapes = [(8, 3, TOK, HD)] + [(8, 2 * c, TOK, HD) for c in CHUNKS]
    return pl.pallas_call(
        pack_kernel,
        grid=(8,),
        in_specs=[
            wide,
            wide,
            wide,
            thin,
            thin,
            pl.BlockSpec(log_norm.shape, lambda u: (0, 0)),
            pl.BlockSpec(doc_block.shape, lambda u: (0, 0)),
        ],
        out_specs=[pl.BlockSpec((1,) + s[1:], lambda u: (u, 0, 0, 0)) for s in shapes],
        out_shape=[jax.ShapeDtypeStruct(s, BF) for s in shapes],
        compiler_params=pltpu.CompilerParams(vmem_limit_bytes=VMEM_LIMIT),
        cost_estimate=pl.CostEstimate(flops=0, bytes_accessed=11 << 20, transcendentals=0),
        name="pack",
    )(queries, grad_out, attn_out, key_rows, value_rows, log_norm, doc_block)


def attend_kernel(first_head, count, has_sum, *refs):
    second_ref, qd_ref, kvs_ref, kv1_ref, kv2_ref, kv3_ref, kdoc_ref = refs[:7]
    refs = refs[7:]
    if has_sum:
        sum_ref, refs = refs[0], refs[1:]
    dq_ref, dkv_ref, qt_ref, dot_ref, dqt_ref, sel_ref = refs
    kv_refs = (kvs_ref, kv1_ref, kv2_ref, kv3_ref)

    row = lax.broadcasted_iota(jnp.int32, (48, HALF), 0)
    for h in range(count):
        mine = row % HEADS_DEV == first_head + h
        sel_ref[h] = jnp.where(mine & (row < 24), -1.0, 0.0).astype(BF)
        sel_ref[count + h] = jnp.where(mine & (row >= 24), -1.0, 0.0).astype(BF)
    for half in range(2):
        for h in range(count):
            for i in range(4):
                cols = slice(i * TOK, (i + 1) * TOK)
                qt_ref[half, h, :, cols] = qd_ref[half * 4 + i, h].T
                dot_ref[half, h, :, cols] = qd_ref[half * 4 + i, count + h].T
    dqt_ref[...] = jnp.zeros_like(dqt_ref)
    if has_sum:
        dkv_ref[...] = sum_ref[...]
    else:
        dkv_ref[...] = jnp.zeros_like(dkv_ref)

    def rows_of(qhalf, index, q0, qn):
        block = qd_ref[pl.ds(qhalf * 4 + q0 // TOK, qn // TOK), index]
        return block.reshape(qn, HD)

    def tile(step, qhalf, khalf, pieces):
        kv_ref = kv_refs[step]
        kt_all = jnp.concatenate([kv_ref[khalf * 4 + i, 0] for i in range(4)], axis=1)
        vt_all = jnp.concatenate([kv_ref[khalf * 4 + i, 1] for i in range(4)], axis=1)
        docs_all = kdoc_ref[step, khalf]
        for q0, qn, kn, diagonal in pieces:
            kt, vt, docs = kt_all[:, :kn], vt_all[:, :kn], docs_all[:, :kn]
            stats = kvs_ref[pl.ds(qhalf * 4 + q0 // TOK, qn // TOK), 2].reshape(qn, HD)
            dk_sum = jnp.zeros((HD, kn), F32)
            dv_sum = jnp.zeros((HD, kn), F32)
            for h in range(count):
                k_ext = jnp.concatenate(
                    [kt, sel_ref[h, :, :kn], docs, jnp.zeros((64, kn), BF)], axis=0
                )
                v_ext = jnp.concatenate(
                    [vt, sel_ref[count + h, :, :kn], jnp.zeros((80, kn), BF)], axis=0
                )
                q_ext = jnp.concatenate([rows_of(qhalf, h, q0, qn), stats], axis=1)
                do_ext = jnp.concatenate([rows_of(qhalf, count + h, q0, qn), stats], axis=1)
                prob = jnp.exp2(dot(q_ext, k_ext) * EXP2_SCALE)
                if diagonal:
                    qi = lax.broadcasted_iota(jnp.int32, (qn, kn), 0) + q0
                    ki = lax.broadcasted_iota(jnp.int32, (qn, kn), 1)
                    prob = jnp.where(qi >= ki, prob, 0.0)
                dscore = (prob * dot(do_ext, v_ext)).astype(BF)
                prob = prob.astype(BF)
                span = slice(q0, q0 + qn)
                dv_sum += dot(dot_ref[qhalf, h, :, span], prob)
                dk_sum += dot(qt_ref[qhalf, h, :, span], dscore)
                dqt_ref[qhalf, h, :, span] += dot(kt, dscore, NT)
            dkv_ref[step, 0, khalf, :, :kn] += dk_sum
            dkv_ref[step, 1, khalf, :, :kn] += dv_sum

    full = ((0, HALF, HALF, False),)
    corner = ((0, HALF // 2, HALF // 2, True), (HALF // 2, HALF // 2, HALF, True))

    def diagonal(half, carry):
        tile(0, half, half, corner)
        return carry

    lax.fori_loop(0, 2, diagonal, 0)
    tile(0, 1, 0, full)
    for step in range(1, STEPS):

        def both(index, carry, step=step):
            second = second_ref[step]
            tile(step, jnp.where(index == 0, 1, second), jnp.where(index == 0, 0, second), full)
            return carry

        lax.fori_loop(0, 2, both, 0)

    for half in range(2):
        for h in range(count):
            for i in range(4):
                piece = dqt_ref[half, h, :, i * TOK : (i + 1) * TOK]
                dq_ref[half * 4 + i, h] = (piece * SCALE).T.astype(BF)


def attend(first_head, second, qd, kvs, kvs_others, kdoc, dkv):
    count = qd.shape[1] // 2
    has_sum = dkv is not None
    operands = [second, qd, kvs, *kvs_others, kdoc] + ([dkv] if has_sum else [])
    vmem = pl.BlockSpec(memory_space=pltpu.VMEM)
    flops = 9 * 5 * 2 * HALF * HALF * HD * count
    return pl.pallas_call(
        functools.partial(attend_kernel, first_head, count, has_sum),
        in_specs=[pl.BlockSpec(memory_space=pltpu.SMEM)] + [vmem] * (len(operands) - 1),
        out_specs=[vmem, vmem],
        out_shape=[
            jax.ShapeDtypeStruct((8, count, TOK, HD), BF),
            jax.ShapeDtypeStruct((STEPS, 2, 2, HD, HALF), F32),
        ],
        scratch_shapes=[
            pltpu.VMEM((2, count, HD, HALF), BF),
            pltpu.VMEM((2, count, HD, HALF), BF),
            pltpu.VMEM((2, count, HD, HALF), F32),
            pltpu.VMEM((2 * count, 48, HALF), BF),
        ],
        compiler_params=pltpu.CompilerParams(vmem_limit_bytes=VMEM_LIMIT),
        cost_estimate=pl.CostEstimate(
            flops=2 * flops, bytes_accessed=8 << 20, transcendentals=9 * HALF * HALF * count
        ),
        name="attend",
    )(*operands)


def split_kernel(dkv_ref, own_ref, one_ref, two_ref, three_ref):
    for step, ref in ((1, one_ref), (2, two_ref), (3, three_ref)):
        ref[0] = (dkv_ref[step, 0] * SCALE).astype(BF)
        ref[1] = dkv_ref[step, 1].astype(BF)
    own_ref[0] = dkv_ref[0, 0] * SCALE
    own_ref[1] = dkv_ref[0, 1]


def split(dkv):
    shape = (2, 2, HD, HALF)
    return pl.pallas_call(
        split_kernel,
        out_shape=[jax.ShapeDtypeStruct(shape, F32)] + [jax.ShapeDtypeStruct(shape, BF)] * 3,
        compiler_params=pltpu.CompilerParams(vmem_limit_bytes=VMEM_LIMIT),
        name="split",
    )(dkv)


def total_kernel(own_ref, one_ref, two_ref, three_ref, out_ref):
    for pair in range(2):
        for half in range(2):
            total = (
                own_ref[pair, half]
                + one_ref[pair, half].astype(F32)
                + two_ref[pair, half].astype(F32)
                + three_ref[pair, half].astype(F32)
            )
            for i in range(4):
                out_ref[half * 4 + i, pair] = total[:, i * TOK : (i + 1) * TOK].T.astype(BF)


def total(own, one, two, three):
    return pl.pallas_call(
        total_kernel,
        out_shape=jax.ShapeDtypeStruct((8, 2, TOK, HD), BF),
        compiler_params=pltpu.CompilerParams(vmem_limit_bytes=VMEM_LIMIT),
        name="total",
    )(own, one, two, three)


def unpack_q_kernel(*refs):
    out_ref = refs[-1]
    h = 0
    for ref in refs[:-1]:
        for i in range(ref.shape[1]):
            out_ref[:, h * HD : (h + 1) * HD] = ref[0, i]
            h += 1


def unpack_q(parts):
    return pl.pallas_call(
        unpack_q_kernel,
        grid=(8,),
        in_specs=[pl.BlockSpec((1,) + p.shape[1:], lambda u: (u, 0, 0, 0)) for p in parts],
        out_specs=pl.BlockSpec((TOK, HEADS_DEV * HD), lambda u: (0, u)),
        out_shape=jax.ShapeDtypeStruct((TOK, 8 * HEADS_DEV * HD), BF),
        compiler_params=pltpu.CompilerParams(vmem_limit_bytes=VMEM_LIMIT),
        name="unpack_q",
    )(*parts)


def unpack_kv_kernel(pair_ref, k_ref, v_ref):
    for u in range(8):
        k_ref[:, u * HD : (u + 1) * HD] = pair_ref[u, 0]
        v_ref[:, u * HD : (u + 1) * HD] = pair_ref[u, 1]


def unpack_kv(pair):
    shape = jax.ShapeDtypeStruct((TOK, 8 * HD), BF)
    return pl.pallas_call(
        unpack_kv_kernel,
        out_shape=[shape, shape],
        compiler_params=pltpu.CompilerParams(vmem_limit_bytes=VMEM_LIMIT),
        name="unpack_kv",
    )(pair)


def shift(value, axis, steps):
    count = lax.axis_size(axis)
    pairs = [(source, (source + steps) % count) for source in range(count)]
    return lax.ppermute(value, axis, pairs)


def exchange(value):
    return lax.all_to_all(value, "uly", split_axis=0, concat_axis=0, tiled=True)


def local(queries, key_rows, value_rows, grad_out, attn_out, log_norm, doc_ids):
    groups = lax.axis_size("blk")
    group = lax.axis_index("blk")
    member = lax.axis_index("uly")

    first = jnp.where(
        member < 4, group * HALF + member * TOK, (2 * groups - 1 - group) * HALF + (member - 4) * TOK
    )
    my_docs = lax.dynamic_slice_in_dim(doc_ids, first, TOK)
    lane = jnp.arange(128, dtype=jnp.int32)[None, :]
    doc_block = jnp.where(
        (lane >= 48) & (lane < 48 + DOCS) & (my_docs[:, None] != lane - 48), FAR, 0.0
    ).astype(F32)

    kdocs = []
    for step in range(STEPS):
        owner = (group - step) % groups
        low = lax.dynamic_slice_in_dim(doc_ids, owner * HALF, HALF)
        high = lax.dynamic_slice_in_dim(doc_ids, (2 * groups - 1 - owner) * HALF, HALF)
        kdocs.append(jnp.stack([low, high]))
    kdocs = jnp.stack(kdocs)
    kdoc = jnp.where(
        kdocs[:, :, None, :] == jnp.arange(16, dtype=jnp.int32)[None, None, :, None], -1.0, 0.0
    ).astype(BF)
    second = jnp.where(group >= jnp.arange(STEPS), 0, 1).astype(jnp.int32)

    kvs, *qds = pack(queries, grad_out, attn_out, key_rows, value_rows, log_norm, doc_block)
    kvs = exchange(kvs)
    visiting = kvs[:, :2]
    others = []
    for _ in range(1, STEPS):
        visiting = shift(visiting, "blk", 1)
        others.append(visiting)

    dkv = None
    head = 0
    dqs = []
    for qd in qds:
        qd = exchange(qd)
        dq, dkv = attend(head, second, qd, kvs, others, kdoc, dkv)
        head += qd.shape[1] // 2
        dqs.append(exchange(dq))

    own, *sends = split(dkv)
    back = [shift(part, "blk", -step) for step, part in enumerate(sends, start=1)]
    pair = exchange(total(own, *back))
    grad_keys, grad_values = unpack_kv(pair)
    return unpack_q(dqs), grad_keys, grad_values


def solution(mesh):
    rows = P(("blk", "uly"), None)
    return jax.shard_map(
        local,
        mesh=mesh,
        in_specs=(rows, rows, rows, rows, rows, rows, P()),
        out_specs=(rows, rows, rows),
        check_vma=False,
    )
```

time: 370 us -> 227 us (0.61)
  the two profiles are of different devices: /device:TPU:90 before, /device:TPU:0 now
where the time goes in v1:
time: 227 us; the launch traced here: 225 us
  Pallas kernels  82.5 us (36%)
  starting transfers between devices  61.1 us (27%)
  waiting for transfers between devices  54.3 us (24%)
  blocking collectives  18.6 us (8%)
  local copies, waits for them, and re-layouts  6.28 us (3%)
    pallas_call x2, Pallas kernels, attend(): pl.pallas_call(functools.partial(attend_kernel, first_head, count, has_su...  59.7 us
    ppermute x6, waiting for transfers between devices, shift(): return lax.ppermute(value, axis, pairs)  50.7 us
    ppermute x6, starting transfers between devices, shift(): return lax.ppermute(value, axis, pairs)  38.9 us
    all_to_all x5, starting transfers between devices, exchange(): return lax.all_to_all(value, 'uly', split_axis=0, concat_axis=0, tiled=True)  22.3 us
    all_to_all x1, blocking collectives, exchange(): return lax.all_to_all(value, 'uly', split_axis=0, concat_axis=0, tiled=True)  18.6 us
    pallas_call x1, Pallas kernels, pack(): pl.pallas_call(pack_kernel, grid=(8,), in_specs=[wide, wide, wide, thin,...  8.25 us
    pallas_call x1, Pallas kernels, unpack_q(): pl.pallas_call(unpack_q_kernel, grid=(8,), in_specs=[pl.BlockSpec((1,) +...  5.93 us
    unnamed x21, local copies, waits for them, and re-layouts  4.59 us
  transfers between devices with their start and end apart: 11, of which 5 were waited for; matrix products, arithmetic and copies ran while one was open for 1% of the time, Pallas kernels for 32%

profile of v1, /device:TPU:0, one launch (start us, length us, event | category | flops | bytes accessed | tf_op | source)
XLA Modules:
  0.0 225.5 jit_solution(16828610413812452753)
XLA Ops:
  0.7 1.5 copy.10.ln_ref
  2.2 0.8 dynamic_slice.27
  2.9 0.7 and_select_fusion.doc_ref
  3.6 8.2 %pack.1 = (bf16[8,3,128,128]{3,2,1,0:T(8,128)(2,1)}, bf16[8,8,128,128]{3,2,1,0:T(8,128)(2,1)}, bf16[8,8,128,128]{3,2,1,0:T(8,128)(2,1)}) custom-call(bf16[128,8192]{1,0:T(8,128)(2,1)} %q_ref.1, bf16[128,8192]{1,0:T(8,128)(2,1)} %do_ref.1, bf16[128,8192]{1,0:T(8,128)(2,1)} %o_ref.1, bf16[128,1024]{1,0:T(8,128)(2,1)} %k_ref.1, bf16[128,1024]{1,0:T(8,128)(2,1)} %v_ref.1, ...), custom_call_target="tpu_custom_call" | custom-call | bytes 11534336 | tf_op jit(solution)/shard_map/pack/pallas_call | solution.py:80
  11.9 18.6 %all_to_all.30.refs_2_ = bf16[8,3,128,128]{3,2,1,0:T(8,128)(2,1)S(1)} all-to-all(bf16[8,3,128,128]{3,2,1,0:T(8,128)(2,1)} %get-tuple-element.17), channel_id=1, replica_groups=mesh['blk'=16,'uly'=8] {'uly'}, dimensions={0} | all-to-all | bytes 1572864 | tf_op jit(solution)/shard_map/all_to_all | solution.py:299
  30.5 3.6 %all-to-all-start = ((bf16[8,8,128,128]{3,2,1,0:T(8,128)(2,1)}), bf16[8,8,128,128]{3,2,1,0:T(8,128)(2,1)S(1)}, u32[]{:S(2)}, u32[]{:S(2)}) async-start(bf16[8,8,128,128]{3,2,1,0:T(8,128)(2,1)} %get-tuple-element.16), calls=%async_computation | async-start | bytes 4194304 | tf_op jit(solution)/shard_map/all_to_all | solution.py:299
  34.3 17.9 %collective-permute-done.refs_3_ = bf16[8,2,128,128]{3,2,1,0:T(8,128)(2,1)S(1)} collective-permute-done((bf16[8,2,128,128]{3,2,1,0:T(8,128)(2,1)S(1)}, bf16[8,2,128,128]{3,2,1,0:T(8,128)(2,1)S(1)}, u32[]{:S(2)}, u32[]{:S(2)}) %collective-permute-start) | collective-permute-done | bytes 524320 | tf_op jit(solution)/shard_map/ppermute | solution.py:295
  52.1 9.4 %collective-permute-start.1 = (bf16[8,2,128,128]{3,2,1,0:T(8,128)(2,1)S(1)}, bf16[8,2,128,128]{3,2,1,0:T(8,128)(2,1)S(1)}, u32[]{:S(2)}, u32[]{:S(2)}) collective-permute-start(bf16[8,2,128,128]{3,2,1,0:T(8,128)(2,1)S(1)} %collective-permute-done.refs_3_), channel_id=1, source_target_pairs={{0,8},{8,16},{16,24},{24,32},{32,40},{40,48},{48,56},{56,64},{64,7... | collective-permute-start | bytes 1572872 | tf_op jit(solution)/shard_map/ppermute | solution.py:295
  61.6 0.9 fusion
  62.5 6.6 %collective-permute-done.1.refs_4_ = bf16[8,2,128,128]{3,2,1,0:T(8,128)(2,1)S(1)} collective-permute-done((bf16[8,2,128,128]{3,2,1,0:T(8,128)(2,1)S(1)}, bf16[8,2,128,128]{3,2,1,0:T(8,128)(2,1)S(1)}, u32[]{:S(2)}, u32[]{:S(2)}) %collective-permute-start.1) | collective-permute-done | bytes 524320 | tf_op jit(solution)/shard_map/ppermute | solution.py:295
  69.1 2.6 %collective-permute-start.2 = (bf16[8,2,128,128]{3,2,1,0:T(8,128)(2,1)S(1)}, bf16[8,2,128,128]{3,2,1,0:T(8,128)(2,1)}, u32[]{:S(2)}, u32[]{:S(2)}) collective-permute-start(bf16[8,2,128,128]{3,2,1,0:T(8,128)(2,1)S(1)} %collective-permute-done.1.refs_4_), channel_id=1, source_target_pairs={{0,8},{8,16},{16,24},{24,32},{32,40},{40,48},{48,56},{56,64},{64,7... | collective-permute-start | bytes 1572872 | tf_op jit(solution)/shard_map/ppermute | solution.py:295
  71.7 0.5 compare_select_fusion.refs_0_
  72.2 0.7 select_convert_fusion.refs_6_
  72.9 1.3 copy-done.3
  74.2 5.3 %all-to-all-start.3 = ((bf16[8,8,128,128]{3,2,1,0:T(8,128)(2,1)}), bf16[8,8,128,128]{3,2,1,0:T(8,128)(2,1)}, u32[]{:S(2)}, u32[]{:S(2)}) async-start(bf16[8,8,128,128]{3,2,1,0:T(8,128)(2,1)} %get-tuple-element.19), calls=%async_computation.3 | async-start | bytes 4194304 | tf_op jit(solution)/shard_map/all_to_all | solution.py:299
  79.6 1.8 collective-permute-done.2.refs_5_
  81.4 29.2 %attend.2 = (bf16[8,4,128,128]{3,2,1,0:T(8,128)(2,1)}, f32[4,2,2,128,512]{4,3,2,1,0:T(8,128)}) custom-call(s32[4]{0:T(128)} %compare_select_fusion.refs_0_, bf16[8,8,128,128]{3,2,1,0:T(8,128)(2,1)} %copy-done.3, bf16[8,3,128,128]{3,2,1,0:T(8,128)(2,1)} %copy-done.2, bf16[8,2,128,128]{3,2,1,0:T(8,128)(2,1)} %copy-done.8, bf16[8,2,128,128]{3,2,1,0:T(8,128)(2,1)} %copy-done.9, ...), custom_call_target="tpu_custom_call" | custom-call | flops 24159191040 | bytes 8388608 | tf_op jit(solution)/shard_map/attend/pallas_call | solution.py:193
  110.6 3.9 %all-to-all-start.2 = ((bf16[8,4,128,128]{3,2,1,0:T(8,128)(2,1)}), bf16[8,4,128,128]{3,2,1,0:T(8,128)(2,1)S(1)}, u32[]{:S(2)}, u32[]{:S(2)}) async-start(bf16[8,4,128,128]{3,2,1,0:T(8,128)(2,1)} %get-tuple-element.18), calls=%async_computation.2 | async-start | bytes 2097152 | tf_op jit(solution)/shard_map/all_to_all | solution.py:299
  114.5 30.5 %attend.3 = (bf16[8,4,128,128]{3,2,1,0:T(8,128)(2,1)}, f32[4,2,2,128,512]{4,3,2,1,0:T(8,128)}) custom-call(s32[4]{0:T(128)} %compare_select_fusion.refs_0_, bf16[8,8,128,128]{3,2,1,0:T(8,128)(2,1)} %all-to-all-done.3.refs_1_, bf16[8,3,128,128]{3,2,1,0:T(8,128)(2,1)} %copy-done.2, bf16[8,2,128,128]{3,2,1,0:T(8,128)(2,1)} %copy-done.8, ...), custom_call_target="tpu_custom_call" | custom-call | flops 24159191040 | bytes 8388608 | tf_op jit(solution)/shard_map/attend/pallas_call | solution.py:193
  145.0 5.7 %all-to-all-start.4 = ((bf16[8,4,128,128]{3,2,1,0:T(8,128)(2,1)}), bf16[8,4,128,128]{3,2,1,0:T(8,128)(2,1)S(1)}, u32[]{:S(2)}, u32[]{:S(2)}) async-start(bf16[8,4,128,128]{3,2,1,0:T(8,128)(2,1)} %get-tuple-element.21), calls=%async_computation.4 | async-start | bytes 2097152 | tf_op jit(solution)/shard_map/all_to_all | solution.py:299
  150.8 3.8 %split.1 = (f32[2,2,128,512]{3,2,1,0:T(8,128)}, bf16[2,2,128,512]{3,2,1,0:T(8,128)(2,1)}, bf16[2,2,128,512]{3,2,1,0:T(8,128)(2,1)}, bf16[2,2,128,512]{3,2,1,0:T(8,128)(2,1)}) custom-call(f32[4,2,2,128,512]{4,3,2,1,0:T(8,128)} %get-tuple-element.22.dkv_ref), custom_call_target="tpu_custom_call" | custom-call | tf_op jit(solution)/shard_map/split/pallas_call | solution.py:225
  154.6 0.5 collective-permute-start.3
  155.1 25.7 %collective-permute-start.4 = (bf16[2,2,128,512]{3,2,1,0:T(8,128)(2,1)}, bf16[2,2,128,512]{3,2,1,0:T(8,128)(2,1)S(1)}, u32[]{:S(2)}, u32[]{:S(2)}) collective-permute-start(bf16[2,2,128,512]{3,2,1,0:T(8,128)(2,1)} %get-tuple-element.25), channel_id=1, source_target_pairs={{0,112},{8,120},{16,0},{24,8},{32,16},{40,24},{48,32},{56,40},{64,... | collective-permute-start | bytes 1572872 | tf_op jit(solution)/shard_map/ppermute | solution.py:295
  180.8 0.5 collective-permute-start.5
  181.3 24.4 %collective-permute-done.4.two_ref = bf16[2,2,128,512]{3,2,1,0:T(8,128)(2,1)S(1)} collective-permute-done((bf16[2,2,128,512]{3,2,1,0:T(8,128)(2,1)}, bf16[2,2,128,512]{3,2,1,0:T(8,128)(2,1)S(1)}, u32[]{:S(2)}, u32[]{:S(2)}) %collective-permute-start.4) | collective-permute-done | bytes 524320 | tf_op jit(solution)/shard_map/ppermute | solution.py:295
  205.7 0.8 copy-done.6
  206.7 2.8 %total.1 = bf16[8,2,128,128]{3,2,1,0:T(8,128)(2,1)} custom-call(f32[2,2,128,512]{3,2,1,0:T(8,128)} %get-tuple-element.23.own_ref, bf16[2,2,128,512]{3,2,1,0:T(8,128)(2,1)} %copy-done.5, bf16[2,2,128,512]{3,2,1,0:T(8,128)(2,1)} %copy-done.6, bf16[2,2,128,512]{3,2,1,0:T(8,128)(2,1)} %copy-done.7), custom_call_target="tpu_custom_call" | custom-call | tf_op jit(solution)/shard_map/total/pallas_call | solution.py:247
  209.5 3.7 %all-to-all-start.5 = ((bf16[8,2,128,128]{3,2,1,0:T(8,128)(2,1)}), bf16[8,2,128,128]{3,2,1,0:T(8,128)(2,1)S(1)}, u32[]{:S(2)}, u32[]{:S(2)}) async-start(bf16[8,2,128,128]{3,2,1,0:T(8,128)(2,1)} %total.1), calls=%async_computation.5 | async-start | bytes 1048576 | tf_op jit(solution)/shard_map/all_to_all | solution.py:299
  213.2 5.9 %unpack_q.1 = bf16[128,8192]{1,0:T(8,128)(2,1)} custom-call(bf16[8,4,128,128]{3,2,1,0:T(8,128)(2,1)} %copy-done, bf16[8,4,128,128]{3,2,1,0:T(8,128)(2,1)} %copy-done.1), custom_call_target="tpu_custom_call" | custom-call | tf_op jit(solution)/shard_map/unpack_q/pallas_call | solution.py:265
  219.1 3.6 %all-to-all-done.5.pair_ref = bf16[8,2,128,128]{3,2,1,0:T(8,128)(2,1)S(1)} async-done(((bf16[8,2,128,128]{3,2,1,0:T(8,128)(2,1)}), bf16[8,2,128,128]{3,2,1,0:T(8,128)(2,1)S(1)}, u32[]{:S(2)}, u32[]{:S(2)}) %all-to-all-start.5) | async-done | bytes 524320 | tf_op jit(solution)/shard_map/all_to_all | solution.py:299
  222.7 0.8 copy-done.4
  223.5 2.0 unpack_kv.1
  (30 shorter events, 0.4 us)
Async XLA Ops:
  30.5 3.6 %copy-start.2 = (bf16[8,3,128,128]{3,2,1,0:T(8,128)(2,1)}, bf16[8,3,128,128]{3,2,1,0:T(8,128)(2,1)S(1)}, u32[]{:S(2)}) copy-start(bf16[8,3,128,128]{3,2,1,0:T(8,128)(2,1)S(1)} %all_to_all.30.refs_2_) | copy-start | bytes 2359300
  30.5 42.4 %all-to-all-start = ((bf16[8,8,128,128]{3,2,1,0:T(8,128)(2,1)}), bf16[8,8,128,128]{3,2,1,0:T(8,128)(2,1)S(1)}, u32[]{:S(2)}, u32[]{:S(2)}) async-start(bf16[8,8,128,128]{3,2,1,0:T(8,128)(2,1)} %get-tuple-element.16), calls=%async_computation | async-start | bytes 4194304 | tf_op jit(solution)/shard_map/all_to_all | solution.py:299
  34.2 17.9 %collective-permute-start = (bf16[8,2,128,128]{3,2,1,0:T(8,128)(2,1)S(1)}, bf16[8,2,128,128]{3,2,1,0:T(8,128)(2,1)S(1)}, u32[]{:S(2)}, u32[]{:S(2)}) collective-permute-start(bf16[8,2,128,128]{3,2,1,0:T(8,128)(2,1)S(1)} %slice.4), channel_id=1, source_target_pairs={{0,8},{8,16},{16,24},{24,32},{32,40},{40,48},{48,56},{56,64},{64,7... | collective-permute-start | bytes 1572872 | tf_op jit(solution)/shard_map/ppermute | solution.py:295
  52.1 20.8 %copy-start.8 = (bf16[8,2,128,128]{3,2,1,0:T(8,128)(2,1)}, bf16[8,2,128,128]{3,2,1,0:T(8,128)(2,1)S(1)}, u32[]{:S(2)}) copy-start(bf16[8,2,128,128]{3,2,1,0:T(8,128)(2,1)S(1)} %collective-permute-done.refs_3_) | copy-start | bytes 1572868
  52.1 16.9 %collective-permute-start.1 = (bf16[8,2,128,128]{3,2,1,0:T(8,128)(2,1)S(1)}, bf16[8,2,128,128]{3,2,1,0:T(8,128)(2,1)S(1)}, u32[]{:S(2)}, u32[]{:S(2)}) collective-permute-start(bf16[8,2,128,128]{3,2,1,0:T(8,128)(2,1)S(1)} %collective-permute-done.refs_3_), channel_id=1, source_target_pairs={{0,8},{8,16},{16,24},{24,32},{32,40},{40,48},{48,56},{56,64},{64,7... | collective-permute-start | bytes 1572872 | tf_op jit(solution)/shard_map/ppermute | solution.py:295
  69.1 3.9 %copy-start.9 = (bf16[8,2,128,128]{3,2,1,0:T(8,128)(2,1)}, bf16[8,2,128,128]{3,2,1,0:T(8,128)(2,1)S(1)}, u32[]{:S(2)}) copy-start(bf16[8,2,128,128]{3,2,1,0:T(8,128)(2,1)S(1)} %collective-permute-done.1.refs_4_) | copy-start | bytes 1572868
  69.1 12.3 %collective-permute-start.2 = (bf16[8,2,128,128]{3,2,1,0:T(8,128)(2,1)S(1)}, bf16[8,2,128,128]{3,2,1,0:T(8,128)(2,1)}, u32[]{:S(2)}, u32[]{:S(2)}) collective-permute-start(bf16[8,2,128,128]{3,2,1,0:T(8,128)(2,1)S(1)} %collective-permute-done.1.refs_4_), channel_id=1, source_target_pairs={{0,8},{8,16},{16,24},{24,32},{32,40},{40,48},{48,56},{56,64},{64,7... | collective-permute-start | bytes 1572872 | tf_op jit(solution)/shard_map/ppermute | solution.py:295
  72.9 1.3 copy-start.3
  74.2 36.4 %all-to-all-start.3 = ((bf16[8,8,128,128]{3,2,1,0:T(8,128)(2,1)}), bf16[8,8,128,128]{3,2,1,0:T(8,128)(2,1)}, u32[]{:S(2)}, u32[]{:S(2)}) async-start(bf16[8,8,128,128]{3,2,1,0:T(8,128)(2,1)} %get-tuple-element.19), calls=%async_computation.3 | async-start | bytes 4194304 | tf_op jit(solution)/shard_map/all_to_all | solution.py:299
  110.6 34.4 %all-to-all-start.2 = ((bf16[8,4,128,128]{3,2,1,0:T(8,128)(2,1)}), bf16[8,4,128,128]{3,2,1,0:T(8,128)(2,1)S(1)}, u32[]{:S(2)}, u32[]{:S(2)}) async-start(bf16[8,4,128,128]{3,2,1,0:T(8,128)(2,1)} %get-tuple-element.18), calls=%async_computation.2 | async-start | bytes 2097152 | tf_op jit(solution)/shard_map/all_to_all | solution.py:299
  145.0 9.5 %copy-start = (bf16[8,4,128,128]{3,2,1,0:T(8,128)(2,1)}, bf16[8,4,128,128]{3,2,1,0:T(8,128)(2,1)S(1)}, u32[]{:S(2)}) copy-start(bf16[8,4,128,128]{3,2,1,0:T(8,128)(2,1)S(1)} %all-to-all-done.2.refs_0_) | copy-start | bytes 3145732
  145.0 64.5 %all-to-all-start.4 = ((bf16[8,4,128,128]{3,2,1,0:T(8,128)(2,1)}), bf16[8,4,128,128]{3,2,1,0:T(8,128)(2,1)S(1)}, u32[]{:S(2)}, u32[]{:S(2)}) async-start(bf16[8,4,128,128]{3,2,1,0:T(8,128)(2,1)} %get-tuple-element.21), calls=%async_computation.4 | async-start | bytes 2097152 | tf_op jit(solution)/shard_map/all_to_all | solution.py:299
  154.6 26.7 %collective-permute-start.3 = (bf16[2,2,128,512]{3,2,1,0:T(8,128)(2,1)}, bf16[2,2,128,512]{3,2,1,0:T(8,128)(2,1)S(1)}, u32[]{:S(2)}, u32[]{:S(2)}) collective-permute-start(bf16[2,2,128,512]{3,2,1,0:T(8,128)(2,1)} %get-tuple-element.24), channel_id=1, source_target_pairs={{0,120},{8,0},{16,8},{24,16},{32,24},{40,32},{48,40},{56,48},{64,5... | collective-permute-start | bytes 1572872 | tf_op jit(solution)/shard_map/ppermute | solution.py:295
  155.1 50.6 %collective-permute-start.4 = (bf16[2,2,128,512]{3,2,1,0:T(8,128)(2,1)}, bf16[2,2,128,512]{3,2,1,0:T(8,128)(2,1)S(1)}, u32[]{:S(2)}, u32[]{:S(2)}) collective-permute-start(bf16[2,2,128,512]{3,2,1,0:T(8,128)(2,1)} %get-tuple-element.25), channel_id=1, source_target_pairs={{0,112},{8,120},{16,0},{24,8},{32,16},{40,24},{48,32},{56,40},{64,... | collective-permute-start | bytes 1572872 | tf_op jit(solution)/shard_map/ppermute | solution.py:295
  180.8 25.0 %collective-permute-start.5 = (bf16[2,2,128,512]{3,2,1,0:T(8,128)(2,1)}, bf16[2,2,128,512]{3,2,1,0:T(8,128)(2,1)S(1)}, u32[]{:S(2)}, u32[]{:S(2)}) collective-permute-start(bf16[2,2,128,512]{3,2,1,0:T(8,128)(2,1)} %get-tuple-element.26), channel_id=1, source_target_pairs={{0,104},{8,112},{16,120},{24,0},{32,8},{40,16},{48,24},{56,32},{64... | collective-permute-start | bytes 1572872 | tf_op jit(solution)/shard_map/ppermute | solution.py:295
  181.3 24.5 %copy-start.5 = (bf16[2,2,128,512]{3,2,1,0:T(8,128)(2,1)}, bf16[2,2,128,512]{3,2,1,0:T(8,128)(2,1)S(1)}, u32[]{:S(2)}) copy-start(bf16[2,2,128,512]{3,2,1,0:T(8,128)(2,1)S(1)} %collective-permute-done.3.one_ref) | copy-start | bytes 1572868
  205.7 0.8 copy-start.6
  205.7 1.0 copy-start.7
  209.5 3.7 %copy-start.1 = (bf16[8,4,128,128]{3,2,1,0:T(8,128)(2,1)}, bf16[8,4,128,128]{3,2,1,0:T(8,128)(2,1)S(1)}, u32[]{:S(2)}) copy-start(bf16[8,4,128,128]{3,2,1,0:T(8,128)(2,1)S(1)} %all-to-all-done.4.refs_1_) | copy-start | bytes 3145732
  209.5 13.2 %all-to-all-start.5 = ((bf16[8,2,128,128]{3,2,1,0:T(8,128)(2,1)}), bf16[8,2,128,128]{3,2,1,0:T(8,128)(2,1)S(1)}, u32[]{:S(2)}, u32[]{:S(2)}) async-start(bf16[8,2,128,128]{3,2,1,0:T(8,128)(2,1)} %total.1), calls=%async_computation.5 | async-start | bytes 1048576 | tf_op jit(solution)/shard_map/all_to_all | solution.py:299
  222.7 0.8 copy-start.4

commit v2 on v1

v2 whole, which is shorter than its diff:
```python
import functools
import math

import jax
import jax.numpy as jnp
from jax import lax
from jax.experimental import pallas as pl
from jax.experimental.pallas import tpu as pltpu
from jax.sharding import PartitionSpec as P

HD = 128
STEPS = 4
DOCS = 8
TOK = 128
HEADS_DEV = 8
HALF = 512
CHUNKS = (3, 3, 2)
PARTS = 3
FAR = 32768.0
SCALE = HD ** (-0.5)
EXP2_SCALE = SCALE * math.log2(math.e)
NORM_SCALE = HD ** 0.5
BF = jnp.bfloat16
F32 = jnp.float32
BM, BN, PIPE = 256, 256, True
BM, BN = 256, 256
PACK_PER = 4
VMEM_LIMIT = 60 * 1024 * 1024

NN = (((1,), (0,)), ((), ()))
NT = (((1,), (1,)), ((), ()))


def dot(a, b, dims=NN):
    return lax.dot_general(a, b, dims, preferred_element_type=F32)


def parts_of(x):
    high = x.astype(BF)
    rest = x - high.astype(F32)
    mid = rest.astype(BF)
    low = (rest - mid.astype(F32)).astype(BF)
    return high, mid, low


def pack_kv_kernel(k_ref, v_ref, kv_ref):
    for u in range(8):
        kv_ref[u, 0] = k_ref[:, u * HD : (u + 1) * HD].T
        kv_ref[u, 1] = v_ref[:, u * HD : (u + 1) * HD].T


def pack_kv(key_rows, value_rows):
    return pl.pallas_call(
        pack_kv_kernel,
        out_shape=jax.ShapeDtypeStruct((8, 2, HD, TOK), BF),
        compiler_params=pltpu.CompilerParams(vmem_limit_bytes=VMEM_LIMIT),
        cost_estimate=pl.CostEstimate(flops=0, bytes_accessed=1 << 20, transcendentals=0),
        name="pack_kv",
    )(key_rows, value_rows)


def pack_q_kernel(per, q_ref, do_ref, o_ref, ln_ref, doc_ref, _, *refs):
    *qd_refs, pick_ref = refs
    step = pl.program_id(0)
    heads = ln_ref.shape[1]
    width = HEADS_DEV * HD

    @pl.when(step == 0)
    def _():
        head = lax.broadcasted_iota(jnp.int32, pick_ref.shape, 0) // HD
        col = lax.broadcasted_iota(jnp.int32, pick_ref.shape, 1)
        pick = (col >= 24) & (col < 48) & (head == col % HEADS_DEV)
        pick_ref[...] = jnp.where(pick, 1.0, 0.0).astype(BF)

    head = lax.broadcasted_iota(jnp.int32, (heads, 128), 0)
    col = lax.broadcasted_iota(jnp.int32, (heads, 128), 1)
    lane = lax.broadcasted_iota(jnp.int32, (TOK, 128), 1)
    norm_parts = parts_of(ln_ref[...] * NORM_SCALE)
    for i in range(per):
        first = i * width
        norm = jnp.zeros((TOK, 128), F32)
        for j, part in enumerate(norm_parts):
            mine = head == (step * per + i) * HEADS_DEV + col % HEADS_DEV
            pick = (col // HEADS_DEV == j) & mine
            norm += dot(part, jnp.where(pick, 1.0, 0.0).astype(BF))
        cols = slice(first, first + width)
        high, low, _ = parts_of(do_ref[:, cols].astype(F32) * o_ref[:, cols].astype(F32))
        delta = dot(high, pick_ref[...]) + dot(low, pick_ref[...])
        high, mid, low = parts_of(delta)
        delta = jnp.where(lane < 32, high, jnp.where(lane < 40, mid, low))
        stats = jnp.where(lane < 24, norm.astype(BF), jnp.where(lane < 48, delta, doc_ref[...]))
        h = 0
        for index, ref in enumerate(qd_refs):
            count = ref.shape[1] // 2
            for c in range(count):
                cols = slice(first + h * HD, first + (h + 1) * HD)
                ref[i, c] = q_ref[:, cols]
                ref[i, count + c] = do_ref[:, cols]
                h += 1
            if index == 0:
                ref[i, 2 * count] = stats


def pack_q(queries, grad_out, attn_out, log_norm, doc_block, after):
    per = PACK_PER
    wide = pl.BlockSpec((TOK, per * HEADS_DEV * HD), lambda u: (0, u))
    shapes = [(8, 2 * c + (i == 0), TOK, HD) for i, c in enumerate(CHUNKS)]
    return pl.pallas_call(
        functools.partial(pack_q_kernel, per),
        grid=(8 // per,),
        in_specs=[
            wide,
            wide,
            wide,
            pl.BlockSpec(log_norm.shape, lambda u: (0, 0)),
            pl.BlockSpec(doc_block.shape, lambda u: (0, 0)),
            pl.BlockSpec(memory_space=pl.ANY),
        ],
        out_specs=[pl.BlockSpec((per,) + s[1:], lambda u: (u, 0, 0, 0)) for s in shapes],
        out_shape=[jax.ShapeDtypeStruct(s, BF) for s in shapes],
        scratch_shapes=[pltpu.VMEM((HEADS_DEV * HD, 128), BF)],
        compiler_params=pltpu.CompilerParams(vmem_limit_bytes=VMEM_LIMIT),
        cost_estimate=pl.CostEstimate(flops=0, bytes_accessed=11 << 20, transcendentals=0),
        name="pack_q",
    )(queries, grad_out, attn_out, log_norm, doc_block, after)


def attend_kernel(steps, count, first_head, kv_counts, has_dkv, has_dq, afters, last_dq, last_dkv, *refs):
    refs = list(refs)

    def take(n):
        head = refs[:n]
        del refs[:n]
        return head

    second_ref, qd_ref, stat_ref = take(3)
    kv_refs = [take(n) for n in kv_counts]
    (kdoc_ref,) = take(1)
    dkv_in = take(len(steps)) if has_dkv else None
    (dq_in,) = take(1) if has_dq else (None,)
    take(afters)
    (dq_ref,) = take(1)
    dkv_refs = take(len(steps))
    qt_ref, dot_ref, sel_ref, kv_ref, p_ref, ds_ref = take(6)
    (dqt_ref,) = take(1) if last_dq else (dq_ref,)
    sum_refs = take(len(steps)) if last_dkv else dkv_refs

    row = lax.broadcasted_iota(jnp.int32, (48, HALF), 0)
    for h in range(count):
        mine = row % HEADS_DEV == first_head + h
        sel_ref[h] = jnp.where(mine & (row < 24), -1.0, 0.0).astype(BF)
        sel_ref[count + h] = jnp.where(mine & (row >= 24), -1.0, 0.0).astype(BF)
    for half in range(2):
        for i in range(4):
            cols = slice(i * TOK, (i + 1) * TOK)
            for index, sources in enumerate(kv_refs):
                for pair in range(2):
                    block = sources[0][half * 4 + i, pair]
                    for other in sources[1:]:
                        block = block + other[half * 4 + i, pair]
                    kv_ref[index, pair, half, :, cols] = block
    if has_dq:
        dqt_ref[...] = dq_in[...]
    else:
        dqt_ref[...] = jnp.zeros_like(dqt_ref)
    for index in range(len(steps)):
        if has_dkv:
            sum_refs[index][...] = dkv_in[index][...]
        else:
            sum_refs[index][...] = jnp.zeros_like(sum_refs[index])

    def turn_rows(half):
        for i in range(4):
            cols = slice(i * TOK, (i + 1) * TOK)
            for h in range(count):
                qt_ref[half, h, :, cols] = qd_ref[half * 4 + i, h].T
                dot_ref[half, h, :, cols] = qd_ref[half * 4 + i, count + h].T

    def rows_of(qhalf, index, q0, qn):
        block = qd_ref[pl.ds(qhalf * 4 + q0 // TOK, qn // TOK), index]
        return block.reshape(qn, HD)

    def scores(index, qhalf, khalf, h, slot, q0, k0, bm, bn, diagonal):
        kcols = slice(k0, k0 + bn)
        k_ext = jnp.concatenate(
            [
                kv_ref[index, 0, khalf, :, kcols],
                sel_ref[h, :, kcols],
                kdoc_ref[steps[index], khalf, :, kcols],
                jnp.zeros((64, bn), BF),
            ],
            axis=0,
        )
        v_ext = jnp.concatenate(
            [kv_ref[index, 1, khalf, :, kcols], sel_ref[count + h, :, kcols], jnp.zeros((80, bn), BF)],
            axis=0,
        )
        stats = stat_ref[pl.ds(qhalf * 4 + q0 // TOK, bm // TOK), 0].reshape(bm, HD)
        q_ext = jnp.concatenate([rows_of(qhalf, h, q0, bm), stats], axis=1)
        do_ext = jnp.concatenate([rows_of(qhalf, count + h, q0, bm), stats], axis=1)
        prob = jnp.exp2(dot(q_ext, k_ext) * EXP2_SCALE)
        if diagonal:
            qi = lax.broadcasted_iota(jnp.int32, (bm, bn), 0) + q0
            ki = lax.broadcasted_iota(jnp.int32, (bm, bn), 1) + k0
            prob = jnp.where(qi >= ki, prob, 0.0)
        rows = slice(q0, q0 + bm)
        ds_ref[slot, rows, kcols] = (prob * dot(do_ext, v_ext)).astype(BF)
        p_ref[slot, rows, kcols] = prob.astype(BF)

    def grads(index, qhalf, khalf, h, slot, diagonal):
        for k0, kn, q0 in ((0, 256, 0), (256, 256, 256)) if diagonal else ((0, HALF, 0),):
            span = slice(q0, HALF)
            cols = slice(k0, k0 + kn)
            sum_refs[index][1, khalf, :, cols] += dot(dot_ref[qhalf, h, :, span], p_ref[slot, span, cols])
            sum_refs[index][0, khalf, :, cols] += dot(qt_ref[qhalf, h, :, span], ds_ref[slot, span, cols])
        for q0, qn, kn in ((0, 256, 256), (256, 256, 512)) if diagonal else ((0, HALF, HALF),):
            span = slice(q0, q0 + qn)
            dqt_ref[qhalf, h, :, span] += dot(kv_ref[index, 0, khalf, :, :kn], ds_ref[slot, span, :kn], NT)

    def tile(index, qhalf, khalf, diagonal):
        for h in range(count):
            for k0 in range(0, HALF, BN):
                for q0 in range(0, HALF, BM):
                    if diagonal and q0 + BM <= k0:
                        if q0 >= k0 // 256 * 256:
                            ds_ref[h % 2, q0 : q0 + BM, k0 : k0 + BN] = jnp.zeros((BM, BN), BF)
                            p_ref[h % 2, q0 : q0 + BM, k0 : k0 + BN] = jnp.zeros((BM, BN), BF)
                        continue
                    scores(index, qhalf, khalf, h, h % 2, q0, k0, BM, BN, diagonal and q0 < k0 + BN)
            if PIPE and h > 0:
                grads(index, qhalf, khalf, h - 1, (h - 1) % 2, diagonal)
            if not PIPE:
                grads(index, qhalf, khalf, h, h % 2, diagonal)
        if PIPE:
            grads(index, qhalf, khalf, count - 1, (count - 1) % 2, diagonal)

    for index, step in enumerate(steps):
        if step == 0:

            def diagonal(half, carry, index=index):
                if index == 0:
                    turn_rows(half)
                tile(index, half, half, True)
                return carry

            lax.fori_loop(0, 2, diagonal, 0)
            tile(index, 1, 0, False)
        else:

            def both(turn, carry, index=index, step=step):
                second = second_ref[step]
                if index == 0:
                    turn_rows(1 - turn)
                tile(index, jnp.where(turn == 0, 1, second), jnp.where(turn == 0, 0, second), False)
                return carry

            lax.fori_loop(0, 2, both, 0)

    if last_dq:
        for half in range(2):
            for h in range(count):
                for i in range(4):
                    piece = dqt_ref[half, h, :, i * TOK : (i + 1) * TOK]
                    dq_ref[half * 4 + i, h] = (piece * SCALE).astype(BF).T
    if last_dkv:
        for total_ref, sum_ref in zip(dkv_refs, sum_refs):
            total_ref[0] = (sum_ref[0] * SCALE).astype(total_ref.dtype)
            total_ref[1] = sum_ref[1].astype(total_ref.dtype)


def attend(steps, chunk, second, qd, stats, kvs, kdoc, dkv, dq, last_dq, dkv_type, afters=()):
    first_head, count = sum(CHUNKS[:chunk]), CHUNKS[chunk]
    operands = [second, qd, stats]
    kvs = [kvs[step] for step in steps]
    for sources in kvs:
        operands += sources
    operands.append(kdoc)
    operands += [] if dkv is None else [dkv[step] for step in steps]
    operands += [] if dq is None else [dq]
    vmem = pl.BlockSpec(memory_space=pltpu.VMEM)
    stat_index = stats.shape[1] - 1
    stat_spec = pl.BlockSpec((8, 1, TOK, HD), lambda i: (0, stat_index, 0, 0))
    tiles = sum(2.5 if step == 0 else 2 for step in steps)
    flops = int(tiles * 5 * 2 * HALF * HALF * HD * count)
    partial_dq = (2, count, HD, HALF)
    sums = (2, 2, HD, HALF)
    kernel = functools.partial(
        attend_kernel,
        steps,
        count,
        first_head,
        [len(sources) for sources in kvs],
        dkv is not None,
        dq is not None,
        len(afters),
        last_dq,
        dkv_type is not None,
    )
    dq, *dkv = pl.pallas_call(
        kernel,
        grid=(1,),
        in_specs=[pl.BlockSpec(memory_space=pltpu.SMEM), vmem, stat_spec]
        + [vmem] * (len(operands) - 3)
        + [pl.BlockSpec(memory_space=pl.ANY)] * len(afters),
        out_specs=[vmem] * (1 + len(steps)),
        out_shape=[
            jax.ShapeDtypeStruct((8, count, TOK, HD) if last_dq else partial_dq, BF if last_dq else F32),
        ]
        + [jax.ShapeDtypeStruct(sums, dkv_type or F32)] * len(steps),
        scratch_shapes=[
            pltpu.VMEM((2, count, HD, HALF), BF),
            pltpu.VMEM((2, count, HD, HALF), BF),
            pltpu.VMEM((2 * count, 48, HALF), BF),
            pltpu.VMEM((len(steps), 2, 2, HD, HALF), BF),
            pltpu.VMEM((2, HALF, HALF), BF),
            pltpu.VMEM((2, HALF, HALF), BF),
        ]
        + ([pltpu.VMEM(partial_dq, F32)] if last_dq else [])
        + ([pltpu.VMEM(sums, F32)] * len(steps) if dkv_type is not None else []),
        compiler_params=pltpu.CompilerParams(vmem_limit_bytes=VMEM_LIMIT),
        cost_estimate=pl.CostEstimate(
            flops=2 * flops, bytes_accessed=8 << 20, transcendentals=int(tiles) * HALF * HALF * count
        ),
        name="attend",
    )(*operands, *afters)
    return dq, dict(zip(steps, dkv))


def join_kernel(one_ref, two_ref, inner_two_ref, inner_three_ref, to_one_ref, to_two_ref):
    to_one_ref[...] = (one_ref[...].astype(F32) + inner_two_ref[...].astype(F32)).astype(BF)
    to_two_ref[...] = (two_ref[...].astype(F32) + inner_three_ref[...].astype(F32)).astype(BF)


def join(*parts):
    shape = jax.ShapeDtypeStruct((2, 2, HD, HALF), BF)
    return pl.pallas_call(
        join_kernel,
        out_shape=[shape, shape],
        compiler_params=pltpu.CompilerParams(vmem_limit_bytes=VMEM_LIMIT),
        cost_estimate=pl.CostEstimate(flops=0, bytes_accessed=3 << 20, transcendentals=0),
        name="join",
    )(*parts)


def total_kernel(own_ref, *refs):
    *part_refs, out_ref = refs
    for pair in range(2):
        for half in range(2):
            total = own_ref[pair, half]
            for ref in part_refs:
                total += ref[pair, half].astype(F32)
            for i in range(4):
                out_ref[half * 4 + i, pair] = total[:, i * TOK : (i + 1) * TOK].astype(BF).T


def total(*parts):
    return pl.pallas_call(
        total_kernel,
        out_shape=jax.ShapeDtypeStruct((8, 2, TOK, HD), BF),
        compiler_params=pltpu.CompilerParams(vmem_limit_bytes=VMEM_LIMIT),
        cost_estimate=pl.CostEstimate(flops=0, bytes_accessed=4 << 20, transcendentals=0),
        name="total",
    )(*parts)


def unpack_q_kernel(per, *refs):
    out_ref = refs[-1]
    for u in range(per):
        h = u * HEADS_DEV
        for ref in refs[:-1]:
            for i in range(ref.shape[1]):
                out_ref[:, h * HD : (h + 1) * HD] = ref[u, i]
                h += 1


def unpack_q(parts):
    per = PACK_PER
    return pl.pallas_call(
        functools.partial(unpack_q_kernel, per),
        grid=(8 // per,),
        in_specs=[pl.BlockSpec((per,) + p.shape[1:], lambda u: (u, 0, 0, 0)) for p in parts],
        out_specs=pl.BlockSpec((TOK, per * HEADS_DEV * HD), lambda u: (0, u)),
        out_shape=jax.ShapeDtypeStruct((TOK, 8 * HEADS_DEV * HD), BF),
        compiler_params=pltpu.CompilerParams(vmem_limit_bytes=VMEM_LIMIT),
        cost_estimate=pl.CostEstimate(flops=0, bytes_accessed=4 << 20, transcendentals=0),
        name="unpack_q",
    )(*parts)


def unpack_kv_kernel(pair_ref, k_ref, v_ref):
    for u in range(8):
        k_ref[:, u * HD : (u + 1) * HD] = pair_ref[u, 0]
        v_ref[:, u * HD : (u + 1) * HD] = pair_ref[u, 1]


def unpack_kv(pair):
    shape = jax.ShapeDtypeStruct((TOK, 8 * HD), BF)
    return pl.pallas_call(
        unpack_kv_kernel,
        out_shape=[shape, shape],
        compiler_params=pltpu.CompilerParams(vmem_limit_bytes=VMEM_LIMIT),
        name="unpack_kv",
    )(pair)


def move(value, pairs):
    return lax.ppermute(value, "blk", pairs)


def exchange(value):
    return lax.all_to_all(value, "uly", split_axis=0, concat_axis=0, tiled=True)


def local(queries, key_rows, value_rows, grad_out, attn_out, log_norm, doc_ids):
    groups = lax.axis_size("blk")
    group = lax.axis_index("blk")
    member = lax.axis_index("uly")

    first = jnp.where(
        member < 4, group * HALF + member * TOK, (2 * groups - 1 - group) * HALF + (member - 4) * TOK
    )
    my_docs = lax.dynamic_slice_in_dim(doc_ids, first, TOK)
    lane = jnp.arange(128, dtype=jnp.int32)[None, :]
    doc_block = jnp.where(
        (lane >= 48) & (lane < 48 + DOCS) & (my_docs[:, None] != lane - 48), FAR, 0.0
    ).astype(BF)

    kdocs = []
    for step in range(STEPS):
        owner = (group - step) % groups
        low = lax.dynamic_slice_in_dim(doc_ids, owner * HALF, HALF)
        high = lax.dynamic_slice_in_dim(doc_ids, (2 * groups - 1 - owner) * HALF, HALF)
        kdocs.append(jnp.stack([low, high]))
    kdocs = jnp.stack(kdocs)
    kdoc = jnp.where(
        kdocs[:, :, None, :] == jnp.arange(16, dtype=jnp.int32)[None, None, :, None], -1.0, 0.0
    ).astype(BF)
    second = jnp.where(group >= jnp.arange(STEPS), 0, 1).astype(jnp.int32)

    chips = range(groups // 2)
    up = [(i, (i + 1) % groups) for i in range(groups)]
    inner_up = [(2 * m, 2 * m + 1) for m in chips]
    inner_down = [(2 * m + 1, 2 * m) for m in chips]
    down = [[(2 * m, (2 * m - step) % groups) for m in chips] for step in range(STEPS)]

    kv = exchange(pack_kv(key_rows, value_rows))
    one = move(kv, up)
    two, three = (move(kv, [(b, a) for a, b in down[step]]) for step in (2, 3))
    two_inner, three_inner = (move(part, inner_up) for part in (one, two))
    kvs = [[kv], [one], [two, two_inner], [three, three_inner]]

    qds = pack_q(queries, grad_out, attn_out, log_norm, doc_block, kv)
    qds = [exchange(qd) for qd in qds]
    stats = qds[0]
    dkv = None
    dqs = []
    for chunk in range(len(CHUNKS) - 1):
        dq, dkv = attend(
            (0, 1, 2, 3), chunk, second, qds[chunk], stats, kvs, kdoc, dkv, None, True, None
        )
        dqs.append(exchange(dq))
    args = (len(CHUNKS) - 1, second, qds[-1], stats, kvs, kdoc, dkv)
    dq, far = attend((2, 3), *args, None, False, BF)
    inner_two, inner_three = (move(far[step], inner_down) for step in (2, 3))
    from_three = move(far[3], down[3])
    dq, near = attend((1,), *args, dq, False, BF, dqs[:1])
    inner_one = move(near[1], inner_down)
    to_one, to_two = join(near[1], far[2], inner_two, inner_three)
    from_one, from_two = move(to_one, down[1]), move(to_two, down[2])
    dq, own = attend((0,), *args, dq, True, F32, (to_one,))
    dqs.append(exchange(dq))
    pair = exchange(total(own[0], inner_one, from_one, from_two, from_three))
    grad_keys, grad_values = unpack_kv(pair)
    return unpack_q(dqs), grad_keys, grad_values


def solution(mesh):
    rows = P(("blk", "uly"), None)
    return jax.shard_map(
        local,
        mesh=mesh,
        in_specs=(rows, rows, rows, rows, rows, rows, P()),
        out_specs=(rows, rows, rows),
        check_vma=False,
    )
```

time: 227 us -> 222 us (0.978)
  waiting for transfers between devices: 54.3 us -> 42.8 us
    ppermute x6 -> x11, waiting for transfers between devices: 50.7 us -> 23.9 us  [move(): return lax.ppermute(value, 'blk', pairs)]
    all_to_all x5 -> x7, waiting for transfers between devices: 3.58 us -> 18.9 us  [exchange(): return lax.all_to_all(value, 'uly', split_axis=0, concat_axis=0, tiled=True)]
    all_to_all x5 -> x7, starting transfers between devices: 22.3 us -> 33.6 us  [exchange(): return lax.all_to_all(value, 'uly', split_axis=0, concat_axis=0, tiled=True)]
    ppermute x6 -> x11, starting transfers between devices: 38.9 us -> 29.6 us  [move(): return lax.ppermute(value, 'blk', pairs)]
    unnamed x21 -> x31, local copies, waits for them, and re-layouts: 4.59 us -> 6.17 us
    pallas_call x5 -> x9, Pallas kernels: 77.7 us -> 78.9 us  [the longest x5 65.8 us: attend(): pl.pallas_call(kernel, grid=(1,), in_specs=[pl.BlockSpec(memory_space=plt...]
  transfers between devices with their start and end apart: 11 -> 18, of which waited for: 5 -> 5; matrix products, arithmetic and copies ran while one was open for 1% -> 2% of each run, Pallas kernels for 32% -> 34%
where the time goes in v2:
time: 222 us; the launch traced here: 221 us
  Pallas kernels  83.9 us (38%)
  starting transfers between devices  63.2 us (28%)
  waiting for transfers between devices  42.8 us (19%)
  blocking collectives  20 us (9%)
  local copies, waits for them, and re-layouts  7.83 us (4%)
    pallas_call x5, Pallas kernels, attend(): pl.pallas_call(kernel, grid=(1,), in_specs=[pl.BlockSpec(memory_space=plt...  65.8 us
    all_to_all x7, starting transfers between devices, exchange(): return lax.all_to_all(value, 'uly', split_axis=0, concat_axis=0, tiled=True)  33.6 us
    ppermute x11, starting transfers between devices, move(): return lax.ppermute(value, 'blk', pairs)  29.6 us
    ppermute x11, waiting for transfers between devices, move(): return lax.ppermute(value, 'blk', pairs)  23.9 us
    all_to_all x1, blocking collectives, exchange(): return lax.all_to_all(value, 'uly', split_axis=0, concat_axis=0, tiled=True)  20 us
    all_to_all x7, waiting for transfers between devices, exchange(): return lax.all_to_all(value, 'uly', split_axis=0, concat_axis=0, tiled=True)  18.9 us
    unnamed x31, local copies, waits for them, and re-layouts  6.17 us
    pallas_call x1, Pallas kernels, pack_q(): pl.pallas_call(functools.partial(pack_q_kernel, per), grid=(8 // per,), i...  5.68 us
  transfers between devices with their start and end apart: 18, of which 5 were waited for; matrix products, arithmetic and copies ran while one was open for 2% of the time, Pallas kernels for 34%

profile of v2, /device:TPU:0, one launch (start us, length us, event | category | flops | bytes accessed | tf_op | source)
XLA Modules:
  0.0 220.8 jit_solution(1099353779571860989)
XLA Ops:
  0.6 2.0 pack_kv.1
  2.7 5.7 %all-to-all-start = ((bf16[8,2,128,128]{3,2,1,0:T(8,128)(2,1)}), bf16[8,2,128,128]{3,2,1,0:T(8,128)(2,1)S(1)}, u32[]{:S(2)}, u32[]{:S(2)}) async-start(bf16[8,2,128,128]{3,2,1,0:T(8,128)(2,1)} %pack_kv.1), calls=%async_computation | async-start | bytes 1048576 | tf_op jit(solution)/shard_map/all_to_all | solution.py:411
  10.6 7.9 %all-to-all-done._.refs_3_ = bf16[8,2,128,128]{3,2,1,0:T(8,128)(2,1)S(1)} async-done(((bf16[8,2,128,128]{3,2,1,0:T(8,128)(2,1)}), bf16[8,2,128,128]{3,2,1,0:T(8,128)(2,1)S(1)}, u32[]{:S(2)}, u32[]{:S(2)}) %all-to-all-start) | async-done | bytes 524320 | tf_op jit(solution)/shard_map/all_to_all | solution.py:411
  19.3 5.7 %pack_q.1 = (bf16[8,7,128,128]{3,2,1,0:T(8,128)(2,1)}, bf16[8,6,128,128]{3,2,1,0:T(8,128)(2,1)}, bf16[8,4,128,128]{3,2,1,0:T(8,128)(2,1)}) custom-call(bf16[128,8192]{1,0:T(8,128)(2,1)} %q_ref.1, bf16[128,8192]{1,0:T(8,128)(2,1)} %do_ref.1, bf16[128,8192]{1,0:T(8,128)(2,1)} %o_ref.1, f32[128,64]{1,0:T(8,128)} %copy.10.ln_ref, ...), custom_call_target="tpu_custom_call" | custom-call | bytes 11534336 | tf_op jit(solution)/shard_map/pack_q/pallas_call | solution.py:108
  24.9 20.0 %all_to_all.40.refs_1_ = bf16[8,4,128,128]{3,2,1,0:T(8,128)(2,1)} all-to-all(bf16[8,4,128,128]{3,2,1,0:T(8,128)(2,1)} %get-tuple-element.35), channel_id=1, replica_groups=mesh['blk'=16,'uly'=8] {'uly'}, dimensions={0} | all-to-all | bytes 2097152 | tf_op jit(solution)/shard_map/all_to_all | solution.py:411
  45.0 4.5 %all-to-all-start.1 = ((bf16[8,7,128,128]{3,2,1,0:T(8,128)(2,1)}), bf16[8,7,128,128]{3,2,1,0:T(8,128)(2,1)}, u32[]{:S(2)}, u32[]{:S(2)}) async-start(bf16[8,7,128,128]{3,2,1,0:T(8,128)(2,1)} %get-tuple-element.27), calls=%async_computation.1 | async-start | bytes 3670016 | tf_op jit(solution)/shard_map/all_to_all | solution.py:411
  49.5 5.5 %collective-permute-start.1 = (bf16[8,2,128,128]{3,2,1,0:T(8,128)(2,1)S(1)}, bf16[8,2,128,128]{3,2,1,0:T(8,128)(2,1)S(1)}, u32[]{:S(2)}, u32[]{:S(2)}) collective-permute-start(bf16[8,2,128,128]{3,2,1,0:T(8,128)(2,1)S(1)} %copy-done.4), channel_id=1, source_target_pairs={{112,0},{0,16},{16,32},{32,48},{48,64},{64,80},{80,96},{96,112},{1... | collective-permute-start | bytes 1572872 | tf_op jit(solution)/shard_map/ppermute | solution.py:407
  56.0 1.3 collective-permute-start.3
  57.3 22.3 %collective-permute-done.1.refs_5_.refs_3_ = bf16[8,2,128,128]{3,2,1,0:T(8,128)(2,1)S(1)} collective-permute-done((bf16[8,2,128,128]{3,2,1,0:T(8,128)(2,1)S(1)}, bf16[8,2,128,128]{3,2,1,0:T(8,128)(2,1)S(1)}, u32[]{:S(2)}, u32[]{:S(2)}) %collective-permute-start.1) | collective-permute-done | bytes 524320 | tf_op jit(solution)/shard_map/ppermute | solution.py:407
  79.6 2.1 collective-permute-start.4
  81.7 1.6 collective-permute-done.refs_4_.refs_3_
  83.3 2.1 collective-permute-start.2
  86.6 3.8 %all-to-all-start.3 = ((bf16[8,6,128,128]{3,2,1,0:T(8,128)(2,1)}), bf16[8,6,128,128]{3,2,1,0:T(8,128)(2,1)S(1)}, u32[]{:S(2)}, u32[]{:S(2)}) async-start(bf16[8,6,128,128]{3,2,1,0:T(8,128)(2,1)} %get-tuple-element.29), calls=%async_computation.3 | async-start | bytes 3145728 | tf_op jit(solution)/shard_map/all_to_all | solution.py:411
  90.4 21.0 %attend.5 = (bf16[8,3,128,128]{3,2,1,0:T(8,128)(2,1)}, f32[2,2,128,512]{3,2,1,0:T(8,128)}, f32[2,2,128,512]{3,2,1,0:T(8,128)}, f32[2,2,128,512]{3,2,1,0:T(8,128)}, f32[2,2,128,512]{3,2,1,0:T(8,128)}) custom-call(s32[4]{0:T(128)} %compare_select_fusion.refs_0_, bf16[8,7,128,128]{3,2,1,0:T(8,128)(2,1)} %all-to-all-done.1.refs_1_.refs_2_, ...), custom_call_target="tpu_custom_call" | custom-call | flops 17112760320 | bytes 8388608 | tf_op jit(solution)/shard_map/attend/pallas_call | solution.py:299
  112.6 5.7 %all-to-all-start.2 = ((bf16[8,3,128,128]{3,2,1,0:T(8,128)(2,1)}), bf16[8,3,128,128]{3,2,1,0:T(8,128)(2,1)S(1)}, u32[]{:S(2)}, u32[]{:S(2)}) async-start(bf16[8,3,128,128]{3,2,1,0:T(8,128)(2,1)} %get-tuple-element.28), calls=%async_computation.2 | async-start | bytes 1572864 | tf_op jit(solution)/shard_map/all_to_all | solution.py:411
  118.2 21.9 %attend.6 = (bf16[8,3,128,128]{3,2,1,0:T(8,128)(2,1)}, f32[2,2,128,512]{3,2,1,0:T(8,128)}, f32[2,2,128,512]{3,2,1,0:T(8,128)}, f32[2,2,128,512]{3,2,1,0:T(8,128)}, f32[2,2,128,512]{3,2,1,0:T(8,128)}) custom-call(s32[4]{0:T(128)} %compare_select_fusion.refs_0_, bf16[8,6,128,128]{3,2,1,0:T(8,128)(2,1)} %copy-done.6, ...), custom_call_target="tpu_custom_call" | custom-call | flops 17112760320 | bytes 8388608 | tf_op jit(solution)/shard_map/attend/pallas_call | solution.py:299
  140.2 9.7 %attend.7 = (f32[2,2,128,512]{3,2,1,0:T(8,128)}, bf16[2,2,128,512]{3,2,1,0:T(8,128)(2,1)}, bf16[2,2,128,512]{3,2,1,0:T(8,128)(2,1)}) custom-call(s32[4]{0:T(128)} %compare_select_fusion.refs_0_, bf16[8,4,128,128]{3,2,1,0:T(8,128)(2,1)} %all_to_all.40.refs_1_, bf16[8,7,128,128]{3,2,1,0:T(8,128)(2,1)} %all-to-all-done.1.refs_1_.refs_2_, ...), custom_call_target="tpu_custom_call" | custom-call | flops 5368709120 | bytes 8388608 | tf_op jit(solution)/shard_map/attend/pallas_call | solution.py:299
  151.2 1.3 collective-permute-start.6
  152.5 5.7 %all-to-all-start.4 = ((bf16[8,3,128,128]{3,2,1,0:T(8,128)(2,1)}), bf16[8,3,128,128]{3,2,1,0:T(8,128)(2,1)S(1)}, u32[]{:S(2)}, u32[]{:S(2)}) async-start(bf16[8,3,128,128]{3,2,1,0:T(8,128)(2,1)} %get-tuple-element.34), calls=%async_computation.4 | async-start | bytes 1572864 | tf_op jit(solution)/shard_map/all_to_all | solution.py:411
  158.2 5.7 %collective-permute-start.10 = (bf16[2,2,128,512]{3,2,1,0:T(8,128)(2,1)}, bf16[2,2,128,512]{3,2,1,0:T(8,128)(2,1)S(1)}, u32[]{:S(2)}, u32[]{:S(2)}) collective-permute-start(bf16[2,2,128,512]{3,2,1,0:T(8,128)(2,1)} %get-tuple-element.44), channel_id=1, source_target_pairs={{0,104},{16,120},{32,8},{48,24},{64,40},{80,56},{96,72},{112,88},{... | collective-permute-start | bytes 1572872 | tf_op jit(solution)/shard_map/ppermute | solution.py:407
  164.0 6.3 %attend.8 = (f32[2,2,128,512]{3,2,1,0:T(8,128)}, bf16[2,2,128,512]{3,2,1,0:T(8,128)(2,1)}) custom-call(s32[4]{0:T(128)} %compare_select_fusion.refs_0_, bf16[8,4,128,128]{3,2,1,0:T(8,128)(2,1)} %all_to_all.40.refs_1_, bf16[8,7,128,128]{3,2,1,0:T(8,128)(2,1)} %all-to-all-done.1.refs_1_.refs_2_, bf16[8,2,128,128]{3,2,1,0:T(8,128)(2,1)} %copy-done.13, ...), custom_call_target="tpu_custom_call" | custom-call | flops 2684354560 | bytes 8388608 | tf_op jit(solution)/shard_map/attend/pallas_call | solution.py:299
  173.1 2.6 %join.1 = (bf16[2,2,128,512]{3,2,1,0:T(8,128)(2,1)}, bf16[2,2,128,512]{3,2,1,0:T(8,128)(2,1)}) custom-call(bf16[2,2,128,512]{3,2,1,0:T(8,128)(2,1)} %get-tuple-element.42.one_ref, bf16[2,2,128,512]{3,2,1,0:T(8,128)(2,1)} %get-tuple-element.43.two_ref, bf16[2,2,128,512]{3,2,1,0:T(8,128)(2,1)} %copy-done.10, bf16[2,2,128,512]{3,2,1,0:T(8,128)(2,1)} %copy-done.11), custom_call_target="tpu_custom_call" | custom-call | bytes 3145728 | tf_op jit(solution)/shard_map/join/pallas_call | solution.py:336
  175.8 6.7 %collective-permute-start.9 = (bf16[2,2,128,512]{3,2,1,0:T(8,128)(2,1)}, bf16[2,2,128,512]{3,2,1,0:T(8,128)(2,1)S(1)}, u32[]{:S(2)}, u32[]{:S(2)}) collective-permute-start(bf16[2,2,128,512]{3,2,1,0:T(8,128)(2,1)} %get-tuple-element.48), channel_id=1, source_target_pairs={{0,112},{16,0},{32,16},{48,32},{64,48},{80,64},{96,80},{112,96},{1... | collective-permute-start | bytes 1572872 | tf_op jit(solution)/shard_map/ppermute | solution.py:407
  182.5 2.3 %collective-permute-start.8 = (bf16[2,2,128,512]{3,2,1,0:T(8,128)(2,1)}, bf16[2,2,128,512]{3,2,1,0:T(8,128)(2,1)}, u32[]{:S(2)}, u32[]{:S(2)}) collective-permute-start(bf16[2,2,128,512]{3,2,1,0:T(8,128)(2,1)} %get-tuple-element.45.refs_7_), channel_id=1, source_target_pairs={{0,120},{16,8},{32,24},{48,40},{64,56},{80,72},{96,88},{112,104},{... | collective-permute-start | bytes 1572872 | tf_op jit(solution)/shard_map/ppermute | solution.py:407
  184.8 6.9 %attend.9 = (bf16[8,2,128,128]{3,2,1,0:T(8,128)(2,1)}, f32[2,2,128,512]{3,2,1,0:T(8,128)}) custom-call(s32[4]{0:T(128)} %compare_select_fusion.refs_0_, bf16[8,4,128,128]{3,2,1,0:T(8,128)(2,1)} %all_to_all.40.refs_1_, bf16[8,7,128,128]{3,2,1,0:T(8,128)(2,1)} %all-to-all-done.1.refs_1_.refs_2_, bf16[8,2,128,128]{3,2,1,0:T(8,128)(2,1)} %copy-done.3, ...), custom_call_target="tpu_custom_call" | custom-call | flops 3355443200 | bytes 8388608 | tf_op jit(solution)/shard_map/attend/pallas_call | solution.py:299
  191.7 4.8 %all-to-all-start.6 = ((bf16[8,2,128,128]{3,2,1,0:T(8,128)(2,1)}), bf16[8,2,128,128]{3,2,1,0:T(8,128)(2,1)S(1)}, u32[]{:S(2)}, u32[]{:S(2)}) async-start(bf16[8,2,128,128]{3,2,1,0:T(8,128)(2,1)} %get-tuple-element.46), calls=%async_computation.6 | async-start | bytes 1048576 | tf_op jit(solution)/shard_map/all_to_all | solution.py:411
  197.6 3.0 %total.1 = bf16[8,2,128,128]{3,2,1,0:T(8,128)(2,1)} custom-call(f32[2,2,128,512]{3,2,1,0:T(8,128)} %get-tuple-element.47.own_ref, bf16[2,2,128,512]{3,2,1,0:T(8,128)(2,1)} %copy-done.8, bf16[2,2,128,512]{3,2,1,0:T(8,128)(2,1)} %collective-permute-done.8.refs_1_, bf16[2,2,128,512]{3,2,1,0:T(8,128)(2,1)} %copy-done.9, bf16[2,2,128,512]{3,2,1,0:T(8,128)(2,1)} %copy-done.7), custom_call_target="tpu_custom_call" | custom-call | bytes 4194304 | tf_op jit(solution)/shard_map/total/pallas_call | solution.py:357
  200.7 4.5 %all-to-all-done.6.refs_2_ = bf16[8,2,128,128]{3,2,1,0:T(8,128)(2,1)S(1)} async-done(((bf16[8,2,128,128]{3,2,1,0:T(8,128)(2,1)}), bf16[8,2,128,128]{3,2,1,0:T(8,128)(2,1)S(1)}, u32[]{:S(2)}, u32[]{:S(2)}) %all-to-all-start.6) | async-done | bytes 524320 | tf_op jit(solution)/shard_map/all_to_all | solution.py:411
  205.2 3.5 %all-to-all-start.7 = ((bf16[8,2,128,128]{3,2,1,0:T(8,128)(2,1)}), bf16[8,2,128,128]{3,2,1,0:T(8,128)(2,1)S(1)}, u32[]{:S(2)}, u32[]{:S(2)}) async-start(bf16[8,2,128,128]{3,2,1,0:T(8,128)(2,1)} %total.1), calls=%async_computation.7 | async-start | bytes 1048576 | tf_op jit(solution)/shard_map/all_to_all | solution.py:411
  208.7 2.8 %unpack_q.1 = bf16[128,8192]{1,0:T(8,128)(2,1)} custom-call(bf16[8,3,128,128]{3,2,1,0:T(8,128)(2,1)} %copy-done, bf16[8,3,128,128]{3,2,1,0:T(8,128)(2,1)} %copy-done.1, bf16[8,2,128,128]{3,2,1,0:T(8,128)(2,1)} %copy-done.5), custom_call_target="tpu_custom_call" | custom-call | bytes 4194304 | tf_op jit(solution)/shard_map/unpack_q/pallas_call | solution.py:378
  211.5 6.5 %all-to-all-done.7.pair_ref = bf16[8,2,128,128]{3,2,1,0:T(8,128)(2,1)S(1)} async-done(((bf16[8,2,128,128]{3,2,1,0:T(8,128)(2,1)}), bf16[8,2,128,128]{3,2,1,0:T(8,128)(2,1)S(1)}, u32[]{:S(2)}, u32[]{:S(2)}) %all-to-all-start.7) | async-done | bytes 524320 | tf_op jit(solution)/shard_map/all_to_all | solution.py:411
  218.8 2.0 unpack_kv.1
  (57 shorter events, 12.4 us)
Async XLA Ops:
  0.6 7.8 %copy-start.12 = (f32[128,64]{0,1:T(8,128)S(1)}, f32[128,64]{0,1:T(8,128)}, u32[]{:S(2)}) copy-start(f32[128,64]{0,1:T(8,128)} %param.12) | copy-start | bytes 98308
  2.7 15.8 %all-to-all-start = ((bf16[8,2,128,128]{3,2,1,0:T(8,128)(2,1)}), bf16[8,2,128,128]{3,2,1,0:T(8,128)(2,1)S(1)}, u32[]{:S(2)}, u32[]{:S(2)}) async-start(bf16[8,2,128,128]{3,2,1,0:T(8,128)(2,1)} %pack_kv.1), calls=%async_computation | async-start | bytes 1048576 | tf_op jit(solution)/shard_map/all_to_all | solution.py:411
  45.0 4.5 %copy-start.4 = (bf16[8,2,128,128]{3,2,1,0:T(8,128)(2,1)S(1)}, bf16[8,2,128,128]{3,2,1,0:T(8,128)(2,1)}, u32[]{:S(2)}) copy-start(bf16[8,2,128,128]{3,2,1,0:T(8,128)(2,1)} %copy-done.3) | copy-start | bytes 1572868
  45.0 41.7 %all-to-all-start.1 = ((bf16[8,7,128,128]{3,2,1,0:T(8,128)(2,1)}), bf16[8,7,128,128]{3,2,1,0:T(8,128)(2,1)}, u32[]{:S(2)}, u32[]{:S(2)}) async-start(bf16[8,7,128,128]{3,2,1,0:T(8,128)(2,1)} %get-tuple-element.27), calls=%async_computation.1 | async-start | bytes 3670016 | tf_op jit(solution)/shard_map/all_to_all | solution.py:411
  49.5 30.2 %collective-permute-start.1 = (bf16[8,2,128,128]{3,2,1,0:T(8,128)(2,1)S(1)}, bf16[8,2,128,128]{3,2,1,0:T(8,128)(2,1)S(1)}, u32[]{:S(2)}, u32[]{:S(2)}) collective-permute-start(bf16[8,2,128,128]{3,2,1,0:T(8,128)(2,1)S(1)} %copy-done.4), channel_id=1, source_target_pairs={{112,0},{0,16},{16,32},{32,48},{48,64},{64,80},{80,96},{96,112},{1... | collective-permute-start | bytes 1572872 | tf_op jit(solution)/shard_map/ppermute | solution.py:407
  55.0 28.4 %collective-permute-start = (bf16[8,2,128,128]{3,2,1,0:T(8,128)(2,1)S(1)}, bf16[8,2,128,128]{3,2,1,0:T(8,128)(2,1)S(1)}, u32[]{:S(2)}, u32[]{:S(2)}) collective-permute-start(bf16[8,2,128,128]{3,2,1,0:T(8,128)(2,1)S(1)} %copy-done.4), channel_id=1, source_target_pairs={{0,8},{8,16},{16,24},{24,32},{32,40},{40,48},{48,56},{56,64},{64,7... | collective-permute-start | bytes 1572872 | tf_op jit(solution)/shard_map/ppermute | solution.py:407
  56.0 34.4 %collective-permute-start.3 = (bf16[8,2,128,128]{3,2,1,0:T(8,128)(2,1)S(1)}, bf16[8,2,128,128]{3,2,1,0:T(8,128)(2,1)}, u32[]{:S(2)}, u32[]{:S(2)}) collective-permute-start(bf16[8,2,128,128]{3,2,1,0:T(8,128)(2,1)S(1)} %copy-done.4), channel_id=1, source_target_pairs={{104,0},{120,16},{8,32},{24,48},{40,64},{56,80},{72,96},{88,112},{... | collective-permute-start | bytes 1572872 | tf_op jit(solution)/shard_map/ppermute | solution.py:407
  79.6 10.8 %copy-start.14 = (bf16[8,2,128,128]{3,2,1,0:T(8,128)(2,1)}, bf16[8,2,128,128]{3,2,1,0:T(8,128)(2,1)S(1)}, u32[]{:S(2)}) copy-start(bf16[8,2,128,128]{3,2,1,0:T(8,128)(2,1)S(1)} %collective-permute-done.1.refs_5_.refs_3_) | copy-start | bytes 1572868
  79.6 10.8 %collective-permute-start.4 = (bf16[8,2,128,128]{3,2,1,0:T(8,128)(2,1)S(1)}, bf16[8,2,128,128]{3,2,1,0:T(8,128)(2,1)}, u32[]{:S(2)}, u32[]{:S(2)}) collective-permute-start(bf16[8,2,128,128]{3,2,1,0:T(8,128)(2,1)S(1)} %collective-permute-done.1.refs_5_.refs_3_), channel_id=1, source_target_pairs={{0,8},{16,24},{32,40},{48,56},{64,72},{80,88},{96,104},{112,120},{... | collective-permute-start | bytes 1572872 | tf_op jit(solution)/shard_map/ppermute | solution.py:407
  83.3 7.1 %copy-start.13 = (bf16[8,2,128,128]{3,2,1,0:T(8,128)(2,1)}, bf16[8,2,128,128]{3,2,1,0:T(8,128)(2,1)S(1)}, u32[]{:S(2)}) copy-start(bf16[8,2,128,128]{3,2,1,0:T(8,128)(2,1)S(1)} %collective-permute-done.refs_4_.refs_3_) | copy-start | bytes 1572868
  83.3 7.1 %collective-permute-start.2 = (bf16[8,2,128,128]{3,2,1,0:T(8,128)(2,1)S(1)}, bf16[8,2,128,128]{3,2,1,0:T(8,128)(2,1)}, u32[]{:S(2)}, u32[]{:S(2)}) collective-permute-start(bf16[8,2,128,128]{3,2,1,0:T(8,128)(2,1)S(1)} %collective-permute-done.refs_4_.refs_3_), channel_id=1, source_target_pairs={{0,8},{16,24},{32,40},{48,56},{64,72},{80,88},{96,104},{112,120},{... | collective-permute-start | bytes 1572872 | tf_op jit(solution)/shard_map/ppermute | solution.py:407
  86.6 24.8 %all-to-all-start.3 = ((bf16[8,6,128,128]{3,2,1,0:T(8,128)(2,1)}), bf16[8,6,128,128]{3,2,1,0:T(8,128)(2,1)S(1)}, u32[]{:S(2)}, u32[]{:S(2)}) async-start(bf16[8,6,128,128]{3,2,1,0:T(8,128)(2,1)} %get-tuple-element.29), calls=%async_computation.3 | async-start | bytes 3145728 | tf_op jit(solution)/shard_map/all_to_all | solution.py:411
  111.4 1.1 copy-start.6
  112.6 39.9 %all-to-all-start.2 = ((bf16[8,3,128,128]{3,2,1,0:T(8,128)(2,1)}), bf16[8,3,128,128]{3,2,1,0:T(8,128)(2,1)S(1)}, u32[]{:S(2)}, u32[]{:S(2)}) async-start(bf16[8,3,128,128]{3,2,1,0:T(8,128)(2,1)} %get-tuple-element.28), calls=%async_computation.2 | async-start | bytes 1572864 | tf_op jit(solution)/shard_map/all_to_all | solution.py:411
  149.9 21.6 %collective-permute-start.5 = (bf16[2,2,128,512]{3,2,1,0:T(8,128)(2,1)}, bf16[2,2,128,512]{3,2,1,0:T(8,128)(2,1)S(1)}, u32[]{:S(2)}, u32[]{:S(2)}) collective-permute-start(bf16[2,2,128,512]{3,2,1,0:T(8,128)(2,1)} %get-tuple-element.43.two_ref), channel_id=1, source_target_pairs={{8,0},{24,16},{40,32},{56,48},{72,64},{88,80},{104,96},{120,112},{... | collective-permute-start | bytes 1572872 | tf_op jit(solution)/shard_map/ppermute | solution.py:407
  151.2 20.3 %collective-permute-start.6 = (bf16[2,2,128,512]{3,2,1,0:T(8,128)(2,1)}, bf16[2,2,128,512]{3,2,1,0:T(8,128)(2,1)S(1)}, u32[]{:S(2)}, u32[]{:S(2)}) collective-permute-start(bf16[2,2,128,512]{3,2,1,0:T(8,128)(2,1)} %get-tuple-element.44), channel_id=1, source_target_pairs={{8,0},{24,16},{40,32},{56,48},{72,64},{88,80},{104,96},{120,112},{... | collective-permute-start | bytes 1572872 | tf_op jit(solution)/shard_map/ppermute | solution.py:407
  152.5 11.4 %copy-start = (bf16[8,3,128,128]{3,2,1,0:T(8,128)(2,1)}, bf16[8,3,128,128]{3,2,1,0:T(8,128)(2,1)S(1)}, u32[]{:S(2)}) copy-start(bf16[8,3,128,128]{3,2,1,0:T(8,128)(2,1)S(1)} %all-to-all-done.2.refs_7_.refs_0_) | copy-start | bytes 2359300
  152.5 39.1 %all-to-all-start.4 = ((bf16[8,3,128,128]{3,2,1,0:T(8,128)(2,1)}), bf16[8,3,128,128]{3,2,1,0:T(8,128)(2,1)S(1)}, u32[]{:S(2)}, u32[]{:S(2)}) async-start(bf16[8,3,128,128]{3,2,1,0:T(8,128)(2,1)} %get-tuple-element.34), calls=%async_computation.4 | async-start | bytes 1572864 | tf_op jit(solution)/shard_map/all_to_all | solution.py:411
  158.2 38.2 %collective-permute-start.10 = (bf16[2,2,128,512]{3,2,1,0:T(8,128)(2,1)}, bf16[2,2,128,512]{3,2,1,0:T(8,128)(2,1)S(1)}, u32[]{:S(2)}, u32[]{:S(2)}) collective-permute-start(bf16[2,2,128,512]{3,2,1,0:T(8,128)(2,1)} %get-tuple-element.44), channel_id=1, source_target_pairs={{0,104},{16,120},{32,8},{48,24},{64,40},{80,56},{96,72},{112,88},{... | collective-permute-start | bytes 1572872 | tf_op jit(solution)/shard_map/ppermute | solution.py:407
  170.2 26.2 %collective-permute-start.7 = (bf16[2,2,128,512]{3,2,1,0:T(8,128)(2,1)}, bf16[2,2,128,512]{3,2,1,0:T(8,128)(2,1)S(1)}, u32[]{:S(2)}, u32[]{:S(2)}) collective-permute-start(bf16[2,2,128,512]{3,2,1,0:T(8,128)(2,1)} %get-tuple-element.42.one_ref), channel_id=1, source_target_pairs={{8,0},{24,16},{40,32},{56,48},{72,64},{88,80},{104,96},{120,112},{... | collective-permute-start | bytes 1572872 | tf_op jit(solution)/shard_map/ppermute | solution.py:407
  171.5 0.8 copy-start.10
  172.3 0.8 copy-start.11
  175.8 20.7 %collective-permute-start.9 = (bf16[2,2,128,512]{3,2,1,0:T(8,128)(2,1)}, bf16[2,2,128,512]{3,2,1,0:T(8,128)(2,1)S(1)}, u32[]{:S(2)}, u32[]{:S(2)}) collective-permute-start(bf16[2,2,128,512]{3,2,1,0:T(8,128)(2,1)} %get-tuple-element.48), channel_id=1, source_target_pairs={{0,112},{16,0},{32,16},{48,32},{64,48},{80,64},{96,80},{112,96},{1... | collective-permute-start | bytes 1572872 | tf_op jit(solution)/shard_map/ppermute | solution.py:407
  182.5 14.1 %collective-permute-start.8 = (bf16[2,2,128,512]{3,2,1,0:T(8,128)(2,1)}, bf16[2,2,128,512]{3,2,1,0:T(8,128)(2,1)}, u32[]{:S(2)}, u32[]{:S(2)}) collective-permute-start(bf16[2,2,128,512]{3,2,1,0:T(8,128)(2,1)} %get-tuple-element.45.refs_7_), channel_id=1, source_target_pairs={{0,120},{16,8},{32,24},{48,40},{64,56},{80,72},{96,88},{112,104},{... | collective-permute-start | bytes 1572872 | tf_op jit(solution)/shard_map/ppermute | solution.py:407
  191.7 9.0 %copy-start.1 = (bf16[8,3,128,128]{3,2,1,0:T(8,128)(2,1)}, bf16[8,3,128,128]{3,2,1,0:T(8,128)(2,1)S(1)}, u32[]{:S(2)}) copy-start(bf16[8,3,128,128]{3,2,1,0:T(8,128)(2,1)S(1)} %all-to-all-done.4.refs_1_) | copy-start | bytes 2359300
  191.7 13.5 %all-to-all-start.6 = ((bf16[8,2,128,128]{3,2,1,0:T(8,128)(2,1)}), bf16[8,2,128,128]{3,2,1,0:T(8,128)(2,1)S(1)}, u32[]{:S(2)}, u32[]{:S(2)}) async-start(bf16[8,2,128,128]{3,2,1,0:T(8,128)(2,1)} %get-tuple-element.46), calls=%async_computation.6 | async-start | bytes 1048576 | tf_op jit(solution)/shard_map/all_to_all | solution.py:411
  196.5 0.8 copy-start.7
  196.5 1.0 copy-start.8
  196.5 1.1 copy-start.9
  205.2 3.5 %copy-start.5 = (bf16[8,2,128,128]{3,2,1,0:T(8,128)(2,1)}, bf16[8,2,128,128]{3,2,1,0:T(8,128)(2,1)S(1)}, u32[]{:S(2)}) copy-start(bf16[8,2,128,128]{3,2,1,0:T(8,128)(2,1)S(1)} %all-to-all-done.6.refs_2_) | copy-start | bytes 1572868
  205.2 12.8 %all-to-all-start.7 = ((bf16[8,2,128,128]{3,2,1,0:T(8,128)(2,1)}), bf16[8,2,128,128]{3,2,1,0:T(8,128)(2,1)S(1)}, u32[]{:S(2)}, u32[]{:S(2)}) async-start(bf16[8,2,128,128]{3,2,1,0:T(8,128)(2,1)} %total.1), calls=%async_computation.7 | async-start | bytes 1048576 | tf_op jit(solution)/shard_map/all_to_all | solution.py:411
  218.0 0.8 copy-start.2
  (1 other events, 0.8 us)

commit v3 on v2

--- a/solution.py
+++ b/solution.py
@@ -14,7 +14,7 @@
 TOK = 128
 HEADS_DEV = 8
 HALF = 512
-CHUNKS = (3, 3, 2)
+CHUNKS = (4, 4)
 PARTS = 3
 FAR = 32768.0
 SCALE = HD ** (-0.5)
@@ -450,7 +450,10 @@
     kvs = [[kv], [one], [two, two_inner], [three, three_inner]]
 
     qds = pack_q(queries, grad_out, attn_out, log_norm, doc_block, kv)
-    qds = [exchange(qd) for qd in qds]
+    first, *_ = lax.optimization_barrier((qds[0], one, two, three))
+    first = exchange(first)
+    last, *_ = lax.optimization_barrier((qds[1], first, two_inner, three_inner))
+    qds = [first, exchange(last)]
     stats = qds[0]
     dkv = None
     dqs = []
@@ -468,8 +471,11 @@
     to_one, to_two = join(near[1], far[2], inner_two, inner_three)
     from_one, from_two = move(to_one, down[1]), move(to_two, down[2])
     dq, own = attend((0,), *args, dq, True, F32, (to_one,))
+    parts = (inner_one, from_one, from_two, from_three)
+    dq, *parts = lax.optimization_barrier((dq, *parts))
     dqs.append(exchange(dq))
-    pair = exchange(total(own[0], inner_one, from_one, from_two, from_three))
+    pair, *_ = lax.optimization_barrier((total(own[0], *parts), dqs[-1]))
+    pair = exchange(pair)
     grad_keys, grad_values = unpack_kv(pair)
     return unpack_q(dqs), grad_keys, grad_values
 

time: 222 us -> 213 us (0.959)
  starting transfers between devices: 63.2 us -> 56.2 us
  waiting for transfers between devices: 42.8 us -> 47.9 us
  blocking collectives: 20 us -> 15.8 us
  Pallas kernels: 83.9 us -> 80.2 us
    all_to_all x7 -> x5, waiting for transfers between devices: 18.9 us -> 36.7 us  [exchange(): return lax.all_to_all(value, 'uly', split_axis=0, concat_axis=0, tiled=True)]
    ppermute x11, waiting for transfers between devices: 23.9 us -> 11.2 us  [move(): return lax.ppermute(value, 'blk', pairs)]
    all_to_all x7 -> x5, starting transfers between devices: 33.6 us -> 22.2 us  [exchange(): return lax.all_to_all(value, 'uly', split_axis=0, concat_axis=0, tiled=True)]
    ppermute x11, starting transfers between devices: 29.6 us -> 34 us  [move(): return lax.ppermute(value, 'blk', pairs)]
    all_to_all x1, blocking collectives: 20 us -> 15.8 us  [exchange(): return lax.all_to_all(value, 'uly', split_axis=0, concat_axis=0, tiled=True)]
    pallas_call x5 -> x4, Pallas kernels: 65.8 us -> 62 us  [attend(): pl.pallas_call(kernel, grid=(1,), in_specs=[pl.BlockSpec(memory_space=plt...]
    unnamed x31 -> x33, local copies, waits for them, and re-layouts: 6.17 us -> 5.55 us
  transfers between devices with their start and end apart: 18 -> 16, of which waited for: 5 -> 6; matrix products, arithmetic and copies ran while one was open for 2% -> 2% of each run, Pallas kernels for 34% -> 36%
where the time goes in v3:
time: 213 us; the launch traced here: 210 us
  Pallas kernels  80.2 us (38%)
  starting transfers between devices  56.2 us (26%)
  waiting for transfers between devices  47.9 us (22%)
  blocking collectives  15.8 us (7%)
  local copies, waits for them, and re-layouts  7.21 us (3%)
    pallas_call x4, Pallas kernels, attend(): pl.pallas_call(kernel, grid=(1,), in_specs=[pl.BlockSpec(memory_space=plt...  62 us
    all_to_all x5, waiting for transfers between devices, exchange(): return lax.all_to_all(value, 'uly', split_axis=0, concat_axis=0, tiled=True)  36.7 us
    ppermute x11, starting transfers between devices, move(): return lax.ppermute(value, 'blk', pairs)  34 us
    all_to_all x5, starting transfers between devices, exchange(): return lax.all_to_all(value, 'uly', split_axis=0, concat_axis=0, tiled=True)  22.2 us
    all_to_all x1, blocking collectives, exchange(): return lax.all_to_all(value, 'uly', split_axis=0, concat_axis=0, tiled=True)  15.8 us
    ppermute x11, waiting for transfers between devices, move(): return lax.ppermute(value, 'blk', pairs)  11.2 us
    pallas_call x1, Pallas kernels, pack_q(): pl.pallas_call(functools.partial(pack_q_kernel, per), grid=(8 // per,), i...  5.7 us
    unnamed x33, local copies, waits for them, and re-layouts  5.55 us
  transfers between devices with their start and end apart: 16, of which 6 were waited for; matrix products, arithmetic and copies ran while one was open for 2% of the time, Pallas kernels for 36%

profile of v3, /device:TPU:0, one launch (start us, length us, event | category | flops | bytes accessed | tf_op | source)
XLA Modules:
  0.0 210.3 jit_solution(17509801851236903831)
XLA Ops:
  0.6 2.0 pack_kv.1
  2.7 15.8 %all_to_all.30._.refs_3_ = bf16[8,2,128,128]{3,2,1,0:T(8,128)(2,1)S(1)} all-to-all(bf16[8,2,128,128]{3,2,1,0:T(8,128)(2,1)} %pack_kv.1), channel_id=1, replica_groups=mesh['blk'=16,'uly'=8] {'uly'}, dimensions={0} | all-to-all | bytes 1048576 | tf_op jit(solution)/shard_map/all_to_all | solution.py:411
  18.5 1.3 collective-permute-start.2
  19.8 5.5 %collective-permute-start.1 = (bf16[8,2,128,128]{3,2,1,0:T(8,128)(2,1)S(1)}, bf16[8,2,128,128]{3,2,1,0:T(8,128)(2,1)S(1)}, u32[]{:S(2)}, u32[]{:S(2)}) collective-permute-start(bf16[8,2,128,128]{3,2,1,0:T(8,128)(2,1)S(1)} %all_to_all.30._.refs_3_), channel_id=1, source_target_pairs={{112,0},{0,16},{16,32},{32,48},{48,64},{64,80},{80,96},{96,112},{1... | collective-permute-start | bytes 1572872 | tf_op jit(solution)/shard_map/ppermute | solution.py:407
  27.6 5.7 %pack_q.1 = (bf16[8,9,128,128]{3,2,1,0:T(8,128)(2,1)}, bf16[8,8,128,128]{3,2,1,0:T(8,128)(2,1)}) custom-call(bf16[128,8192]{1,0:T(8,128)(2,1)} %q_ref.1, bf16[128,8192]{1,0:T(8,128)(2,1)} %do_ref.1, bf16[128,8192]{1,0:T(8,128)(2,1)} %o_ref.1, f32[128,64]{1,0:T(8,128)} %copy.10.ln_ref, bf16[128,128]{1,0:T(8,128)(2,1)} %select_convert_fusion.1.doc_ref, ...), custom_call_target="tpu_custom_call" | custom-call | bytes 11534336 | tf_op jit(solution)/shard_map/pack_q/pallas_call | solution.py:108
  33.3 7.3 %collective-permute-done.1.refs_5_.refs_3_ = bf16[8,2,128,128]{3,2,1,0:T(8,128)(2,1)S(1)} collective-permute-done((bf16[8,2,128,128]{3,2,1,0:T(8,128)(2,1)S(1)}, bf16[8,2,128,128]{3,2,1,0:T(8,128)(2,1)S(1)}, u32[]{:S(2)}, u32[]{:S(2)}) %collective-permute-start.1) | collective-permute-done | bytes 524320 | tf_op jit(solution)/shard_map/ppermute | solution.py:407
  40.5 3.9 %collective-permute-done.refs_4_.refs_3_ = bf16[8,2,128,128]{3,2,1,0:T(8,128)(2,1)S(1)} collective-permute-done((bf16[8,2,128,128]{3,2,1,0:T(8,128)(2,1)S(1)}, bf16[8,2,128,128]{3,2,1,0:T(8,128)(2,1)S(1)}, u32[]{:S(2)}, u32[]{:S(2)}) %collective-permute-start) | collective-permute-done | bytes 524320 | tf_op jit(solution)/shard_map/ppermute | solution.py:407
  44.4 3.6 %all-to-all-start.1 = ((bf16[8,9,128,128]{3,2,1,0:T(8,128)(2,1)}), bf16[8,9,128,128]{3,2,1,0:T(8,128)(2,1)S(1)}, u32[]{:S(2)}, u32[]{:S(2)}) async-start(bf16[8,9,128,128]{3,2,1,0:T(8,128)(2,1)} %get-tuple-element.30), calls=%async_computation.1 | async-start | bytes 4718592 | tf_op jit(solution)/shard_map/all_to_all | solution.py:411
  49.1 1.3 collective-permute-start.4
  50.4 2.1 collective-permute-start.3
  53.7 18.7 %all-to-all-done.1.refs_1_.refs_2_ = bf16[8,9,128,128]{3,2,1,0:T(8,128)(2,1)S(1)} async-done(((bf16[8,9,128,128]{3,2,1,0:T(8,128)(2,1)}), bf16[8,9,128,128]{3,2,1,0:T(8,128)(2,1)S(1)}, u32[]{:S(2)}, u32[]{:S(2)}) %all-to-all-start.1) | async-done | bytes 2359328 | tf_op jit(solution)/shard_map/all_to_all | solution.py:411
  72.4 1.4 copy-done.2
  73.8 4.5 %all-to-all-start.3 = ((bf16[8,8,128,128]{3,2,1,0:T(8,128)(2,1)}), bf16[8,8,128,128]{3,2,1,0:T(8,128)(2,1)}, u32[]{:S(2)}, u32[]{:S(2)}) async-start(bf16[8,8,128,128]{3,2,1,0:T(8,128)(2,1)} %get-tuple-element.33), calls=%async_computation.3 | async-start | bytes 4194304 | tf_op jit(solution)/shard_map/all_to_all | solution.py:411
  78.4 26.2 %attend.4 = (bf16[8,4,128,128]{3,2,1,0:T(8,128)(2,1)}, f32[2,2,128,512]{3,2,1,0:T(8,128)}, f32[2,2,128,512]{3,2,1,0:T(8,128)}, f32[2,2,128,512]{3,2,1,0:T(8,128)}, f32[2,2,128,512]{3,2,1,0:T(8,128)}) custom-call(s32[4]{0:T(128)} %compare_select_fusion.refs_0_, bf16[8,9,128,128]{3,2,1,0:T(8,128)(2,1)} %copy-done.2, bf16[8,9,128,128]{3,2,1,0:T(8,128)(2,1)} %copy-done.2, ...), custom_call_target="tpu_custom_call" | custom-call | flops 22817013760 | bytes 8388608 | tf_op jit(solution)/shard_map/attend/pallas_call | solution.py:299
  104.6 5.4 %all-to-all-start.2 = ((bf16[8,4,128,128]{3,2,1,0:T(8,128)(2,1)}), bf16[8,4,128,128]{3,2,1,0:T(8,128)(2,1)S(1)}, u32[]{:S(2)}, u32[]{:S(2)}) async-start(bf16[8,4,128,128]{3,2,1,0:T(8,128)(2,1)} %get-tuple-element.31), calls=%async_computation.2 | async-start | bytes 2097152 | tf_op jit(solution)/shard_map/all_to_all | solution.py:411
  110.0 15.2 %attend.5 = (f32[2,4,128,512]{3,2,1,0:T(8,128)}, bf16[2,2,128,512]{3,2,1,0:T(8,128)(2,1)}, bf16[2,2,128,512]{3,2,1,0:T(8,128)(2,1)}) custom-call(s32[4]{0:T(128)} %compare_select_fusion.refs_0_, bf16[8,8,128,128]{3,2,1,0:T(8,128)(2,1)} %all-to-all-done.3.refs_1_, bf16[8,9,128,128]{3,2,1,0:T(8,128)(2,1)} %copy-done.2, bf16[8,2,128,128]{3,2,1,0:T(8,128)(2,1)} %copy-done.14, ...), custom_call_target="tpu_custom_call" | custom-call | flops 10737418240 | bytes 8388608 | tf_op jit(solution)/shard_map/attend/pallas_call | solution.py:299
  125.2 1.3 collective-permute-start.5
  126.5 1.3 collective-permute-start.6
  127.8 4.8 %collective-permute-start.10 = (bf16[2,2,128,512]{3,2,1,0:T(8,128)(2,1)}, bf16[2,2,128,512]{3,2,1,0:T(8,128)(2,1)S(1)}, u32[]{:S(2)}, u32[]{:S(2)}) collective-permute-start(bf16[2,2,128,512]{3,2,1,0:T(8,128)(2,1)} %get-tuple-element.42), channel_id=1, source_target_pairs={{0,104},{16,120},{32,8},{48,24},{64,40},{80,56},{96,72},{112,88},{... | collective-permute-start | bytes 1572872 | tf_op jit(solution)/shard_map/ppermute | solution.py:407
  133.5 9.9 %attend.6 = (f32[2,4,128,512]{3,2,1,0:T(8,128)}, bf16[2,2,128,512]{3,2,1,0:T(8,128)(2,1)}) custom-call(s32[4]{0:T(128)} %compare_select_fusion.refs_0_, bf16[8,8,128,128]{3,2,1,0:T(8,128)(2,1)} %all-to-all-done.3.refs_1_, bf16[8,9,128,128]{3,2,1,0:T(8,128)(2,1)} %copy-done.2, bf16[8,2,128,128]{3,2,1,0:T(8,128)(2,1)} %copy-done.12, ...), custom_call_target="tpu_custom_call" | custom-call | flops 5368709120 | bytes 8388608 | tf_op jit(solution)/shard_map/attend/pallas_call | solution.py:299
  143.4 1.3 collective-permute-start.7
  146.3 2.7 %join.1 = (bf16[2,2,128,512]{3,2,1,0:T(8,128)(2,1)}, bf16[2,2,128,512]{3,2,1,0:T(8,128)(2,1)}) custom-call(bf16[2,2,128,512]{3,2,1,0:T(8,128)(2,1)} %get-tuple-element.40.one_ref, bf16[2,2,128,512]{3,2,1,0:T(8,128)(2,1)} %get-tuple-element.41.two_ref, bf16[2,2,128,512]{3,2,1,0:T(8,128)(2,1)} %copy-done.9, bf16[2,2,128,512]{3,2,1,0:T(8,128)(2,1)} %copy-done.10), custom_call_target="tpu_custom_call" | custom-call | bytes 3145728 | tf_op jit(solution)/shard_map/join/pallas_call | solution.py:336
  149.0 13.4 %collective-permute-start.9 = (bf16[2,2,128,512]{3,2,1,0:T(8,128)(2,1)}, bf16[2,2,128,512]{3,2,1,0:T(8,128)(2,1)S(1)}, u32[]{:S(2)}, u32[]{:S(2)}) collective-permute-start(bf16[2,2,128,512]{3,2,1,0:T(8,128)(2,1)} %get-tuple-element.45), channel_id=1, source_target_pairs={{0,112},{16,0},{32,16},{48,32},{64,48},{80,64},{96,80},{112,96},{1... | collective-permute-start | bytes 1572872 | tf_op jit(solution)/shard_map/ppermute | solution.py:407
  162.4 1.7 collective-permute-start.8
  164.1 10.8 %attend.7 = (bf16[8,4,128,128]{3,2,1,0:T(8,128)(2,1)}, f32[2,2,128,512]{3,2,1,0:T(8,128)}) custom-call(s32[4]{0:T(128)} %compare_select_fusion.refs_0_, bf16[8,8,128,128]{3,2,1,0:T(8,128)(2,1)} %all-to-all-done.3.refs_1_, bf16[8,9,128,128]{3,2,1,0:T(8,128)(2,1)} %copy-done.2, bf16[8,2,128,128]{3,2,1,0:T(8,128)(2,1)} %copy-done.4, ...), custom_call_target="tpu_custom_call" | custom-call | flops 6710886400 | bytes 8388608 | tf_op jit(solution)/shard_map/attend/pallas_call | solution.py:299
  175.0 5.1 %all-to-all-start.4 = ((bf16[8,4,128,128]{3,2,1,0:T(8,128)(2,1)}), bf16[8,4,128,128]{3,2,1,0:T(8,128)(2,1)S(1)}, u32[]{:S(2)}, u32[]{:S(2)}) async-start(bf16[8,4,128,128]{3,2,1,0:T(8,128)(2,1)} %get-tuple-element.46), calls=%async_computation.4 | async-start | bytes 2097152 | tf_op jit(solution)/shard_map/all_to_all | solution.py:411
  180.1 3.1 %total.1 = bf16[8,2,128,128]{3,2,1,0:T(8,128)(2,1)} custom-call(f32[2,2,128,512]{3,2,1,0:T(8,128)} %get-tuple-element.47.own_ref, bf16[2,2,128,512]{3,2,1,0:T(8,128)(2,1)} %copy-done.6, bf16[2,2,128,512]{3,2,1,0:T(8,128)(2,1)} %copy-done.8, bf16[2,2,128,512]{3,2,1,0:T(8,128)(2,1)} %copy-done.7, bf16[2,2,128,512]{3,2,1,0:T(8,128)(2,1)} %copy-done.5), custom_call_target="tpu_custom_call" | custom-call | bytes 4194304 | tf_op jit(solution)/shard_map/total/pallas_call | solution.py:357
  183.2 10.8 %all-to-all-done.4.refs_1_ = bf16[8,4,128,128]{3,2,1,0:T(8,128)(2,1)S(1)} async-done(((bf16[8,4,128,128]{3,2,1,0:T(8,128)(2,1)}), bf16[8,4,128,128]{3,2,1,0:T(8,128)(2,1)S(1)}, u32[]{:S(2)}, u32[]{:S(2)}) %all-to-all-start.4) | async-done | bytes 1048608 | tf_op jit(solution)/shard_map/all_to_all | solution.py:411
  194.0 3.5 %all-to-all-start.5 = ((bf16[8,2,128,128]{3,2,1,0:T(8,128)(2,1)}), bf16[8,2,128,128]{3,2,1,0:T(8,128)(2,1)S(1)}, u32[]{:S(2)}, u32[]{:S(2)}) async-start(bf16[8,2,128,128]{3,2,1,0:T(8,128)(2,1)} %total.1), calls=%async_computation.5 | async-start | bytes 1048576 | tf_op jit(solution)/shard_map/all_to_all | solution.py:411
  197.5 2.8 %unpack_q.1 = bf16[128,8192]{1,0:T(8,128)(2,1)} custom-call(bf16[8,4,128,128]{3,2,1,0:T(8,128)(2,1)} %copy-done, bf16[8,4,128,128]{3,2,1,0:T(8,128)(2,1)} %copy-done.1), custom_call_target="tpu_custom_call" | custom-call | bytes 4194304 | tf_op jit(solution)/shard_map/unpack_q/pallas_call | solution.py:378
  200.3 7.2 %all-to-all-done.5.pair_ref = bf16[8,2,128,128]{3,2,1,0:T(8,128)(2,1)S(1)} async-done(((bf16[8,2,128,128]{3,2,1,0:T(8,128)(2,1)}), bf16[8,2,128,128]{3,2,1,0:T(8,128)(2,1)S(1)}, u32[]{:S(2)}, u32[]{:S(2)}) %all-to-all-start.5) | async-done | bytes 524320 | tf_op jit(solution)/shard_map/all_to_all | solution.py:411
  208.3 2.0 unpack_kv.1
  (54 shorter events, 7.9 us)
Async XLA Ops:
  0.6 24.7 %copy-start.11 = (f32[128,64]{0,1:T(8,128)S(1)}, f32[128,64]{0,1:T(8,128)}, u32[]{:S(2)}) copy-start(f32[128,64]{0,1:T(8,128)} %param.12) | copy-start | bytes 98308
  18.5 9.1 %copy-start.4 = (bf16[8,2,128,128]{3,2,1,0:T(8,128)(2,1)}, bf16[8,2,128,128]{3,2,1,0:T(8,128)(2,1)S(1)}, u32[]{:S(2)}) copy-start(bf16[8,2,128,128]{3,2,1,0:T(8,128)(2,1)S(1)} %all_to_all.30._.refs_3_) | copy-start | bytes 1572868
  18.5 14.8 %collective-permute-start.2 = (bf16[8,2,128,128]{3,2,1,0:T(8,128)(2,1)S(1)}, bf16[8,2,128,128]{3,2,1,0:T(8,128)(2,1)S(1)}, u32[]{:S(2)}, u32[]{:S(2)}) collective-permute-start(bf16[8,2,128,128]{3,2,1,0:T(8,128)(2,1)S(1)} %all_to_all.30._.refs_3_), channel_id=1, source_target_pairs={{104,0},{120,16},{8,32},{24,48},{40,64},{56,80},{72,96},{88,112},{... | collective-permute-start | bytes 1572872 | tf_op jit(solution)/shard_map/ppermute | solution.py:407
  19.8 20.8 %collective-permute-start.1 = (bf16[8,2,128,128]{3,2,1,0:T(8,128)(2,1)S(1)}, bf16[8,2,128,128]{3,2,1,0:T(8,128)(2,1)S(1)}, u32[]{:S(2)}, u32[]{:S(2)}) collective-permute-start(bf16[8,2,128,128]{3,2,1,0:T(8,128)(2,1)S(1)} %all_to_all.30._.refs_3_), channel_id=1, source_target_pairs={{112,0},{0,16},{16,32},{32,48},{48,64},{64,80},{80,96},{96,112},{1... | collective-permute-start | bytes 1572872 | tf_op jit(solution)/shard_map/ppermute | solution.py:407
  25.3 19.2 %collective-permute-start = (bf16[8,2,128,128]{3,2,1,0:T(8,128)(2,1)S(1)}, bf16[8,2,128,128]{3,2,1,0:T(8,128)(2,1)S(1)}, u32[]{:S(2)}, u32[]{:S(2)}) collective-permute-start(bf16[8,2,128,128]{3,2,1,0:T(8,128)(2,1)S(1)} %all_to_all.30._.refs_3_), channel_id=1, source_target_pairs={{0,8},{8,16},{16,24},{24,32},{32,40},{40,48},{48,56},{56,64},{64,7... | collective-permute-start | bytes 1572872 | tf_op jit(solution)/shard_map/ppermute | solution.py:407
  33.3 11.2 %copy-start.13 = (bf16[8,2,128,128]{3,2,1,0:T(8,128)(2,1)}, bf16[8,2,128,128]{3,2,1,0:T(8,128)(2,1)S(1)}, u32[]{:S(2)}) copy-start(bf16[8,2,128,128]{3,2,1,0:T(8,128)(2,1)S(1)} %collective-permute-done.2.refs_7_.refs_5_) | copy-start | bytes 1572868
  40.5 3.9 %copy-start.14 = (bf16[8,2,128,128]{3,2,1,0:T(8,128)(2,1)}, bf16[8,2,128,128]{3,2,1,0:T(8,128)(2,1)S(1)}, u32[]{:S(2)}) copy-start(bf16[8,2,128,128]{3,2,1,0:T(8,128)(2,1)S(1)} %collective-permute-done.1.refs_5_.refs_3_) | copy-start | bytes 1572868
  44.4 6.0 %copy-start.12 = (bf16[8,2,128,128]{3,2,1,0:T(8,128)(2,1)}, bf16[8,2,128,128]{3,2,1,0:T(8,128)(2,1)S(1)}, u32[]{:S(2)}) copy-start(bf16[8,2,128,128]{3,2,1,0:T(8,128)(2,1)S(1)} %collective-permute-done.refs_4_.refs_3_) | copy-start | bytes 1572868
  44.4 28.0 %all-to-all-start.1 = ((bf16[8,9,128,128]{3,2,1,0:T(8,128)(2,1)}), bf16[8,9,128,128]{3,2,1,0:T(8,128)(2,1)S(1)}, u32[]{:S(2)}, u32[]{:S(2)}) async-start(bf16[8,9,128,128]{3,2,1,0:T(8,128)(2,1)} %get-tuple-element.30), calls=%async_computation.1 | async-start | bytes 4718592 | tf_op jit(solution)/shard_map/all_to_all | solution.py:411
  49.1 4.7 %collective-permute-start.4 = (bf16[8,2,128,128]{3,2,1,0:T(8,128)(2,1)}, bf16[8,2,128,128]{3,2,1,0:T(8,128)(2,1)S(1)}, u32[]{:S(2)}, u32[]{:S(2)}) collective-permute-start(bf16[8,2,128,128]{3,2,1,0:T(8,128)(2,1)} %copy-done.14), channel_id=1, source_target_pairs={{0,8},{16,24},{32,40},{48,56},{64,72},{80,88},{96,104},{112,120},{... | collective-permute-start | bytes 1572872 | tf_op jit(solution)/shard_map/ppermute | solution.py:407
  50.4 3.3 %collective-permute-start.3 = (bf16[8,2,128,128]{3,2,1,0:T(8,128)(2,1)S(1)}, bf16[8,2,128,128]{3,2,1,0:T(8,128)(2,1)}, u32[]{:S(2)}, u32[]{:S(2)}) collective-permute-start(bf16[8,2,128,128]{3,2,1,0:T(8,128)(2,1)S(1)} %collective-permute-done.refs_4_.refs_3_), channel_id=1, source_target_pairs={{0,8},{16,24},{32,40},{48,56},{64,72},{80,88},{96,104},{112,120},{... | collective-permute-start | bytes 1572872 | tf_op jit(solution)/shard_map/ppermute | solution.py:407
  53.7 18.7 %copy-start.15 = (bf16[8,2,128,128]{3,2,1,0:T(8,128)(2,1)}, bf16[8,2,128,128]{3,2,1,0:T(8,128)(2,1)S(1)}, u32[]{:S(2)}) copy-start(bf16[8,2,128,128]{3,2,1,0:T(8,128)(2,1)S(1)} %collective-permute-done.4.refs_8_.refs_6_) | copy-start | bytes 1572868
  72.4 1.4 copy-start.2
  73.8 30.7 %all-to-all-start.3 = ((bf16[8,8,128,128]{3,2,1,0:T(8,128)(2,1)}), bf16[8,8,128,128]{3,2,1,0:T(8,128)(2,1)}, u32[]{:S(2)}, u32[]{:S(2)}) async-start(bf16[8,8,128,128]{3,2,1,0:T(8,128)(2,1)} %get-tuple-element.33), calls=%async_computation.3 | async-start | bytes 4194304 | tf_op jit(solution)/shard_map/all_to_all | solution.py:411
  104.6 28.0 %all-to-all-start.2 = ((bf16[8,4,128,128]{3,2,1,0:T(8,128)(2,1)}), bf16[8,4,128,128]{3,2,1,0:T(8,128)(2,1)S(1)}, u32[]{:S(2)}, u32[]{:S(2)}) async-start(bf16[8,4,128,128]{3,2,1,0:T(8,128)(2,1)} %get-tuple-element.31), calls=%async_computation.2 | async-start | bytes 2097152 | tf_op jit(solution)/shard_map/all_to_all | solution.py:411
  125.2 19.5 %collective-permute-start.5 = (bf16[2,2,128,512]{3,2,1,0:T(8,128)(2,1)}, bf16[2,2,128,512]{3,2,1,0:T(8,128)(2,1)S(1)}, u32[]{:S(2)}, u32[]{:S(2)}) collective-permute-start(bf16[2,2,128,512]{3,2,1,0:T(8,128)(2,1)} %get-tuple-element.41.two_ref), channel_id=1, source_target_pairs={{8,0},{24,16},{40,32},{56,48},{72,64},{88,80},{104,96},{120,112},{... | collective-permute-start | bytes 1572872 | tf_op jit(solution)/shard_map/ppermute | solution.py:407
  126.5 18.2 %collective-permute-start.6 = (bf16[2,2,128,512]{3,2,1,0:T(8,128)(2,1)}, bf16[2,2,128,512]{3,2,1,0:T(8,128)(2,1)S(1)}, u32[]{:S(2)}, u32[]{:S(2)}) collective-permute-start(bf16[2,2,128,512]{3,2,1,0:T(8,128)(2,1)} %get-tuple-element.42), channel_id=1, source_target_pairs={{8,0},{24,16},{40,32},{56,48},{72,64},{88,80},{104,96},{120,112},{... | collective-permute-start | bytes 1572872 | tf_op jit(solution)/shard_map/ppermute | solution.py:407
  127.8 47.1 %collective-permute-start.10 = (bf16[2,2,128,512]{3,2,1,0:T(8,128)(2,1)}, bf16[2,2,128,512]{3,2,1,0:T(8,128)(2,1)S(1)}, u32[]{:S(2)}, u32[]{:S(2)}) collective-permute-start(bf16[2,2,128,512]{3,2,1,0:T(8,128)(2,1)} %get-tuple-element.42), channel_id=1, source_target_pairs={{0,104},{16,120},{32,8},{48,24},{64,40},{80,56},{96,72},{112,88},{... | collective-permute-start | bytes 1572872 | tf_op jit(solution)/shard_map/ppermute | solution.py:407
  132.5 1.0 copy-start
  143.4 31.5 %collective-permute-start.7 = (bf16[2,2,128,512]{3,2,1,0:T(8,128)(2,1)}, bf16[2,2,128,512]{3,2,1,0:T(8,128)(2,1)S(1)}, u32[]{:S(2)}, u32[]{:S(2)}) collective-permute-start(bf16[2,2,128,512]{3,2,1,0:T(8,128)(2,1)} %get-tuple-element.40.one_ref), channel_id=1, source_target_pairs={{8,0},{24,16},{40,32},{56,48},{72,64},{88,80},{104,96},{120,112},{... | collective-permute-start | bytes 1572872 | tf_op jit(solution)/shard_map/ppermute | solution.py:407
  144.7 0.8 copy-start.9
  145.5 0.8 copy-start.10
  149.0 25.9 %collective-permute-start.9 = (bf16[2,2,128,512]{3,2,1,0:T(8,128)(2,1)}, bf16[2,2,128,512]{3,2,1,0:T(8,128)(2,1)S(1)}, u32[]{:S(2)}, u32[]{:S(2)}) collective-permute-start(bf16[2,2,128,512]{3,2,1,0:T(8,128)(2,1)} %get-tuple-element.45), channel_id=1, source_target_pairs={{0,112},{16,0},{32,16},{48,32},{64,48},{80,64},{96,80},{112,96},{1... | collective-permute-start | bytes 1572872 | tf_op jit(solution)/shard_map/ppermute | solution.py:407
  162.4 12.6 %collective-permute-start.8 = (bf16[2,2,128,512]{3,2,1,0:T(8,128)(2,1)}, bf16[2,2,128,512]{3,2,1,0:T(8,128)(2,1)S(1)}, u32[]{:S(2)}, u32[]{:S(2)}) collective-permute-start(bf16[2,2,128,512]{3,2,1,0:T(8,128)(2,1)} %get-tuple-element.43.refs_7_), channel_id=1, source_target_pairs={{0,120},{16,8},{32,24},{48,40},{64,56},{80,72},{96,88},{112,104},{... | collective-permute-start | bytes 1572872 | tf_op jit(solution)/shard_map/ppermute | solution.py:407
  174.9 5.2 %copy-start.6 = (bf16[2,2,128,512]{3,2,1,0:T(8,128)(2,1)}, bf16[2,2,128,512]{3,2,1,0:T(8,128)(2,1)S(1)}, u32[]{:S(2)}) copy-start(bf16[2,2,128,512]{3,2,1,0:T(8,128)(2,1)S(1)} %collective-permute-done.7.refs_0_) | copy-start | bytes 1572868
  174.9 5.2 %copy-start.5 = (bf16[2,2,128,512]{3,2,1,0:T(8,128)(2,1)}, bf16[2,2,128,512]{3,2,1,0:T(8,128)(2,1)S(1)}, u32[]{:S(2)}) copy-start(bf16[2,2,128,512]{3,2,1,0:T(8,128)(2,1)S(1)} %collective-permute-done.10.refs_3_) | copy-start | bytes 1572868
  174.9 5.2 %copy-start.7 = (bf16[2,2,128,512]{3,2,1,0:T(8,128)(2,1)}, bf16[2,2,128,512]{3,2,1,0:T(8,128)(2,1)S(1)}, u32[]{:S(2)}) copy-start(bf16[2,2,128,512]{3,2,1,0:T(8,128)(2,1)S(1)} %collective-permute-done.9.refs_2_) | copy-start | bytes 1572868
  175.0 5.1 %copy-start.8 = (bf16[2,2,128,512]{3,2,1,0:T(8,128)(2,1)}, bf16[2,2,128,512]{3,2,1,0:T(8,128)(2,1)S(1)}, u32[]{:S(2)}) copy-start(bf16[2,2,128,512]{3,2,1,0:T(8,128)(2,1)S(1)} %collective-permute-done.8.refs_1_) | copy-start | bytes 1572868
  175.0 19.0 %all-to-all-start.4 = ((bf16[8,4,128,128]{3,2,1,0:T(8,128)(2,1)}), bf16[8,4,128,128]{3,2,1,0:T(8,128)(2,1)S(1)}, u32[]{:S(2)}, u32[]{:S(2)}) async-start(bf16[8,4,128,128]{3,2,1,0:T(8,128)(2,1)} %get-tuple-element.46), calls=%async_computation.4 | async-start | bytes 2097152 | tf_op jit(solution)/shard_map/all_to_all | solution.py:411
  194.0 3.5 %copy-start.1 = (bf16[8,4,128,128]{3,2,1,0:T(8,128)(2,1)}, bf16[8,4,128,128]{3,2,1,0:T(8,128)(2,1)S(1)}, u32[]{:S(2)}) copy-start(bf16[8,4,128,128]{3,2,1,0:T(8,128)(2,1)S(1)} %all-to-all-done.4.refs_1_) | copy-start | bytes 3145732
  194.0 13.5 %all-to-all-start.5 = ((bf16[8,2,128,128]{3,2,1,0:T(8,128)(2,1)}), bf16[8,2,128,128]{3,2,1,0:T(8,128)(2,1)S(1)}, u32[]{:S(2)}, u32[]{:S(2)}) async-start(bf16[8,2,128,128]{3,2,1,0:T(8,128)(2,1)} %total.1), calls=%async_computation.5 | async-start | bytes 1048576 | tf_op jit(solution)/shard_map/all_to_all | solution.py:411
  207.5 0.8 copy-start.3

commit v4 on v2

--- a/solution.py
+++ b/solution.py
@@ -59,7 +59,7 @@
     )(key_rows, value_rows)
 
 
-def pack_q_kernel(per, q_ref, do_ref, o_ref, ln_ref, doc_ref, _, *refs):
+def pack_q_kernel(per, q_ref, do_ref, o_ref, ln_ref, doc_ref, *refs):
     *qd_refs, pick_ref = refs
     step = pl.program_id(0)
     heads = ln_ref.shape[1]
@@ -101,7 +101,7 @@
                 ref[i, 2 * count] = stats
 
 
-def pack_q(queries, grad_out, attn_out, log_norm, doc_block, after):
+def pack_q(queries, grad_out, attn_out, log_norm, doc_block):
     per = PACK_PER
     wide = pl.BlockSpec((TOK, per * HEADS_DEV * HD), lambda u: (0, u))
     shapes = [(8, 2 * c + (i == 0), TOK, HD) for i, c in enumerate(CHUNKS)]
@@ -114,7 +114,6 @@
             wide,
             pl.BlockSpec(log_norm.shape, lambda u: (0, 0)),
             pl.BlockSpec(doc_block.shape, lambda u: (0, 0)),
-            pl.BlockSpec(memory_space=pl.ANY),
         ],
         out_specs=[pl.BlockSpec((per,) + s[1:], lambda u: (u, 0, 0, 0)) for s in shapes],
         out_shape=[jax.ShapeDtypeStruct(s, BF) for s in shapes],
@@ -122,10 +121,10 @@
         compiler_params=pltpu.CompilerParams(vmem_limit_bytes=VMEM_LIMIT),
         cost_estimate=pl.CostEstimate(flops=0, bytes_accessed=11 << 20, transcendentals=0),
         name="pack_q",
-    )(queries, grad_out, attn_out, log_norm, doc_block, after)
-
-
-def attend_kernel(steps, count, first_head, kv_counts, has_dkv, has_dq, afters, last_dq, last_dkv, *refs):
+    )(queries, grad_out, attn_out, log_norm, doc_block)
+
+
+def attend_kernel(count, first_head, kv_counts, has_dkv, has_dq, last, *refs):
     refs = list(refs)
 
     def take(n):
@@ -136,14 +135,12 @@
     second_ref, qd_ref, stat_ref = take(3)
     kv_refs = [take(n) for n in kv_counts]
     (kdoc_ref,) = take(1)
-    dkv_in = take(len(steps)) if has_dkv else None
+    (dkv_in,) = take(1) if has_dkv else (None,)
     (dq_in,) = take(1) if has_dq else (None,)
-    take(afters)
     (dq_ref,) = take(1)
-    dkv_refs = take(len(steps))
-    qt_ref, dot_ref, sel_ref, kv_ref, p_ref, ds_ref = take(6)
-    (dqt_ref,) = take(1) if last_dq else (dq_ref,)
-    sum_refs = take(len(steps)) if last_dkv else dkv_refs
+    dkv_refs = take(3 if last else 1)
+    qt_ref, dot_ref, sel_ref, kv_ref, p_ref, ds_ref, dqt_ref = take(7)
+    (sum_ref,) = take(1) if last else dkv_refs
 
     row = lax.broadcasted_iota(jnp.int32, (48, HALF), 0)
     for h in range(count):
@@ -159,15 +156,11 @@
                     for other in sources[1:]:
                         block = block + other[half * 4 + i, pair]
                     kv_ref[index, pair, half, :, cols] = block
-    if has_dq:
-        dqt_ref[...] = dq_in[...]
+    dqt_ref[...] = jnp.zeros_like(dqt_ref)
+    if has_dkv:
+        sum_ref[...] = dkv_in[...]
     else:
-        dqt_ref[...] = jnp.zeros_like(dqt_ref)
-    for index in range(len(steps)):
-        if has_dkv:
-            sum_refs[index][...] = dkv_in[index][...]
-        else:
-            sum_refs[index][...] = jnp.zeros_like(sum_refs[index])
+        sum_ref[...] = jnp.zeros_like(sum_ref)
 
     def turn_rows(half):
         for i in range(4):
@@ -186,7 +179,7 @@
             [
                 kv_ref[index, 0, khalf, :, kcols],
                 sel_ref[h, :, kcols],
-                kdoc_ref[steps[index], khalf, :, kcols],
+                kdoc_ref[index, khalf, :, kcols],
                 jnp.zeros((64, bn), BF),
             ],
             axis=0,
@@ -211,8 +204,8 @@
         for k0, kn, q0 in ((0, 256, 0), (256, 256, 256)) if diagonal else ((0, HALF, 0),):
             span = slice(q0, HALF)
             cols = slice(k0, k0 + kn)
-            sum_refs[index][1, khalf, :, cols] += dot(dot_ref[qhalf, h, :, span], p_ref[slot, span, cols])
-            sum_refs[index][0, khalf, :, cols] += dot(qt_ref[qhalf, h, :, span], ds_ref[slot, span, cols])
+            sum_ref[index, 1, khalf, :, cols] += dot(dot_ref[qhalf, h, :, span], p_ref[slot, span, cols])
+            sum_ref[index, 0, khalf, :, cols] += dot(qt_ref[qhalf, h, :, span], ds_ref[slot, span, cols])
         for q0, qn, kn in ((0, 256, 256), (256, 256, 512)) if diagonal else ((0, HALF, HALF),):
             span = slice(q0, q0 + qn)
             dqt_ref[qhalf, h, :, span] += dot(kv_ref[index, 0, khalf, :, :kn], ds_ref[slot, span, :kn], NT)
@@ -234,119 +227,110 @@
         if PIPE:
             grads(index, qhalf, khalf, count - 1, (count - 1) % 2, diagonal)
 
-    for index, step in enumerate(steps):
-        if step == 0:
-
-            def diagonal(half, carry, index=index):
-                if index == 0:
-                    turn_rows(half)
-                tile(index, half, half, True)
-                return carry
-
-            lax.fori_loop(0, 2, diagonal, 0)
-            tile(index, 1, 0, False)
-        else:
-
-            def both(turn, carry, index=index, step=step):
-                second = second_ref[step]
-                if index == 0:
-                    turn_rows(1 - turn)
-                tile(index, jnp.where(turn == 0, 1, second), jnp.where(turn == 0, 0, second), False)
-                return carry
-
-            lax.fori_loop(0, 2, both, 0)
-
-    if last_dq:
-        for half in range(2):
-            for h in range(count):
-                for i in range(4):
-                    piece = dqt_ref[half, h, :, i * TOK : (i + 1) * TOK]
-                    dq_ref[half * 4 + i, h] = (piece * SCALE).astype(BF).T
-    if last_dkv:
-        for total_ref, sum_ref in zip(dkv_refs, sum_refs):
-            total_ref[0] = (sum_ref[0] * SCALE).astype(total_ref.dtype)
-            total_ref[1] = sum_ref[1].astype(total_ref.dtype)
-
-
-def attend(steps, chunk, second, qd, stats, kvs, kdoc, dkv, dq, last_dq, dkv_type, afters=()):
+    def diagonal(half, carry):
+        turn_rows(half)
+        tile(0, half, half, True)
+        return carry
+
+    lax.fori_loop(0, 2, diagonal, 0)
+    tile(0, 1, 0, False)
+    for step in range(1, STEPS):
+
+        def both(turn, carry, step=step):
+            second = second_ref[step]
+            tile(step, jnp.where(turn == 0, 1, second), jnp.where(turn == 0, 0, second), False)
+            return carry
+
+        lax.fori_loop(0, 2, both, 0)
+
+    ahead = dq_ref.shape[1] - count
+    if has_dq:
+        dq_ref[:, :ahead] = dq_in[...]
+    for half in range(2):
+        for h in range(count):
+            for i in range(4):
+                piece = dqt_ref[half, h, :, i * TOK : (i + 1) * TOK]
+                dq_ref[half * 4 + i, ahead + h] = (piece * SCALE).astype(BF).T
+    if last:
+        own_ref, others_ref, three_ref = dkv_refs
+        for pair, scale in ((0, SCALE), (1, 1.0)):
+            own_ref[pair] = sum_ref[0, pair] * scale
+            for step in range(1, STEPS):
+                others_ref[step - 1, pair] = (sum_ref[step, pair] * scale).astype(BF)
+            three_ref[pair] = others_ref[STEPS - 2, pair]
+
+
+def attend(chunk, second, qd, stats, kvs, kdoc, dkv, dq, last):
     first_head, count = sum(CHUNKS[:chunk]), CHUNKS[chunk]
     operands = [second, qd, stats]
-    kvs = [kvs[step] for step in steps]
     for sources in kvs:
         operands += sources
     operands.append(kdoc)
-    operands += [] if dkv is None else [dkv[step] for step in steps]
+    operands += [] if dkv is None else [dkv]
     operands += [] if dq is None else [dq]
     vmem = pl.BlockSpec(memory_space=pltpu.VMEM)
     stat_index = stats.shape[1] - 1
     stat_spec = pl.BlockSpec((8, 1, TOK, HD), lambda i: (0, stat_index, 0, 0))
-    tiles = sum(2.5 if step == 0 else 2 for step in steps)
-    flops = int(tiles * 5 * 2 * HALF * HALF * HD * count)
-    partial_dq = (2, count, HD, HALF)
-    sums = (2, 2, HD, HALF)
+    flops = int(8.5 * 5 * 2 * HALF * HALF * HD * count)
+    out_heads = count + (0 if dq is None else dq.shape[1])
+    sums = (STEPS, 2, 2, HD, HALF)
+    shapes = [((8, out_heads, TOK, HD), BF)]
+    shapes += [(sums[1:], F32), ((3,) + sums[1:], BF), (sums[1:], BF)] if last else [(sums, F32)]
     kernel = functools.partial(
         attend_kernel,
-        steps,
         count,
         first_head,
         [len(sources) for sources in kvs],
         dkv is not None,
         dq is not None,
-        len(afters),
-        last_dq,
-        dkv_type is not None,
+        last,
     )
-    dq, *dkv = pl.pallas_call(
+    return pl.pallas_call(
         kernel,
         grid=(1,),
         in_specs=[pl.BlockSpec(memory_space=pltpu.SMEM), vmem, stat_spec]
-        + [vmem] * (len(operands) - 3)
-        + [pl.BlockSpec(memory_space=pl.ANY)] * len(afters),
-        out_specs=[vmem] * (1 + len(steps)),
-        out_shape=[
-            jax.ShapeDtypeStruct((8, count, TOK, HD) if last_dq else partial_dq, BF if last_dq else F32),
-        ]
-        + [jax.ShapeDtypeStruct(sums, dkv_type or F32)] * len(steps),
+        + [vmem] * (len(operands) - 3),
+        out_specs=[vmem] * len(shapes),
+        out_shape=[jax.ShapeDtypeStruct(*shape) for shape in shapes],
         scratch_shapes=[
             pltpu.VMEM((2, count, HD, HALF), BF),
             pltpu.VMEM((2, count, HD, HALF), BF),
             pltpu.VMEM((2 * count, 48, HALF), BF),
-            pltpu.VMEM((len(steps), 2, 2, HD, HALF), BF),
+            pltpu.VMEM(sums, BF),
             pltpu.VMEM((2, HALF, HALF), BF),
             pltpu.VMEM((2, HALF, HALF), BF),
+            pltpu.VMEM((2, count, HD, HALF), F32),
         ]
-        + ([pltpu.VMEM(partial_dq, F32)] if last_dq else [])
-        + ([pltpu.VMEM(sums, F32)] * len(steps) if dkv_type is not None else []),
+        + ([pltpu.VMEM(sums, F32)] if last else []),
         compiler_params=pltpu.CompilerParams(vmem_limit_bytes=VMEM_LIMIT),
         cost_estimate=pl.CostEstimate(
-            flops=2 * flops, bytes_accessed=8 << 20, transcendentals=int(tiles) * HALF * HALF * count
+            flops=2 * flops, bytes_accessed=8 << 20, transcendentals=8 * HALF * HALF * count
         ),
         name="attend",
-    )(*operands, *afters)
-    return dq, dict(zip(steps, dkv))
-
-
-def join_kernel(one_ref, two_ref, inner_two_ref, inner_three_ref, to_one_ref, to_two_ref):
-    to_one_ref[...] = (one_ref[...].astype(F32) + inner_two_ref[...].astype(F32)).astype(BF)
-    to_two_ref[...] = (two_ref[...].astype(F32) + inner_three_ref[...].astype(F32)).astype(BF)
-
-
-def join(*parts):
-    shape = jax.ShapeDtypeStruct((2, 2, HD, HALF), BF)
+    )(*operands)
+
+
+def join_kernel(mine_ref, theirs_ref, to_one_ref, to_two_ref):
+    for ref, step in ((to_one_ref, 0), (to_two_ref, 1)):
+        ref[...] = (mine_ref[step].astype(F32) + theirs_ref[step + 1].astype(F32)).astype(BF)
+
+
+def join(mine, theirs):
+    shape = jax.ShapeDtypeStruct(mine.shape[1:], BF)
     return pl.pallas_call(
         join_kernel,
         out_shape=[shape, shape],
         compiler_params=pltpu.CompilerParams(vmem_limit_bytes=VMEM_LIMIT),
         cost_estimate=pl.CostEstimate(flops=0, bytes_accessed=3 << 20, transcendentals=0),
         name="join",
-    )(*parts)
-
-
-def total_kernel(own_ref, *refs):
+    )(mine, theirs)
+
+
+def total_kernel(own_ref, theirs_ref, *refs):
     *part_refs, out_ref = refs
     for pair in range(2):
         for half in range(2):
-            total = own_ref[pair, half]
+            total = own_ref[pair, half] + theirs_ref[0, pair, half].astype(F32)
             for ref in part_refs:
                 total += ref[pair, half].astype(F32)
             for i in range(4):
@@ -449,28 +433,34 @@
     two_inner, three_inner = (move(part, inner_up) for part in (one, two))
     kvs = [[kv], [one], [two, two_inner], [three, three_inner]]
 
-    qds = pack_q(queries, grad_out, attn_out, log_norm, doc_block, kv)
-    qds = [exchange(qd) for qd in qds]
-    stats = qds[0]
-    dkv = None
+    packed = pack_q(queries, grad_out, attn_out, log_norm, doc_block)
+    last = len(CHUNKS) - 1
+    qds, dkv, dq = [exchange(packed[0])], None, None
     dqs = []
-    for chunk in range(len(CHUNKS) - 1):
-        dq, dkv = attend(
-            (0, 1, 2, 3), chunk, second, qds[chunk], stats, kvs, kdoc, dkv, None, True, None
+    for chunk in range(last + 1):
+        if chunk < last:
+            before = (two_inner, three_inner) if dq is None else (dq,)
+            ahead, *_ = lax.optimization_barrier((packed[chunk + 1], qds[chunk], *before))
+            qds.append(exchange(ahead))
+        ready = dq if chunk == last else None
+        dq, *dkvs = attend(
+            chunk, second, qds[chunk], qds[0], kvs, kdoc, dkv, ready, chunk == last
         )
-        dqs.append(exchange(dq))
-    args = (len(CHUNKS) - 1, second, qds[-1], stats, kvs, kdoc, dkv)
-    dq, far = attend((2, 3), *args, None, False, BF)
-    inner_two, inner_three = (move(far[step], inner_down) for step in (2, 3))
-    from_three = move(far[3], down[3])
-    dq, near = attend((1,), *args, dq, False, BF, dqs[:1])
-    inner_one = move(near[1], inner_down)
-    to_one, to_two = join(near[1], far[2], inner_two, inner_three)
+        dkv = dkvs[0]
+        if chunk != last - 1:
+            dqs.append(dq)
+    own, others, three = dkvs
+    early, *_ = lax.optimization_barrier((dqs[0], qds[last]))
+    dqs = [exchange(early), exchange(dqs[1])]
+    others, sent = lax.optimization_barrier((others, dqs[0]))
+    dqs = [sent, *dqs[1:]]
+    theirs = move(others, inner_down)
+    from_three = move(three, down[3])
+    to_one, to_two = join(others, theirs)
     from_one, from_two = move(to_one, down[1]), move(to_two, down[2])
-    dq, own = attend((0,), *args, dq, True, F32, (to_one,))
-    dqs.append(exchange(dq))
-    pair = exchange(total(own[0], inner_one, from_one, from_two, from_three))
-    grad_keys, grad_values = unpack_kv(pair)
+    pair = total(own, theirs, from_one, from_two, from_three)
+    pair, *_ = lax.optimization_barrier((pair, dqs[-1]))
+    grad_keys, grad_values = unpack_kv(exchange(pair))
     return unpack_q(dqs), grad_keys, grad_values
 
 

time: 222 us -> 200 us (0.901)
  blocking collectives: 20 us -> 0 us
  waiting for transfers between devices: 42.8 us -> 49.7 us
  starting transfers between devices: 63.2 us -> 58 us
  Pallas kernels: 83.9 us -> 81.3 us
    all_to_all x1 -> x0, blocking collectives: 20 us -> none  [exchange(): return lax.all_to_all(value, 'uly', split_axis=0, concat_axis=0, tiled=True)]
    ppermute x11 -> x9, waiting for transfers between devices: 23.9 us -> 41.4 us  [move(): return lax.ppermute(value, 'blk', pairs)]
    all_to_all x7, waiting for transfers between devices: 18.9 us -> 8.22 us  [exchange(): return lax.all_to_all(value, 'uly', split_axis=0, concat_axis=0, tiled=True)]
    ppermute x11 -> x9, starting transfers between devices: 29.6 us -> 24 us  [move(): return lax.ppermute(value, 'blk', pairs)]
    pallas_call x5 -> x3, Pallas kernels: 65.8 us -> 62.5 us  [attend(): pl.pallas_call(kernel, grid=(1,), in_specs=[pl.BlockSpec(memory_space=plt...]
    unnamed x31 -> x29, local copies, waits for them, and re-layouts: 6.17 us -> 5.25 us
  transfers between devices with their start and end apart: 18 -> 16, of which waited for: 5 -> 6; matrix products, arithmetic and copies ran while one was open for 2% -> 2% of each run, Pallas kernels for 34% -> 39%
where the time goes in v4:
time: 200 us; the launch traced here: 199 us
  Pallas kernels  81.3 us (41%)
  starting transfers between devices  58 us (29%)
  waiting for transfers between devices  49.7 us (25%)
  local copies, waits for them, and re-layouts  6.91 us (3%)
    pallas_call x3, Pallas kernels, attend(): pl.pallas_call(kernel, grid=(1,), in_specs=[pl.BlockSpec(memory_space=plt...  62.5 us
    ppermute x9, waiting for transfers between devices, move(): return lax.ppermute(value, 'blk', pairs)  41.4 us
    all_to_all x7, starting transfers between devices, exchange(): return lax.all_to_all(value, 'uly', split_axis=0, concat_axis=0, tiled=True)  33.9 us
    ppermute x9, starting transfers between devices, move(): return lax.ppermute(value, 'blk', pairs)  24 us
    all_to_all x7, waiting for transfers between devices, exchange(): return lax.all_to_all(value, 'uly', split_axis=0, concat_axis=0, tiled=True)  8.22 us
    pallas_call x1, Pallas kernels, pack_q(): pl.pallas_call(functools.partial(pack_q_kernel, per), grid=(8 // per,), i...  5.65 us
    unnamed x29, local copies, waits for them, and re-layouts  5.25 us
  transfers between devices with their start and end apart: 16, of which 6 were waited for; matrix products, arithmetic and copies ran while one was open for 2% of the time, Pallas kernels for 39%

profile of v4, /device:TPU:0, one launch (start us, length us, event | category | flops | bytes accessed | tf_op | source)
XLA Modules:
  0.0 198.7 jit_solution(13983079873561758863)
XLA Ops:
  0.6 2.0 %pack_kv.1 = bf16[8,2,128,128]{3,2,1,0:T(8,128)(2,1)} custom-call(bf16[128,1024]{1,0:T(8,128)(2,1)} %k_ref.1, bf16[128,1024]{1,0:T(8,128)(2,1)} %v_ref.1), custom_call_target="tpu_custom_call" | custom-call | bytes 1048576 | tf_op jit(solution)/shard_map/pack_kv/pallas_call | solution.py:53
  2.7 5.7 %all-to-all-start.1 = ((bf16[8,2,128,128]{3,2,1,0:T(8,128)(2,1)}), bf16[8,2,128,128]{3,2,1,0:T(8,128)(2,1)}, u32[]{:S(2)}, u32[]{:S(2)}) async-start(bf16[8,2,128,128]{3,2,1,0:T(8,128)(2,1)} %pack_kv.1), calls=%async_computation.1 | async-start | bytes 1048576 | tf_op jit(solution)/shard_map/all_to_all | solution.py:395
  10.6 5.6 %pack_q.1 = (bf16[8,7,128,128]{3,2,1,0:T(8,128)(2,1)}, bf16[8,6,128,128]{3,2,1,0:T(8,128)(2,1)}, bf16[8,4,128,128]{3,2,1,0:T(8,128)(2,1)}) custom-call(bf16[128,8192]{1,0:T(8,128)(2,1)} %q_ref.1, bf16[128,8192]{1,0:T(8,128)(2,1)} %do_ref.1, bf16[128,8192]{1,0:T(8,128)(2,1)} %o_ref.1, f32[128,64]{1,0:T(8,128)} %copy.10.ln_ref, ...), custom_call_target="tpu_custom_call" | custom-call | bytes 11534336 | tf_op jit(solution)/shard_map/pack_q/pallas_call | solution.py:108
  16.3 2.3 %all-to-all-done.1.refs_3_ = bf16[8,2,128,128]{3,2,1,0:T(8,128)(2,1)} async-done(((bf16[8,2,128,128]{3,2,1,0:T(8,128)(2,1)}), bf16[8,2,128,128]{3,2,1,0:T(8,128)(2,1)}, u32[]{:S(2)}, u32[]{:S(2)}) %all-to-all-start.1) | async-done | bytes 524320 | tf_op jit(solution)/shard_map/all_to_all | solution.py:395
  18.6 3.6 %all-to-all-start = ((bf16[8,7,128,128]{3,2,1,0:T(8,128)(2,1)}), bf16[8,7,128,128]{3,2,1,0:T(8,128)(2,1)S(1)}, u32[]{:S(2)}, u32[]{:S(2)}) async-start(bf16[8,7,128,128]{3,2,1,0:T(8,128)(2,1)} %get-tuple-element.26), calls=%async_computation | async-start | bytes 3670016 | tf_op jit(solution)/shard_map/all_to_all | solution.py:395
  22.2 5.5 %collective-permute-start.2 = (bf16[8,2,128,128]{3,2,1,0:T(8,128)(2,1)}, bf16[8,2,128,128]{3,2,1,0:T(8,128)(2,1)S(1)}, u32[]{:S(2)}, u32[]{:S(2)}) collective-permute-start(bf16[8,2,128,128]{3,2,1,0:T(8,128)(2,1)} %all-to-all-done.1.refs_3_), channel_id=1, source_target_pairs={{112,0},{0,16},{16,32},{32,48},{48,64},{64,80},{80,96},{96,112},{1... | collective-permute-start | bytes 1572872 | tf_op jit(solution)/shard_map/ppermute | solution.py:391
  27.9 0.9 fusion
  28.8 1.3 collective-permute-start.4
  30.1 23.9 %collective-permute-done.2.refs_5_ = bf16[8,2,128,128]{3,2,1,0:T(8,128)(2,1)S(1)} collective-permute-done((bf16[8,2,128,128]{3,2,1,0:T(8,128)(2,1)}, bf16[8,2,128,128]{3,2,1,0:T(8,128)(2,1)S(1)}, u32[]{:S(2)}, u32[]{:S(2)}) %collective-permute-start.2) | collective-permute-done | bytes 524320 | tf_op jit(solution)/shard_map/ppermute | solution.py:391
  54.0 1.3 collective-permute-start.3
  55.3 2.2 %collective-permute-done.refs_4_ = bf16[8,2,128,128]{3,2,1,0:T(8,128)(2,1)S(1)} collective-permute-done((bf16[8,2,128,128]{3,2,1,0:T(8,128)(2,1)}, bf16[8,2,128,128]{3,2,1,0:T(8,128)(2,1)S(1)}, u32[]{:S(2)}, u32[]{:S(2)}) %collective-permute-start) | collective-permute-done | bytes 524320 | tf_op jit(solution)/shard_map/ppermute | solution.py:391
  57.5 2.1 %collective-permute-start.1 = (bf16[8,2,128,128]{3,2,1,0:T(8,128)(2,1)S(1)}, bf16[8,2,128,128]{3,2,1,0:T(8,128)(2,1)}, u32[]{:S(2)}, u32[]{:S(2)}) collective-permute-start(bf16[8,2,128,128]{3,2,1,0:T(8,128)(2,1)S(1)} %collective-permute-done.refs_4_), channel_id=1, source_target_pairs={{0,8},{16,24},{32,40},{48,56},{64,72},{80,88},{96,104},{112,120},{... | collective-permute-start | bytes 1572872 | tf_op jit(solution)/shard_map/ppermute | solution.py:391
  61.7 3.8 %all-to-all-start.2 = ((bf16[8,6,128,128]{3,2,1,0:T(8,128)(2,1)}), bf16[8,6,128,128]{3,2,1,0:T(8,128)(2,1)S(1)}, u32[]{:S(2)}, u32[]{:S(2)}) async-start(bf16[8,6,128,128]{3,2,1,0:T(8,128)(2,1)} %get-tuple-element.27), calls=%async_computation.2 | async-start | bytes 3145728 | tf_op jit(solution)/shard_map/all_to_all | solution.py:395
  65.5 21.6 %attend.3 = (bf16[8,3,128,128]{3,2,1,0:T(8,128)(2,1)}, f32[4,2,2,128,512]{4,3,2,1,0:T(8,128)}) custom-call(s32[4]{0:T(128)} %compare_select_fusion.refs_0_, bf16[8,7,128,128]{3,2,1,0:T(8,128)(2,1)} %copy-done.4, bf16[8,7,128,128]{3,2,1,0:T(8,128)(2,1)} %copy-done.4, bf16[8,2,128,128]{3,2,1,0:T(8,128)(2,1)} %all-to-all-done.1.refs_3_, ...), custom_call_target="tpu_custom_call" | custom-call | flops 17112760320 | bytes 8388608 | tf_op jit(solution)/shard_map/attend/pallas_call | solution.py:288
  87.1 5.5 %all-to-all-start.3 = ((bf16[8,4,128,128]{3,2,1,0:T(8,128)(2,1)}), bf16[8,4,128,128]{3,2,1,0:T(8,128)(2,1)S(1)}, u32[]{:S(2)}, u32[]{:S(2)}) async-start(bf16[8,4,128,128]{3,2,1,0:T(8,128)(2,1)} %get-tuple-element.29), calls=%async_computation.3 | async-start | bytes 2097152 | tf_op jit(solution)/shard_map/all_to_all | solution.py:395
  92.6 22.8 %attend.4 = (bf16[8,3,128,128]{3,2,1,0:T(8,128)(2,1)}, f32[4,2,2,128,512]{4,3,2,1,0:T(8,128)}) custom-call(s32[4]{0:T(128)} %compare_select_fusion.refs_0_, bf16[8,6,128,128]{3,2,1,0:T(8,128)(2,1)} %copy-done.5, bf16[8,7,128,128]{3,2,1,0:T(8,128)(2,1)} %copy-done.4, bf16[8,2,128,128]{3,2,1,0:T(8,128)(2,1)} %all-to-all-done.1.refs_3_, ...), custom_call_target="tpu_custom_call" | custom-call | flops 17112760320 | bytes 8388608 | tf_op jit(solution)/shard_map/attend/pallas_call | solution.py:288
  115.5 5.7 %all-to-all-start.4 = ((bf16[8,3,128,128]{3,2,1,0:T(8,128)(2,1)}), bf16[8,3,128,128]{3,2,1,0:T(8,128)(2,1)S(1)}, u32[]{:S(2)}, u32[]{:S(2)}) async-start(bf16[8,3,128,128]{3,2,1,0:T(8,128)(2,1)} %get-tuple-element.34), calls=%async_computation.4 | async-start | bytes 1572864 | tf_op jit(solution)/shard_map/all_to_all | solution.py:395
  121.2 18.0 %attend.5 = (bf16[8,5,128,128]{3,2,1,0:T(8,128)(2,1)}, f32[2,2,128,512]{3,2,1,0:T(8,128)}, bf16[3,2,2,128,512]{4,3,2,1,0:T(8,128)(2,1)}, bf16[2,2,128,512]{3,2,1,0:T(8,128)(2,1)}) custom-call(s32[4]{0:T(128)} %compare_select_fusion.refs_0_, bf16[8,4,128,128]{3,2,1,0:T(8,128)(2,1)} %copy-done.6, bf16[8,7,128,128]{3,2,1,0:T(8,128)(2,1)} %copy-done.4, ...), custom_call_target="tpu_custom_call" | custom-call | flops 11408506880 | bytes 8388608 | tf_op jit(solution)/shard_map/attend/pallas_call | solution.py:288
  140.1 1.3 collective-permute-start.5
  141.4 5.7 %all-to-all-start.5 = ((bf16[8,5,128,128]{3,2,1,0:T(8,128)(2,1)}), bf16[8,5,128,128]{3,2,1,0:T(8,128)(2,1)S(1)}, u32[]{:S(2)}, u32[]{:S(2)}) async-start(bf16[8,5,128,128]{3,2,1,0:T(8,128)(2,1)} %get-tuple-element.36), calls=%async_computation.5 | async-start | bytes 2621440 | tf_op jit(solution)/shard_map/all_to_all | solution.py:395
  147.0 4.9 %collective-permute-start.8 = (bf16[2,2,128,512]{3,2,1,0:T(8,128)(2,1)}, bf16[2,2,128,512]{3,2,1,0:T(8,128)(2,1)S(1)}, u32[]{:S(2)}, u32[]{:S(2)}) collective-permute-start(bf16[2,2,128,512]{3,2,1,0:T(8,128)(2,1)} %get-tuple-element.41), channel_id=1, source_target_pairs={{0,104},{16,120},{32,8},{48,24},{64,40},{80,56},{96,72},{112,88},{... | collective-permute-start | bytes 1572872 | tf_op jit(solution)/shard_map/ppermute | solution.py:391
  151.9 1.1 copy-done
  153.1 3.0 %join.1 = (bf16[2,2,128,512]{3,2,1,0:T(8,128)(2,1)}, bf16[2,2,128,512]{3,2,1,0:T(8,128)(2,1)}) custom-call(bf16[3,2,2,128,512]{4,3,2,1,0:T(8,128)(2,1)} %get-tuple-element.38.mine_ref, bf16[3,2,2,128,512]{4,3,2,1,0:T(8,128)(2,1)} %copy-done), custom_call_target="tpu_custom_call" | custom-call | bytes 3145728 | tf_op jit(solution)/shard_map/join/pallas_call | solution.py:320
  156.1 5.0 %collective-permute-start.6 = (bf16[2,2,128,512]{3,2,1,0:T(8,128)(2,1)}, bf16[2,2,128,512]{3,2,1,0:T(8,128)(2,1)S(1)}, u32[]{:S(2)}, u32[]{:S(2)}) collective-permute-start(bf16[2,2,128,512]{3,2,1,0:T(8,128)(2,1)} %get-tuple-element.39), channel_id=1, source_target_pairs={{0,120},{16,8},{32,24},{48,40},{64,56},{80,72},{96,88},{112,104},{... | collective-permute-start | bytes 1572872 | tf_op jit(solution)/shard_map/ppermute | solution.py:391
  161.1 2.7 %collective-permute-start.7 = (bf16[2,2,128,512]{3,2,1,0:T(8,128)(2,1)}, bf16[2,2,128,512]{3,2,1,0:T(8,128)(2,1)S(1)}, u32[]{:S(2)}, u32[]{:S(2)}) collective-permute-start(bf16[2,2,128,512]{3,2,1,0:T(8,128)(2,1)} %get-tuple-element.40), channel_id=1, source_target_pairs={{0,112},{16,0},{32,16},{48,32},{64,48},{80,64},{96,80},{112,96},{1... | collective-permute-start | bytes 1572872 | tf_op jit(solution)/shard_map/ppermute | solution.py:391
  163.8 6.6 %collective-permute-done.6.refs_0_ = bf16[2,2,128,512]{3,2,1,0:T(8,128)(2,1)S(1)} collective-permute-done((bf16[2,2,128,512]{3,2,1,0:T(8,128)(2,1)}, bf16[2,2,128,512]{3,2,1,0:T(8,128)(2,1)S(1)}, u32[]{:S(2)}, u32[]{:S(2)}) %collective-permute-start.6) | collective-permute-done | bytes 524320 | tf_op jit(solution)/shard_map/ppermute | solution.py:391
  170.4 8.7 %collective-permute-done.7.refs_1_ = bf16[2,2,128,512]{3,2,1,0:T(8,128)(2,1)S(1)} collective-permute-done((bf16[2,2,128,512]{3,2,1,0:T(8,128)(2,1)}, bf16[2,2,128,512]{3,2,1,0:T(8,128)(2,1)S(1)}, u32[]{:S(2)}, u32[]{:S(2)}) %collective-permute-start.7) | collective-permute-done | bytes 524320 | tf_op jit(solution)/shard_map/ppermute | solution.py:391
  179.9 3.3 %total.1 = bf16[8,2,128,128]{3,2,1,0:T(8,128)(2,1)} custom-call(f32[2,2,128,512]{3,2,1,0:T(8,128)} %get-tuple-element.37.own_ref, bf16[3,2,2,128,512]{4,3,2,1,0:T(8,128)(2,1)} %copy-done, bf16[2,2,128,512]{3,2,1,0:T(8,128)(2,1)} %copy-done.8, bf16[2,2,128,512]{3,2,1,0:T(8,128)(2,1)} %copy-done.9, bf16[2,2,128,512]{3,2,1,0:T(8,128)(2,1)} %copy-done.7), custom_call_target="tpu_custom_call" | custom-call | bytes 4194304 | tf_op jit(solution)/shard_map/total/pallas_call | solution.py:341
  183.3 4.0 %all-to-all-start.6 = ((bf16[8,2,128,128]{3,2,1,0:T(8,128)(2,1)}), bf16[8,2,128,128]{3,2,1,0:T(8,128)(2,1)S(1)}, u32[]{:S(2)}, u32[]{:S(2)}) async-start(bf16[8,2,128,128]{3,2,1,0:T(8,128)(2,1)} %total.1), calls=%async_computation.6 | async-start | bytes 1048576 | tf_op jit(solution)/shard_map/all_to_all | solution.py:395
  187.2 2.8 %unpack_q.1 = bf16[128,8192]{1,0:T(8,128)(2,1)} custom-call(bf16[8,3,128,128]{3,2,1,0:T(8,128)(2,1)} %copy-done.2, bf16[8,5,128,128]{3,2,1,0:T(8,128)(2,1)} %copy-done.1), custom_call_target="tpu_custom_call" | custom-call | bytes 4194304 | tf_op jit(solution)/shard_map/unpack_q/pallas_call | solution.py:362
  190.1 5.9 %all-to-all-done.6.pair_ref = bf16[8,2,128,128]{3,2,1,0:T(8,128)(2,1)S(1)} async-done(((bf16[8,2,128,128]{3,2,1,0:T(8,128)(2,1)}), bf16[8,2,128,128]{3,2,1,0:T(8,128)(2,1)S(1)}, u32[]{:S(2)}, u32[]{:S(2)}) %all-to-all-start.6) | async-done | bytes 524320 | tf_op jit(solution)/shard_map/all_to_all | solution.py:395
  196.7 2.0 unpack_kv.1
  (48 shorter events, 6.9 us)
Async XLA Ops:
  0.6 7.8 %copy-start.10 = (f32[128,64]{0,1:T(8,128)S(1)}, f32[128,64]{0,1:T(8,128)}, u32[]{:S(2)}) copy-start(f32[128,64]{0,1:T(8,128)} %param.12) | copy-start | bytes 98308
  2.7 15.9 %all-to-all-start.1 = ((bf16[8,2,128,128]{3,2,1,0:T(8,128)(2,1)}), bf16[8,2,128,128]{3,2,1,0:T(8,128)(2,1)}, u32[]{:S(2)}, u32[]{:S(2)}) async-start(bf16[8,2,128,128]{3,2,1,0:T(8,128)(2,1)} %pack_kv.1), calls=%async_computation.1 | async-start | bytes 1048576 | tf_op jit(solution)/shard_map/all_to_all | solution.py:395
  18.6 43.0 %all-to-all-start = ((bf16[8,7,128,128]{3,2,1,0:T(8,128)(2,1)}), bf16[8,7,128,128]{3,2,1,0:T(8,128)(2,1)S(1)}, u32[]{:S(2)}, u32[]{:S(2)}) async-start(bf16[8,7,128,128]{3,2,1,0:T(8,128)(2,1)} %get-tuple-element.26), calls=%async_computation | async-start | bytes 3670016 | tf_op jit(solution)/shard_map/all_to_all | solution.py:395
  22.2 31.8 %collective-permute-start.2 = (bf16[8,2,128,128]{3,2,1,0:T(8,128)(2,1)}, bf16[8,2,128,128]{3,2,1,0:T(8,128)(2,1)S(1)}, u32[]{:S(2)}, u32[]{:S(2)}) collective-permute-start(bf16[8,2,128,128]{3,2,1,0:T(8,128)(2,1)} %all-to-all-done.1.refs_3_), channel_id=1, source_target_pairs={{112,0},{0,16},{16,32},{32,48},{48,64},{64,80},{80,96},{96,112},{1... | collective-permute-start | bytes 1572872 | tf_op jit(solution)/shard_map/ppermute | solution.py:391
  27.7 29.8 %collective-permute-start = (bf16[8,2,128,128]{3,2,1,0:T(8,128)(2,1)}, bf16[8,2,128,128]{3,2,1,0:T(8,128)(2,1)S(1)}, u32[]{:S(2)}, u32[]{:S(2)}) collective-permute-start(bf16[8,2,128,128]{3,2,1,0:T(8,128)(2,1)} %all-to-all-done.1.refs_3_), channel_id=1, source_target_pairs={{0,8},{8,16},{16,24},{24,32},{32,40},{40,48},{48,56},{56,64},{64,7... | collective-permute-start | bytes 1572872 | tf_op jit(solution)/shard_map/ppermute | solution.py:391
  28.8 36.7 %collective-permute-start.4 = (bf16[8,2,128,128]{3,2,1,0:T(8,128)(2,1)}, bf16[8,2,128,128]{3,2,1,0:T(8,128)(2,1)}, u32[]{:S(2)}, u32[]{:S(2)}) collective-permute-start(bf16[8,2,128,128]{3,2,1,0:T(8,128)(2,1)} %all-to-all-done.1.refs_3_), channel_id=1, source_target_pairs={{104,0},{120,16},{8,32},{24,48},{40,64},{56,80},{72,96},{88,112},{... | collective-permute-start | bytes 1572872 | tf_op jit(solution)/shard_map/ppermute | solution.py:391
  54.0 7.7 %copy-start.11 = (bf16[8,2,128,128]{3,2,1,0:T(8,128)(2,1)}, bf16[8,2,128,128]{3,2,1,0:T(8,128)(2,1)S(1)}, u32[]{:S(2)}) copy-start(bf16[8,2,128,128]{3,2,1,0:T(8,128)(2,1)S(1)} %collective-permute-done.2.refs_5_) | copy-start | bytes 1572868
  54.0 6.8 %collective-permute-start.3 = (bf16[8,2,128,128]{3,2,1,0:T(8,128)(2,1)S(1)}, bf16[8,2,128,128]{3,2,1,0:T(8,128)(2,1)S(1)}, u32[]{:S(2)}, u32[]{:S(2)}) collective-permute-start(bf16[8,2,128,128]{3,2,1,0:T(8,128)(2,1)S(1)} %collective-permute-done.2.refs_5_), channel_id=1, source_target_pairs={{0,8},{16,24},{32,40},{48,56},{64,72},{80,88},{96,104},{112,120},{... | collective-permute-start | bytes 1572872 | tf_op jit(solution)/shard_map/ppermute | solution.py:391
  57.5 4.2 %copy-start.12 = (bf16[8,2,128,128]{3,2,1,0:T(8,128)(2,1)}, bf16[8,2,128,128]{3,2,1,0:T(8,128)(2,1)S(1)}, u32[]{:S(2)}) copy-start(bf16[8,2,128,128]{3,2,1,0:T(8,128)(2,1)S(1)} %collective-permute-done.refs_4_) | copy-start | bytes 1572868
  57.5 4.1 %collective-permute-start.1 = (bf16[8,2,128,128]{3,2,1,0:T(8,128)(2,1)S(1)}, bf16[8,2,128,128]{3,2,1,0:T(8,128)(2,1)}, u32[]{:S(2)}, u32[]{:S(2)}) collective-permute-start(bf16[8,2,128,128]{3,2,1,0:T(8,128)(2,1)S(1)} %collective-permute-done.refs_4_), channel_id=1, source_target_pairs={{0,8},{16,24},{32,40},{48,56},{64,72},{80,88},{96,104},{112,120},{... | collective-permute-start | bytes 1572872 | tf_op jit(solution)/shard_map/ppermute | solution.py:391
  60.8 0.8 copy-start.13
  61.7 3.8 %copy-start.4 = (bf16[8,7,128,128]{3,2,1,0:T(8,128)(2,1)}, bf16[8,7,128,128]{3,2,1,0:T(8,128)(2,1)S(1)}, u32[]{:S(2)}) copy-start(bf16[8,7,128,128]{3,2,1,0:T(8,128)(2,1)S(1)} %all-to-all-done.refs_1_.refs_2_) | copy-start | bytes 5505028
  61.7 25.5 %all-to-all-start.2 = ((bf16[8,6,128,128]{3,2,1,0:T(8,128)(2,1)}), bf16[8,6,128,128]{3,2,1,0:T(8,128)(2,1)S(1)}, u32[]{:S(2)}, u32[]{:S(2)}) async-start(bf16[8,6,128,128]{3,2,1,0:T(8,128)(2,1)} %get-tuple-element.27), calls=%async_computation.2 | async-start | bytes 3145728 | tf_op jit(solution)/shard_map/all_to_all | solution.py:395
  87.1 5.5 %copy-start.5 = (bf16[8,6,128,128]{3,2,1,0:T(8,128)(2,1)}, bf16[8,6,128,128]{3,2,1,0:T(8,128)(2,1)S(1)}, u32[]{:S(2)}) copy-start(bf16[8,6,128,128]{3,2,1,0:T(8,128)(2,1)S(1)} %all-to-all-done.2.refs_1_) | copy-start | bytes 4718596
  87.1 28.3 %all-to-all-start.3 = ((bf16[8,4,128,128]{3,2,1,0:T(8,128)(2,1)}), bf16[8,4,128,128]{3,2,1,0:T(8,128)(2,1)S(1)}, u32[]{:S(2)}, u32[]{:S(2)}) async-start(bf16[8,4,128,128]{3,2,1,0:T(8,128)(2,1)} %get-tuple-element.29), calls=%async_computation.3 | async-start | bytes 2097152 | tf_op jit(solution)/shard_map/all_to_all | solution.py:395
  115.4 5.7 %copy-start.6 = (bf16[8,4,128,128]{3,2,1,0:T(8,128)(2,1)}, bf16[8,4,128,128]{3,2,1,0:T(8,128)(2,1)S(1)}, u32[]{:S(2)}) copy-start(bf16[8,4,128,128]{3,2,1,0:T(8,128)(2,1)S(1)} %all-to-all-done.3.refs_1_) | copy-start | bytes 3145732
  115.5 23.7 %all-to-all-start.4 = ((bf16[8,3,128,128]{3,2,1,0:T(8,128)(2,1)}), bf16[8,3,128,128]{3,2,1,0:T(8,128)(2,1)S(1)}, u32[]{:S(2)}, u32[]{:S(2)}) async-start(bf16[8,3,128,128]{3,2,1,0:T(8,128)(2,1)} %get-tuple-element.34), calls=%async_computation.4 | async-start | bytes 1572864 | tf_op jit(solution)/shard_map/all_to_all | solution.py:395
  139.2 0.9 copy-start.2
  140.1 11.8 %collective-permute-start.5 = (bf16[3,2,2,128,512]{4,3,2,1,0:T(8,128)(2,1)}, bf16[3,2,2,128,512]{4,3,2,1,0:T(8,128)(2,1)S(1)}, u32[]{:S(2)}, u32[]{:S(2)}) collective-permute-start(bf16[3,2,2,128,512]{4,3,2,1,0:T(8,128)(2,1)} %get-tuple-element.38.mine_ref), channel_id=1, source_target_pairs={{8,0},{24,16},{40,32},{56,48},{72,64},{88,80},{104,96},{120,112},{... | collective-permute-start | bytes 4718600 | tf_op jit(solution)/shard_map/ppermute | solution.py:391
  141.4 41.9 %all-to-all-start.5 = ((bf16[8,5,128,128]{3,2,1,0:T(8,128)(2,1)}), bf16[8,5,128,128]{3,2,1,0:T(8,128)(2,1)S(1)}, u32[]{:S(2)}, u32[]{:S(2)}) async-start(bf16[8,5,128,128]{3,2,1,0:T(8,128)(2,1)} %get-tuple-element.36), calls=%async_computation.5 | async-start | bytes 2621440 | tf_op jit(solution)/shard_map/all_to_all | solution.py:395
  147.0 16.7 %collective-permute-start.8 = (bf16[2,2,128,512]{3,2,1,0:T(8,128)(2,1)}, bf16[2,2,128,512]{3,2,1,0:T(8,128)(2,1)S(1)}, u32[]{:S(2)}, u32[]{:S(2)}) collective-permute-start(bf16[2,2,128,512]{3,2,1,0:T(8,128)(2,1)} %get-tuple-element.41), channel_id=1, source_target_pairs={{0,104},{16,120},{32,8},{48,24},{64,40},{80,56},{96,72},{112,88},{... | collective-permute-start | bytes 1572872 | tf_op jit(solution)/shard_map/ppermute | solution.py:391
  151.9 1.1 copy-start
  156.1 14.3 %collective-permute-start.6 = (bf16[2,2,128,512]{3,2,1,0:T(8,128)(2,1)}, bf16[2,2,128,512]{3,2,1,0:T(8,128)(2,1)S(1)}, u32[]{:S(2)}, u32[]{:S(2)}) collective-permute-start(bf16[2,2,128,512]{3,2,1,0:T(8,128)(2,1)} %get-tuple-element.39), channel_id=1, source_target_pairs={{0,120},{16,8},{32,24},{48,40},{64,56},{80,72},{96,88},{112,104},{... | collective-permute-start | bytes 1572872 | tf_op jit(solution)/shard_map/ppermute | solution.py:391
  161.1 18.0 %collective-permute-start.7 = (bf16[2,2,128,512]{3,2,1,0:T(8,128)(2,1)}, bf16[2,2,128,512]{3,2,1,0:T(8,128)(2,1)S(1)}, u32[]{:S(2)}, u32[]{:S(2)}) collective-permute-start(bf16[2,2,128,512]{3,2,1,0:T(8,128)(2,1)} %get-tuple-element.40), channel_id=1, source_target_pairs={{0,112},{16,0},{32,16},{48,32},{64,48},{80,64},{96,80},{112,96},{1... | collective-permute-start | bytes 1572872 | tf_op jit(solution)/shard_map/ppermute | solution.py:391
  163.8 15.3 %copy-start.7 = (bf16[2,2,128,512]{3,2,1,0:T(8,128)(2,1)}, bf16[2,2,128,512]{3,2,1,0:T(8,128)(2,1)S(1)}, u32[]{:S(2)}) copy-start(bf16[2,2,128,512]{3,2,1,0:T(8,128)(2,1)S(1)} %collective-permute-done.8.refs_2_) | copy-start | bytes 1572868
  170.4 8.7 %copy-start.8 = (bf16[2,2,128,512]{3,2,1,0:T(8,128)(2,1)}, bf16[2,2,128,512]{3,2,1,0:T(8,128)(2,1)S(1)}, u32[]{:S(2)}) copy-start(bf16[2,2,128,512]{3,2,1,0:T(8,128)(2,1)S(1)} %collective-permute-done.6.refs_0_) | copy-start | bytes 1572868
  179.1 0.8 copy-start.9
  183.3 4.0 %copy-start.1 = (bf16[8,5,128,128]{3,2,1,0:T(8,128)(2,1)}, bf16[8,5,128,128]{3,2,1,0:T(8,128)(2,1)S(1)}, u32[]{:S(2)}) copy-start(bf16[8,5,128,128]{3,2,1,0:T(8,128)(2,1)S(1)} %all-to-all-done.5.refs_1_) | copy-start | bytes 3932164
  183.3 12.7 %all-to-all-start.6 = ((bf16[8,2,128,128]{3,2,1,0:T(8,128)(2,1)}), bf16[8,2,128,128]{3,2,1,0:T(8,128)(2,1)S(1)}, u32[]{:S(2)}, u32[]{:S(2)}) async-start(bf16[8,2,128,128]{3,2,1,0:T(8,128)(2,1)} %total.1), calls=%async_computation.6 | async-start | bytes 1048576 | tf_op jit(solution)/shard_map/all_to_all | solution.py:395
  195.9 0.8 copy-start.3

commit v5 on v4

--- a/solution.py
+++ b/solution.py
@@ -14,7 +14,7 @@
 TOK = 128
 HEADS_DEV = 8
 HALF = 512
-CHUNKS = (3, 3, 2)
+CHUNKS = (4, 4)
 PARTS = 3
 FAR = 32768.0
 SCALE = HD ** (-0.5)
@@ -132,35 +132,98 @@
         del refs[:n]
         return head
 
-    second_ref, qd_ref, stat_ref = take(3)
-    kv_refs = [take(n) for n in kv_counts]
+    second_ref, qd_hbm, stat_hbm = take(3)
+    kv_hbm = [take(n) for n in kv_counts]
     (kdoc_ref,) = take(1)
     (dkv_in,) = take(1) if has_dkv else (None,)
     (dq_in,) = take(1) if has_dq else (None,)
     (dq_ref,) = take(1)
-    dkv_refs = take(3 if last else 1)
+    dkv_out = take(3 if last else 1)
     qt_ref, dot_ref, sel_ref, kv_ref, p_ref, ds_ref, dqt_ref = take(7)
-    (sum_ref,) = take(1) if last else dkv_refs
+    qd_ref, stat_ref, raw_ref, sum_ref, sems = take(5)
+    (others_ref,) = take(1) if last else (None,)
+    ahead = dq_ref.shape[1] - count
+
+    def qd_copy(half):
+        rows = pl.ds(half * 4, 4)
+        return pltpu.make_async_copy(
+            qd_hbm.at[rows, 0 : 2 * count], qd_ref.at[rows], sems.at[half]
+        )
+
+    stat_copy = pltpu.make_async_copy(
+        stat_hbm.at[:, stat_hbm.shape[1] - 1], stat_ref, sems.at[2]
+    )
+    loads = []
+    slot = 0
+    for step, sources in enumerate(kv_hbm):
+        loads.append([])
+        for source in sources:
+            loads[-1].append(pltpu.make_async_copy(source, raw_ref.at[slot], sems.at[3 + slot]))
+            slot += 1
+        if has_dkv:
+            loads[-1].append(
+                pltpu.make_async_copy(dkv_in.at[step], sum_ref.at[step], sems.at[9 + step])
+            )
+    stores = []
+    if last:
+        own_out, others_out, three_out = dkv_out
+        stores.append(pltpu.make_async_copy(sum_ref.at[0], own_out, sems.at[13]))
+        for step in range(1, STEPS):
+            stores.append(
+                pltpu.make_async_copy(
+                    others_ref.at[step - 1], others_out.at[step - 1], sems.at[13 + step]
+                )
+            )
+        three_store = pltpu.make_async_copy(others_ref.at[STEPS - 2], three_out, sems.at[17])
+    else:
+        for step in range(STEPS):
+            stores.append(
+                pltpu.make_async_copy(sum_ref.at[step], dkv_out[0].at[step], sems.at[13 + step])
+            )
+    if has_dq:
+        dq_copy = pltpu.make_async_copy(dq_in, dq_ref.at[:, 0:ahead], sems.at[18])
+
+    qd_copy(0).start()
+    stat_copy.start()
+    for copy in loads[0]:
+        copy.start()
+    qd_copy(1).start()
+    for step_loads in loads[1:]:
+        for copy in step_loads:
+            copy.start()
+    if has_dq:
+        dq_copy.start()
 
     row = lax.broadcasted_iota(jnp.int32, (48, HALF), 0)
     for h in range(count):
         mine = row % HEADS_DEV == first_head + h
         sel_ref[h] = jnp.where(mine & (row < 24), -1.0, 0.0).astype(BF)
         sel_ref[count + h] = jnp.where(mine & (row >= 24), -1.0, 0.0).astype(BF)
-    for half in range(2):
-        for i in range(4):
-            cols = slice(i * TOK, (i + 1) * TOK)
-            for index, sources in enumerate(kv_refs):
+    dqt_ref[...] = jnp.zeros_like(dqt_ref)
+    if not has_dkv:
+        sum_ref[...] = jnp.zeros_like(sum_ref)
+
+    def begin(step):
+        for copy in loads[step]:
+            copy.wait()
+        first = sum(kv_counts[:step])
+        for half in range(2):
+            for i in range(4):
                 for pair in range(2):
-                    block = sources[0][half * 4 + i, pair]
-                    for other in sources[1:]:
-                        block = block + other[half * 4 + i, pair]
-                    kv_ref[index, pair, half, :, cols] = block
-    dqt_ref[...] = jnp.zeros_like(dqt_ref)
-    if has_dkv:
-        sum_ref[...] = dkv_in[...]
-    else:
-        sum_ref[...] = jnp.zeros_like(sum_ref)
+                    block = raw_ref[first, half * 4 + i, pair]
+                    for other in range(first + 1, first + kv_counts[step]):
+                        block = block + raw_ref[other, half * 4 + i, pair]
+                    kv_ref[step, pair, half, :, i * TOK : (i + 1) * TOK] = block
+
+    def end(step):
+        if last and step == 0:
+            sum_ref[0, 0] = sum_ref[0, 0] * SCALE
+        elif last:
+            others_ref[step - 1, 0] = (sum_ref[step, 0] * SCALE).astype(BF)
+            others_ref[step - 1, 1] = sum_ref[step, 1].astype(BF)
+        stores[step].start()
+        if last and step == STEPS - 1:
+            three_store.start()
 
     def turn_rows(half):
         for i in range(4):
@@ -188,7 +251,7 @@
             [kv_ref[index, 1, khalf, :, kcols], sel_ref[count + h, :, kcols], jnp.zeros((80, bn), BF)],
             axis=0,
         )
-        stats = stat_ref[pl.ds(qhalf * 4 + q0 // TOK, bm // TOK), 0].reshape(bm, HD)
+        stats = stat_ref[pl.ds(qhalf * 4 + q0 // TOK, bm // TOK)].reshape(bm, HD)
         q_ext = jnp.concatenate([rows_of(qhalf, h, q0, bm), stats], axis=1)
         do_ext = jnp.concatenate([rows_of(qhalf, count + h, q0, bm), stats], axis=1)
         prob = jnp.exp2(dot(q_ext, k_ext) * EXP2_SCALE)
@@ -227,14 +290,20 @@
         if PIPE:
             grads(index, qhalf, khalf, count - 1, (count - 1) % 2, diagonal)
 
+    stat_copy.wait()
+    begin(0)
+
     def diagonal(half, carry):
+        qd_copy(half).wait()
         turn_rows(half)
         tile(0, half, half, True)
         return carry
 
     lax.fori_loop(0, 2, diagonal, 0)
     tile(0, 1, 0, False)
+    end(0)
     for step in range(1, STEPS):
+        begin(step)
 
         def both(turn, carry, step=step):
             second = second_ref[step]
@@ -242,22 +311,19 @@
             return carry
 
         lax.fori_loop(0, 2, both, 0)
-
-    ahead = dq_ref.shape[1] - count
-    if has_dq:
-        dq_ref[:, :ahead] = dq_in[...]
+        end(step)
+
     for half in range(2):
         for h in range(count):
             for i in range(4):
                 piece = dqt_ref[half, h, :, i * TOK : (i + 1) * TOK]
                 dq_ref[half * 4 + i, ahead + h] = (piece * SCALE).astype(BF).T
+    if has_dq:
+        dq_copy.wait()
+    for copy in stores:
+        copy.wait()
     if last:
-        own_ref, others_ref, three_ref = dkv_refs
-        for pair, scale in ((0, SCALE), (1, 1.0)):
-            own_ref[pair] = sum_ref[0, pair] * scale
-            for step in range(1, STEPS):
-                others_ref[step - 1, pair] = (sum_ref[step, pair] * scale).astype(BF)
-            three_ref[pair] = others_ref[STEPS - 2, pair]
+        three_store.wait()
 
 
 def attend(chunk, second, qd, stats, kvs, kdoc, dkv, dq, last):
@@ -269,8 +335,7 @@
     operands += [] if dkv is None else [dkv]
     operands += [] if dq is None else [dq]
     vmem = pl.BlockSpec(memory_space=pltpu.VMEM)
-    stat_index = stats.shape[1] - 1
-    stat_spec = pl.BlockSpec((8, 1, TOK, HD), lambda i: (0, stat_index, 0, 0))
+    anywhere = pl.BlockSpec(memory_space=pl.ANY)
     flops = int(8.5 * 5 * 2 * HALF * HALF * HD * count)
     out_heads = count + (0 if dq is None else dq.shape[1])
     sums = (STEPS, 2, 2, HD, HALF)
@@ -287,10 +352,13 @@
     )
     return pl.pallas_call(
         kernel,
-        grid=(1,),
-        in_specs=[pl.BlockSpec(memory_space=pltpu.SMEM), vmem, stat_spec]
-        + [vmem] * (len(operands) - 3),
-        out_specs=[vmem] * len(shapes),
+        in_specs=[
+            pl.BlockSpec(memory_space=pltpu.SMEM),
+            *[anywhere] * (2 + sum(len(sources) for sources in kvs)),
+            vmem,
+            *[anywhere] * ((dkv is not None) + (dq is not None)),
+        ],
+        out_specs=[vmem] + [anywhere] * (len(shapes) - 1),
         out_shape=[jax.ShapeDtypeStruct(*shape) for shape in shapes],
         scratch_shapes=[
             pltpu.VMEM((2, count, HD, HALF), BF),
@@ -300,8 +368,13 @@
             pltpu.VMEM((2, HALF, HALF), BF),
             pltpu.VMEM((2, HALF, HALF), BF),
             pltpu.VMEM((2, count, HD, HALF), F32),
+            pltpu.VMEM((8, 2 * count, TOK, HD), BF),
+            pltpu.VMEM((8, TOK, HD), BF),
+            pltpu.VMEM((sum(len(sources) for sources in kvs), 8, 2, HD, TOK), BF),
+            pltpu.VMEM(sums, F32),
+            pltpu.SemaphoreType.DMA((19,)),
         ]
-        + ([pltpu.VMEM(sums, F32)] if last else []),
+        + ([pltpu.VMEM((3,) + sums[1:], BF)] if last else []),
         compiler_params=pltpu.CompilerParams(vmem_limit_bytes=VMEM_LIMIT),
         cost_estimate=pl.CostEstimate(
             flops=2 * flops, bytes_accessed=8 << 20, transcendentals=8 * HALF * HALF * count
@@ -310,41 +383,55 @@
     )(*operands)
 
 
-def join_kernel(mine_ref, theirs_ref, to_one_ref, to_two_ref):
-    for ref, step in ((to_one_ref, 0), (to_two_ref, 1)):
-        ref[...] = (mine_ref[step].astype(F32) + theirs_ref[step + 1].astype(F32)).astype(BF)
+def join_kernel(mine_ref, inner_two_ref, inner_three_ref, to_one_ref, to_two_ref):
+    to_one_ref[...] = (mine_ref[0].astype(F32) + inner_two_ref[0].astype(F32)).astype(BF)
+    to_two_ref[...] = (mine_ref[1].astype(F32) + inner_three_ref[0].astype(F32)).astype(BF)
 
 
 def join(mine, theirs):
+    def block(steps, first):
+        return pl.BlockSpec((steps, 1, 2, HD, HALF), lambda pair: (first, pair, 0, 0, 0))
+
+    out = pl.BlockSpec((1, 2, HD, HALF), lambda pair: (pair, 0, 0, 0))
     shape = jax.ShapeDtypeStruct(mine.shape[1:], BF)
     return pl.pallas_call(
         join_kernel,
+        grid=(2,),
+        in_specs=[block(2, 0), block(1, 1), block(1, 2)],
+        out_specs=[out, out],
         out_shape=[shape, shape],
         compiler_params=pltpu.CompilerParams(vmem_limit_bytes=VMEM_LIMIT),
         cost_estimate=pl.CostEstimate(flops=0, bytes_accessed=3 << 20, transcendentals=0),
         name="join",
-    )(mine, theirs)
+    )(mine, theirs, theirs)
 
 
 def total_kernel(own_ref, theirs_ref, *refs):
     *part_refs, out_ref = refs
-    for pair in range(2):
-        for half in range(2):
-            total = own_ref[pair, half] + theirs_ref[0, pair, half].astype(F32)
-            for ref in part_refs:
-                total += ref[pair, half].astype(F32)
-            for i in range(4):
-                out_ref[half * 4 + i, pair] = total[:, i * TOK : (i + 1) * TOK].astype(BF).T
-
-
-def total(*parts):
+    for half in range(2):
+        total = own_ref[0, half] + theirs_ref[0, 0, half].astype(F32)
+        for ref in part_refs:
+            total += ref[0, half].astype(F32)
+        for i in range(4):
+            out_ref[half * 4 + i, 0] = total[:, i * TOK : (i + 1) * TOK].astype(BF).T
+
+
+def total(own, theirs, *parts):
+    part = pl.BlockSpec((1, 2, HD, HALF), lambda pair: (pair, 0, 0, 0))
     return pl.pallas_call(
         total_kernel,
+        grid=(2,),
+        in_specs=[
+            part,
+            pl.BlockSpec((1, 1, 2, HD, HALF), lambda pair: (0, pair, 0, 0, 0)),
+            *[part] * len(parts),
+        ],
+        out_specs=pl.BlockSpec((8, 1, TOK, HD), lambda pair: (0, pair, 0, 0)),
         out_shape=jax.ShapeDtypeStruct((8, 2, TOK, HD), BF),
         compiler_params=pltpu.CompilerParams(vmem_limit_bytes=VMEM_LIMIT),
         cost_estimate=pl.CostEstimate(flops=0, bytes_accessed=4 << 20, transcendentals=0),
         name="total",
-    )(*parts)
+    )(own, theirs, *parts)
 
 
 def unpack_q_kernel(per, *refs):
@@ -434,34 +521,21 @@
     kvs = [[kv], [one], [two, two_inner], [three, three_inner]]
 
     packed = pack_q(queries, grad_out, attn_out, log_norm, doc_block)
-    last = len(CHUNKS) - 1
-    qds, dkv, dq = [exchange(packed[0])], None, None
-    dqs = []
-    for chunk in range(last + 1):
-        if chunk < last:
-            before = (two_inner, three_inner) if dq is None else (dq,)
-            ahead, *_ = lax.optimization_barrier((packed[chunk + 1], qds[chunk], *before))
-            qds.append(exchange(ahead))
-        ready = dq if chunk == last else None
-        dq, *dkvs = attend(
-            chunk, second, qds[chunk], qds[0], kvs, kdoc, dkv, ready, chunk == last
-        )
-        dkv = dkvs[0]
-        if chunk != last - 1:
-            dqs.append(dq)
-    own, others, three = dkvs
-    early, *_ = lax.optimization_barrier((dqs[0], qds[last]))
-    dqs = [exchange(early), exchange(dqs[1])]
-    others, sent = lax.optimization_barrier((others, dqs[0]))
-    dqs = [sent, *dqs[1:]]
+    early = exchange(packed[0])
+    late, *_ = lax.optimization_barrier((packed[1], early, two_inner, three_inner))
+    late = exchange(late)
+    dq, dkv = attend(0, second, early, early, kvs, kdoc, None, None, False)
+    dq, own, others, three = attend(1, second, late, early, kvs, kdoc, dkv, dq, True)
+
     theirs = move(others, inner_down)
+    dq = exchange(dq)
     from_three = move(three, down[3])
     to_one, to_two = join(others, theirs)
     from_one, from_two = move(to_one, down[1]), move(to_two, down[2])
     pair = total(own, theirs, from_one, from_two, from_three)
-    pair, *_ = lax.optimization_barrier((pair, dqs[-1]))
+    pair, *_ = lax.optimization_barrier((pair, dq))
     grad_keys, grad_values = unpack_kv(exchange(pair))
-    return unpack_q(dqs), grad_keys, grad_values
+    return unpack_q([dq]), grad_keys, grad_values
 
 
 def solution(mesh):

time: 200 us -> 193 us (0.965)
  waiting for transfers between devices: 49.7 us -> 61.9 us
  Pallas kernels: 81.3 us -> 70.9 us
  starting transfers between devices: 58 us -> 48.7 us
    ppermute x9, waiting for transfers between devices: 41.4 us -> 53.1 us  [move(): return lax.ppermute(value, 'blk', pairs)]
    pallas_call x5 -> x4, Pallas kernels: 68.8 us -> 58.4 us  [the longest x2 53.3 us: attend(): pl.pallas_call(kernel, in_specs=[pl.BlockSpec(memory_space=pltpu.SMEM), *...]
    all_to_all x7 -> x5, starting transfers between devices: 33.9 us -> 23.7 us  [exchange(): return lax.all_to_all(value, 'uly', split_axis=0, concat_axis=0, tiled=True)]
    all_to_all x7 -> x5, waiting for transfers between devices: 8.22 us -> 8.72 us  [exchange(): return lax.all_to_all(value, 'uly', split_axis=0, concat_axis=0, tiled=True)]
    unnamed x29 -> x23, local copies, waits for them, and re-layouts: 5.25 us -> 5.68 us
  transfers between devices with their start and end apart: 16 -> 14, of which waited for: 6 -> 6; matrix products, arithmetic and copies ran while one was open for 2% -> 2% of each run, Pallas kernels for 39% -> 21%
where the time goes in v5:
time: 193 us; the launch traced here: 192 us
  Pallas kernels  70.9 us (37%)
  waiting for transfers between devices  61.9 us (32%)
  starting transfers between devices  48.7 us (25%)
  local copies, waits for them, and re-layouts  7.34 us (4%)
  other arithmetic  1.93 us (1%)
    pallas_call x2, Pallas kernels, attend(): pl.pallas_call(kernel, in_specs=[pl.BlockSpec(memory_space=pltpu.SMEM), *...  53.3 us
    ppermute x9, waiting for transfers between devices, move(): return lax.ppermute(value, 'blk', pairs)  53.1 us
    ppermute x9, starting transfers between devices, move(): return lax.ppermute(value, 'blk', pairs)  25.1 us
    all_to_all x5, starting transfers between devices, exchange(): return lax.all_to_all(value, 'uly', split_axis=0, concat_axis=0, tiled=True)  23.7 us
    all_to_all x5, waiting for transfers between devices, exchange(): return lax.all_to_all(value, 'uly', split_axis=0, concat_axis=0, tiled=True)  8.72 us
    pallas_call x1, Pallas kernels, pack_q(): pl.pallas_call(functools.partial(pack_q_kernel, per), grid=(8 // per,), i...  5.7 us
    unnamed x23, local copies, waits for them, and re-layouts  5.68 us
  transfers between devices with their start and end apart: 14, of which 6 were waited for; matrix products, arithmetic and copies ran while one was open for 2% of the time, Pallas kernels for 21%

profile of v5, /device:TPU:0, one launch (start us, length us, event | category | flops | bytes accessed | tf_op | source)
XLA Modules:
  0.0 191.7 jit_solution(5065728268981577187)
XLA Ops:
  0.6 2.0 %pack_kv.1 = bf16[8,2,128,128]{3,2,1,0:T(8,128)(2,1)} custom-call(bf16[128,1024]{1,0:T(8,128)(2,1)} %k_ref.1, bf16[128,1024]{1,0:T(8,128)(2,1)} %v_ref.1), custom_call_target="tpu_custom_call" | custom-call | bytes 1048576 | tf_op jit(solution)/shard_map/pack_kv/pallas_call | solution.py:53
  2.7 5.7 %all-to-all-start.1 = ((bf16[8,2,128,128]{3,2,1,0:T(8,128)(2,1)}), bf16[8,2,128,128]{3,2,1,0:T(8,128)(2,1)S(1)}, u32[]{:S(2)}, u32[]{:S(2)}) async-start(bf16[8,2,128,128]{3,2,1,0:T(8,128)(2,1)} %pack_kv.1), calls=%async_computation.1 | async-start | bytes 1048576 | tf_op jit(solution)/shard_map/all_to_all | solution.py:482
  10.6 5.7 %pack_q.1 = (bf16[8,9,128,128]{3,2,1,0:T(8,128)(2,1)}, bf16[8,8,128,128]{3,2,1,0:T(8,128)(2,1)}) custom-call(bf16[128,8192]{1,0:T(8,128)(2,1)} %q_ref.1, bf16[128,8192]{1,0:T(8,128)(2,1)} %do_ref.1, bf16[128,8192]{1,0:T(8,128)(2,1)} %o_ref.1, f32[128,64]{1,0:T(8,128)} %copy.10.ln_ref, bf16[128,128]{1,0:T(8,128)(2,1)} %select_convert_fusion.1.doc_ref), custom_call_target="tpu_custom_call" | custom-call | bytes 11534336 | tf_op jit(solution)/shard_map/pack_q/pallas_call | solution.py:108
  16.3 2.2 %all-to-all-done.1.refs_3_ = bf16[8,2,128,128]{3,2,1,0:T(8,128)(2,1)S(1)} async-done(((bf16[8,2,128,128]{3,2,1,0:T(8,128)(2,1)}), bf16[8,2,128,128]{3,2,1,0:T(8,128)(2,1)S(1)}, u32[]{:S(2)}, u32[]{:S(2)}) %all-to-all-start.1) | async-done | bytes 524320 | tf_op jit(solution)/shard_map/all_to_all | solution.py:482
  18.5 3.6 %all-to-all-start = ((bf16[8,9,128,128]{3,2,1,0:T(8,128)(2,1)}), bf16[8,9,128,128]{3,2,1,0:T(8,128)(2,1)S(1)}, u32[]{:S(2)}, u32[]{:S(2)}) async-start(bf16[8,9,128,128]{3,2,1,0:T(8,128)(2,1)} %get-tuple-element.18), calls=%async_computation | async-start | bytes 4718592 | tf_op jit(solution)/shard_map/all_to_all | solution.py:482
  22.1 5.5 %collective-permute-start.2 = (bf16[8,2,128,128]{3,2,1,0:T(8,128)(2,1)S(1)}, bf16[8,2,128,128]{3,2,1,0:T(8,128)(2,1)S(1)}, u32[]{:S(2)}, u32[]{:S(2)}) collective-permute-start(bf16[8,2,128,128]{3,2,1,0:T(8,128)(2,1)S(1)} %all-to-all-done.1.refs_3_), channel_id=1, source_target_pairs={{112,0},{0,16},{16,32},{32,48},{48,64},{64,80},{80,96},{96,112},{1... | collective-permute-start | bytes 1572872 | tf_op jit(solution)/shard_map/ppermute | solution.py:478
  27.8 0.9 fusion
  28.7 1.3 collective-permute-start.4
  30.0 28.7 %collective-permute-done.2.refs_5_ = bf16[8,2,128,128]{3,2,1,0:T(8,128)(2,1)S(1)} collective-permute-done((bf16[8,2,128,128]{3,2,1,0:T(8,128)(2,1)S(1)}, bf16[8,2,128,128]{3,2,1,0:T(8,128)(2,1)S(1)}, u32[]{:S(2)}, u32[]{:S(2)}) %collective-permute-start.2) | collective-permute-done | bytes 524320 | tf_op jit(solution)/shard_map/ppermute | solution.py:478
  58.7 1.3 collective-permute-start.3
  60.1 2.1 %collective-permute-start.1 = (bf16[8,2,128,128]{3,2,1,0:T(8,128)(2,1)}, bf16[8,2,128,128]{3,2,1,0:T(8,128)(2,1)}, u32[]{:S(2)}, u32[]{:S(2)}) collective-permute-start(bf16[8,2,128,128]{3,2,1,0:T(8,128)(2,1)} %collective-permute-done.refs_4_), channel_id=1, source_target_pairs={{0,8},{16,24},{32,40},{48,56},{64,72},{80,88},{96,104},{112,120},{... | collective-permute-start | bytes 1572872 | tf_op jit(solution)/shard_map/ppermute | solution.py:478
  63.4 0.8 copy-done.9
  64.2 1.4 copy-done.1
  65.6 5.5 %all-to-all-start.2 = ((bf16[8,8,128,128]{3,2,1,0:T(8,128)(2,1)}), bf16[8,8,128,128]{3,2,1,0:T(8,128)(2,1)}, u32[]{:S(2)}, u32[]{:S(2)}) async-start(bf16[8,8,128,128]{3,2,1,0:T(8,128)(2,1)} %get-tuple-element.19), calls=%async_computation.2 | async-start | bytes 4194304 | tf_op jit(solution)/shard_map/all_to_all | solution.py:482
  71.2 25.9 %attend.2 = (bf16[8,4,128,128]{3,2,1,0:T(8,128)(2,1)}, f32[4,2,2,128,512]{4,3,2,1,0:T(8,128)}) custom-call(s32[4]{0:T(128)} %compare_select_fusion.refs_0_, bf16[8,9,128,128]{3,2,1,0:T(8,128)(2,1)} %copy-done.1, bf16[8,9,128,128]{3,2,1,0:T(8,128)(2,1)} %copy-done.1, bf16[8,2,128,128]{3,2,1,0:T(8,128)(2,1)} %copy-done.6, ...), custom_call_target="tpu_custom_call" | custom-call | flops 22817013760 | bytes 8388608 | tf_op jit(solution)/shard_map/attend/pallas_call | solution.py:353
  97.7 27.4 %attend.3 = (bf16[8,8,128,128]{3,2,1,0:T(8,128)(2,1)}, f32[2,2,128,512]{3,2,1,0:T(8,128)}, bf16[3,2,2,128,512]{4,3,2,1,0:T(8,128)(2,1)}, bf16[2,2,128,512]{3,2,1,0:T(8,128)(2,1)}) custom-call(s32[4]{0:T(128)} %compare_select_fusion.refs_0_, bf16[8,8,128,128]{3,2,1,0:T(8,128)(2,1)} %all-to-all-done.2.refs_1_, bf16[8,9,128,128]{3,2,1,0:T(8,128)(2,1)} %copy-done.1, ...), custom_call_target="tpu_custom_call" | custom-call | flops 22817013760 | bytes 8388608 | tf_op jit(solution)/shard_map/attend/pallas_call | solution.py:353
  125.2 1.3 collective-permute-start.5
  126.5 5.2 %all-to-all-start.3 = ((bf16[8,8,128,128]{3,2,1,0:T(8,128)(2,1)}), bf16[8,8,128,128]{3,2,1,0:T(8,128)(2,1)}, u32[]{:S(2)}, u32[]{:S(2)}) async-start(bf16[8,8,128,128]{3,2,1,0:T(8,128)(2,1)} %get-tuple-element.22), calls=%async_computation.3 | async-start | bytes 4194304 | tf_op jit(solution)/shard_map/all_to_all | solution.py:482
  131.7 5.5 %collective-permute-start.8 = (bf16[2,2,128,512]{3,2,1,0:T(8,128)(2,1)S(1)}, bf16[2,2,128,512]{3,2,1,0:T(8,128)(2,1)S(1)}, u32[]{:S(2)}, u32[]{:S(2)}) collective-permute-start(bf16[2,2,128,512]{3,2,1,0:T(8,128)(2,1)S(1)} %copy-done.10), channel_id=1, source_target_pairs={{0,104},{16,120},{32,8},{48,24},{64,40},{80,56},{96,72},{112,88},{... | collective-permute-start | bytes 1572872 | tf_op jit(solution)/shard_map/ppermute | solution.py:478
  137.2 1.1 copy-done
  138.3 2.4 %join.1 = (bf16[2,2,128,512]{3,2,1,0:T(8,128)(2,1)}, bf16[2,2,128,512]{3,2,1,0:T(8,128)(2,1)}) custom-call(bf16[3,2,2,128,512]{4,3,2,1,0:T(8,128)(2,1)} %get-tuple-element.24.mine_ref, bf16[3,2,2,128,512]{4,3,2,1,0:T(8,128)(2,1)} %copy-done, bf16[3,2,2,128,512]{4,3,2,1,0:T(8,128)(2,1)} %copy-done), custom_call_target="tpu_custom_call" | custom-call | bytes 3145728 | tf_op jit(solution)/shard_map/join/pallas_call | solution.py:397
  140.7 5.3 %collective-permute-start.6 = (bf16[2,2,128,512]{3,2,1,0:T(8,128)(2,1)}, bf16[2,2,128,512]{3,2,1,0:T(8,128)(2,1)S(1)}, u32[]{:S(2)}, u32[]{:S(2)}) collective-permute-start(bf16[2,2,128,512]{3,2,1,0:T(8,128)(2,1)} %get-tuple-element.25), channel_id=1, source_target_pairs={{0,120},{16,8},{32,24},{48,40},{64,56},{80,72},{96,88},{112,104},{... | collective-permute-start | bytes 1572872 | tf_op jit(solution)/shard_map/ppermute | solution.py:478
  146.0 2.7 %collective-permute-start.7 = (bf16[2,2,128,512]{3,2,1,0:T(8,128)(2,1)}, bf16[2,2,128,512]{3,2,1,0:T(8,128)(2,1)S(1)}, u32[]{:S(2)}, u32[]{:S(2)}) collective-permute-start(bf16[2,2,128,512]{3,2,1,0:T(8,128)(2,1)} %get-tuple-element.26), channel_id=1, source_target_pairs={{0,112},{16,0},{32,16},{48,32},{64,48},{80,64},{96,80},{112,96},{1... | collective-permute-start | bytes 1572872 | tf_op jit(solution)/shard_map/ppermute | solution.py:478
  148.7 9.3 %collective-permute-done.6.refs_0_ = bf16[2,2,128,512]{3,2,1,0:T(8,128)(2,1)S(1)} collective-permute-done((bf16[2,2,128,512]{3,2,1,0:T(8,128)(2,1)}, bf16[2,2,128,512]{3,2,1,0:T(8,128)(2,1)S(1)}, u32[]{:S(2)}, u32[]{:S(2)}) %collective-permute-start.6) | collective-permute-done | bytes 524320 | tf_op jit(solution)/shard_map/ppermute | solution.py:478
  158.0 15.1 %collective-permute-done.7.refs_1_ = bf16[2,2,128,512]{3,2,1,0:T(8,128)(2,1)S(1)} collective-permute-done((bf16[2,2,128,512]{3,2,1,0:T(8,128)(2,1)}, bf16[2,2,128,512]{3,2,1,0:T(8,128)(2,1)S(1)}, u32[]{:S(2)}, u32[]{:S(2)}) %collective-permute-start.7) | collective-permute-done | bytes 524320 | tf_op jit(solution)/shard_map/ppermute | solution.py:478
  173.2 0.8 copy-done.5
  173.9 2.7 %total.1 = bf16[8,2,128,128]{3,2,1,0:T(8,128)(2,1)} custom-call(f32[2,2,128,512]{3,2,1,0:T(8,128)} %get-tuple-element.23.own_ref, bf16[3,2,2,128,512]{4,3,2,1,0:T(8,128)(2,1)} %copy-done, bf16[2,2,128,512]{3,2,1,0:T(8,128)(2,1)} %copy-done.4, bf16[2,2,128,512]{3,2,1,0:T(8,128)(2,1)} %copy-done.5, bf16[2,2,128,512]{3,2,1,0:T(8,128)(2,1)} %copy-done.3), custom_call_target="tpu_custom_call" | custom-call | bytes 4194304 | tf_op jit(solution)/shard_map/total/pallas_call | solution.py:421
  176.6 3.6 %all-to-all-start.4 = ((bf16[8,2,128,128]{3,2,1,0:T(8,128)(2,1)}), bf16[8,2,128,128]{3,2,1,0:T(8,128)(2,1)S(1)}, u32[]{:S(2)}, u32[]{:S(2)}) async-start(bf16[8,2,128,128]{3,2,1,0:T(8,128)(2,1)} %total.1), calls=%async_computation.4 | async-start | bytes 1048576 | tf_op jit(solution)/shard_map/all_to_all | solution.py:482
  180.3 2.8 %unpack_q.1 = bf16[128,8192]{1,0:T(8,128)(2,1)} custom-call(bf16[8,8,128,128]{3,2,1,0:T(8,128)(2,1)} %all-to-all-done.3.refs_0_), custom_call_target="tpu_custom_call" | custom-call | bytes 4194304 | tf_op jit(solution)/shard_map/unpack_q/pallas_call | solution.py:449
  183.1 5.9 %all-to-all-done.4.pair_ref = bf16[8,2,128,128]{3,2,1,0:T(8,128)(2,1)S(1)} async-done(((bf16[8,2,128,128]{3,2,1,0:T(8,128)(2,1)}), bf16[8,2,128,128]{3,2,1,0:T(8,128)(2,1)S(1)}, u32[]{:S(2)}, u32[]{:S(2)}) %all-to-all-start.4) | async-done | bytes 524320 | tf_op jit(solution)/shard_map/all_to_all | solution.py:482
  189.0 0.8 copy-done.2
  189.8 2.0 %unpack_kv.1 = (bf16[128,1024]{1,0:T(8,128)(2,1)}, bf16[128,1024]{1,0:T(8,128)(2,1)}) custom-call(bf16[8,2,128,128]{3,2,1,0:T(8,128)(2,1)} %copy-done.2), custom_call_target="tpu_custom_call" | custom-call | tf_op jit(solution)/shard_map/unpack_kv/pallas_call | solution.py:469
  (37 shorter events, 4.2 us)
Async XLA Ops:
  0.6 7.8 %copy-start.7 = (f32[128,64]{0,1:T(8,128)S(1)}, f32[128,64]{0,1:T(8,128)}, u32[]{:S(2)}) copy-start(f32[128,64]{0,1:T(8,128)} %param.12) | copy-start | bytes 98308
  2.7 15.8 %all-to-all-start.1 = ((bf16[8,2,128,128]{3,2,1,0:T(8,128)(2,1)}), bf16[8,2,128,128]{3,2,1,0:T(8,128)(2,1)S(1)}, u32[]{:S(2)}, u32[]{:S(2)}) async-start(bf16[8,2,128,128]{3,2,1,0:T(8,128)(2,1)} %pack_kv.1), calls=%async_computation.1 | async-start | bytes 1048576 | tf_op jit(solution)/shard_map/all_to_all | solution.py:482
  18.5 10.2 %copy-start.6 = (bf16[8,2,128,128]{3,2,1,0:T(8,128)(2,1)}, bf16[8,2,128,128]{3,2,1,0:T(8,128)(2,1)S(1)}, u32[]{:S(2)}) copy-start(bf16[8,2,128,128]{3,2,1,0:T(8,128)(2,1)S(1)} %all-to-all-done.1.refs_3_) | copy-start | bytes 1572868
  18.5 45.7 %all-to-all-start = ((bf16[8,9,128,128]{3,2,1,0:T(8,128)(2,1)}), bf16[8,9,128,128]{3,2,1,0:T(8,128)(2,1)S(1)}, u32[]{:S(2)}, u32[]{:S(2)}) async-start(bf16[8,9,128,128]{3,2,1,0:T(8,128)(2,1)} %get-tuple-element.18), calls=%async_computation | async-start | bytes 4718592 | tf_op jit(solution)/shard_map/all_to_all | solution.py:482
  22.1 36.6 %collective-permute-start.2 = (bf16[8,2,128,128]{3,2,1,0:T(8,128)(2,1)S(1)}, bf16[8,2,128,128]{3,2,1,0:T(8,128)(2,1)S(1)}, u32[]{:S(2)}, u32[]{:S(2)}) collective-permute-start(bf16[8,2,128,128]{3,2,1,0:T(8,128)(2,1)S(1)} %all-to-all-done.1.refs_3_), channel_id=1, source_target_pairs={{112,0},{0,16},{16,32},{32,48},{48,64},{64,80},{80,96},{96,112},{1... | collective-permute-start | bytes 1572872 | tf_op jit(solution)/shard_map/ppermute | solution.py:478
  27.6 32.4 %collective-permute-start = (bf16[8,2,128,128]{3,2,1,0:T(8,128)(2,1)S(1)}, bf16[8,2,128,128]{3,2,1,0:T(8,128)(2,1)}, u32[]{:S(2)}, u32[]{:S(2)}) collective-permute-start(bf16[8,2,128,128]{3,2,1,0:T(8,128)(2,1)S(1)} %all-to-all-done.1.refs_3_), channel_id=1, source_target_pairs={{0,8},{8,16},{16,24},{24,32},{32,40},{40,48},{48,56},{56,64},{64,7... | collective-permute-start | bytes 1572872 | tf_op jit(solution)/shard_map/ppermute | solution.py:478
  28.7 42.4 %collective-permute-start.4 = (bf16[8,2,128,128]{3,2,1,0:T(8,128)(2,1)S(1)}, bf16[8,2,128,128]{3,2,1,0:T(8,128)(2,1)}, u32[]{:S(2)}, u32[]{:S(2)}) collective-permute-start(bf16[8,2,128,128]{3,2,1,0:T(8,128)(2,1)S(1)} %all-to-all-done.1.refs_3_), channel_id=1, source_target_pairs={{104,0},{120,16},{8,32},{24,48},{40,64},{56,80},{72,96},{88,112},{... | collective-permute-start | bytes 1572872 | tf_op jit(solution)/shard_map/ppermute | solution.py:478
  58.7 5.5 %copy-start.8 = (bf16[8,2,128,128]{3,2,1,0:T(8,128)(2,1)}, bf16[8,2,128,128]{3,2,1,0:T(8,128)(2,1)S(1)}, u32[]{:S(2)}) copy-start(bf16[8,2,128,128]{3,2,1,0:T(8,128)(2,1)S(1)} %collective-permute-done.2.refs_5_) | copy-start | bytes 1572868
  58.7 4.7 %collective-permute-start.3 = (bf16[8,2,128,128]{3,2,1,0:T(8,128)(2,1)S(1)}, bf16[8,2,128,128]{3,2,1,0:T(8,128)(2,1)S(1)}, u32[]{:S(2)}, u32[]{:S(2)}) collective-permute-start(bf16[8,2,128,128]{3,2,1,0:T(8,128)(2,1)S(1)} %collective-permute-done.2.refs_5_), channel_id=1, source_target_pairs={{0,8},{16,24},{32,40},{48,56},{64,72},{80,88},{96,104},{112,120},{... | collective-permute-start | bytes 1572872 | tf_op jit(solution)/shard_map/ppermute | solution.py:478
  60.1 4.1 %collective-permute-start.1 = (bf16[8,2,128,128]{3,2,1,0:T(8,128)(2,1)}, bf16[8,2,128,128]{3,2,1,0:T(8,128)(2,1)}, u32[]{:S(2)}, u32[]{:S(2)}) collective-permute-start(bf16[8,2,128,128]{3,2,1,0:T(8,128)(2,1)} %collective-permute-done.refs_4_), channel_id=1, source_target_pairs={{0,8},{16,24},{32,40},{48,56},{64,72},{80,88},{96,104},{112,120},{... | collective-permute-start | bytes 1572872 | tf_op jit(solution)/shard_map/ppermute | solution.py:478
  63.4 0.8 copy-start.9
  64.2 1.4 copy-start.1
  65.6 32.1 %all-to-all-start.2 = ((bf16[8,8,128,128]{3,2,1,0:T(8,128)(2,1)}), bf16[8,8,128,128]{3,2,1,0:T(8,128)(2,1)}, u32[]{:S(2)}, u32[]{:S(2)}) async-start(bf16[8,8,128,128]{3,2,1,0:T(8,128)(2,1)} %get-tuple-element.19), calls=%async_computation.2 | async-start | bytes 4194304 | tf_op jit(solution)/shard_map/all_to_all | solution.py:482
  125.2 12.0 %collective-permute-start.5 = (bf16[3,2,2,128,512]{4,3,2,1,0:T(8,128)(2,1)}, bf16[3,2,2,128,512]{4,3,2,1,0:T(8,128)(2,1)S(1)}, u32[]{:S(2)}, u32[]{:S(2)}) collective-permute-start(bf16[3,2,2,128,512]{4,3,2,1,0:T(8,128)(2,1)} %get-tuple-element.24.mine_ref), channel_id=1, source_target_pairs={{8,0},{24,16},{40,32},{56,48},{72,64},{88,80},{104,96},{120,112},{... | collective-permute-start | bytes 4718600 | tf_op jit(solution)/shard_map/ppermute | solution.py:478
  126.5 5.2 %copy-start.10 = (bf16[2,2,128,512]{3,2,1,0:T(8,128)(2,1)S(1)}, bf16[2,2,128,512]{3,2,1,0:T(8,128)(2,1)}, u32[]{:S(2)}) copy-start(bf16[2,2,128,512]{3,2,1,0:T(8,128)(2,1)} %get-tuple-element.27) | copy-start | bytes 1572868
  126.5 50.2 %all-to-all-start.3 = ((bf16[8,8,128,128]{3,2,1,0:T(8,128)(2,1)}), bf16[8,8,128,128]{3,2,1,0:T(8,128)(2,1)}, u32[]{:S(2)}, u32[]{:S(2)}) async-start(bf16[8,8,128,128]{3,2,1,0:T(8,128)(2,1)} %get-tuple-element.22), calls=%async_computation.3 | async-start | bytes 4194304 | tf_op jit(solution)/shard_map/all_to_all | solution.py:482
  131.7 17.0 %collective-permute-start.8 = (bf16[2,2,128,512]{3,2,1,0:T(8,128)(2,1)S(1)}, bf16[2,2,128,512]{3,2,1,0:T(8,128)(2,1)S(1)}, u32[]{:S(2)}, u32[]{:S(2)}) collective-permute-start(bf16[2,2,128,512]{3,2,1,0:T(8,128)(2,1)S(1)} %copy-done.10), channel_id=1, source_target_pairs={{0,104},{16,120},{32,8},{48,24},{64,40},{80,56},{96,72},{112,88},{... | collective-permute-start | bytes 1572872 | tf_op jit(solution)/shard_map/ppermute | solution.py:478
  137.2 1.1 copy-start
  140.7 17.3 %collective-permute-start.6 = (bf16[2,2,128,512]{3,2,1,0:T(8,128)(2,1)}, bf16[2,2,128,512]{3,2,1,0:T(8,128)(2,1)S(1)}, u32[]{:S(2)}, u32[]{:S(2)}) collective-permute-start(bf16[2,2,128,512]{3,2,1,0:T(8,128)(2,1)} %get-tuple-element.25), channel_id=1, source_target_pairs={{0,120},{16,8},{32,24},{48,40},{64,56},{80,72},{96,88},{112,104},{... | collective-permute-start | bytes 1572872 | tf_op jit(solution)/shard_map/ppermute | solution.py:478
  146.0 27.1 %collective-permute-start.7 = (bf16[2,2,128,512]{3,2,1,0:T(8,128)(2,1)}, bf16[2,2,128,512]{3,2,1,0:T(8,128)(2,1)S(1)}, u32[]{:S(2)}, u32[]{:S(2)}) collective-permute-start(bf16[2,2,128,512]{3,2,1,0:T(8,128)(2,1)} %get-tuple-element.26), channel_id=1, source_target_pairs={{0,112},{16,0},{32,16},{48,32},{64,48},{80,64},{96,80},{112,96},{1... | collective-permute-start | bytes 1572872 | tf_op jit(solution)/shard_map/ppermute | solution.py:478
  148.7 24.4 %copy-start.3 = (bf16[2,2,128,512]{3,2,1,0:T(8,128)(2,1)}, bf16[2,2,128,512]{3,2,1,0:T(8,128)(2,1)S(1)}, u32[]{:S(2)}) copy-start(bf16[2,2,128,512]{3,2,1,0:T(8,128)(2,1)S(1)} %collective-permute-done.8.refs_2_) | copy-start | bytes 1572868
  158.0 15.1 %copy-start.4 = (bf16[2,2,128,512]{3,2,1,0:T(8,128)(2,1)}, bf16[2,2,128,512]{3,2,1,0:T(8,128)(2,1)S(1)}, u32[]{:S(2)}) copy-start(bf16[2,2,128,512]{3,2,1,0:T(8,128)(2,1)S(1)} %collective-permute-done.6.refs_0_) | copy-start | bytes 1572868
  173.1 0.8 copy-start.5
  176.6 12.3 %all-to-all-start.4 = ((bf16[8,2,128,128]{3,2,1,0:T(8,128)(2,1)}), bf16[8,2,128,128]{3,2,1,0:T(8,128)(2,1)S(1)}, u32[]{:S(2)}, u32[]{:S(2)}) async-start(bf16[8,2,128,128]{3,2,1,0:T(8,128)(2,1)} %total.1), calls=%async_computation.4 | async-start | bytes 1048576 | tf_op jit(solution)/shard_map/all_to_all | solution.py:482
  189.0 0.8 copy-start.2

commit v6 on v5

--- a/solution.py
+++ b/solution.py
@@ -124,7 +124,7 @@
     )(queries, grad_out, attn_out, log_norm, doc_block)
 
 
-def attend_kernel(count, first_head, kv_counts, has_dkv, has_dq, last, *refs):
+def attend_kernel(count, first_head, kv_counts, has_dkv, last, *refs):
     refs = list(refs)
 
     def take(n):
@@ -136,13 +136,11 @@
     kv_hbm = [take(n) for n in kv_counts]
     (kdoc_ref,) = take(1)
     (dkv_in,) = take(1) if has_dkv else (None,)
-    (dq_in,) = take(1) if has_dq else (None,)
     (dq_ref,) = take(1)
     dkv_out = take(3 if last else 1)
     qt_ref, dot_ref, sel_ref, kv_ref, p_ref, ds_ref, dqt_ref = take(7)
     qd_ref, stat_ref, raw_ref, sum_ref, sems = take(5)
     (others_ref,) = take(1) if last else (None,)
-    ahead = dq_ref.shape[1] - count
 
     def qd_copy(half):
         rows = pl.ds(half * 4, 4)
@@ -180,8 +178,6 @@
             stores.append(
                 pltpu.make_async_copy(sum_ref.at[step], dkv_out[0].at[step], sems.at[13 + step])
             )
-    if has_dq:
-        dq_copy = pltpu.make_async_copy(dq_in, dq_ref.at[:, 0:ahead], sems.at[18])
 
     qd_copy(0).start()
     stat_copy.start()
@@ -191,8 +187,6 @@
     for step_loads in loads[1:]:
         for copy in step_loads:
             copy.start()
-    if has_dq:
-        dq_copy.start()
 
     row = lax.broadcasted_iota(jnp.int32, (48, HALF), 0)
     for h in range(count):
@@ -317,29 +311,25 @@
         for h in range(count):
             for i in range(4):
                 piece = dqt_ref[half, h, :, i * TOK : (i + 1) * TOK]
-                dq_ref[half * 4 + i, ahead + h] = (piece * SCALE).astype(BF).T
-    if has_dq:
-        dq_copy.wait()
+                dq_ref[half * 4 + i, h] = (piece * SCALE).astype(BF).T
     for copy in stores:
         copy.wait()
     if last:
         three_store.wait()
 
 
-def attend(chunk, second, qd, stats, kvs, kdoc, dkv, dq, last):
+def attend(chunk, second, qd, stats, kvs, kdoc, dkv, last):
     first_head, count = sum(CHUNKS[:chunk]), CHUNKS[chunk]
     operands = [second, qd, stats]
     for sources in kvs:
         operands += sources
     operands.append(kdoc)
     operands += [] if dkv is None else [dkv]
-    operands += [] if dq is None else [dq]
     vmem = pl.BlockSpec(memory_space=pltpu.VMEM)
     anywhere = pl.BlockSpec(memory_space=pl.ANY)
     flops = int(8.5 * 5 * 2 * HALF * HALF * HD * count)
-    out_heads = count + (0 if dq is None else dq.shape[1])
     sums = (STEPS, 2, 2, HD, HALF)
-    shapes = [((8, out_heads, TOK, HD), BF)]
+    shapes = [((8, count, TOK, HD), BF)]
     shapes += [(sums[1:], F32), ((3,) + sums[1:], BF), (sums[1:], BF)] if last else [(sums, F32)]
     kernel = functools.partial(
         attend_kernel,
@@ -347,7 +337,6 @@
         first_head,
         [len(sources) for sources in kvs],
         dkv is not None,
-        dq is not None,
         last,
     )
     return pl.pallas_call(
@@ -356,7 +345,7 @@
             pl.BlockSpec(memory_space=pltpu.SMEM),
             *[anywhere] * (2 + sum(len(sources) for sources in kvs)),
             vmem,
-            *[anywhere] * ((dkv is not None) + (dq is not None)),
+            *[anywhere] * (dkv is not None),
         ],
         out_specs=[vmem] + [anywhere] * (len(shapes) - 1),
         out_shape=[jax.ShapeDtypeStruct(*shape) for shape in shapes],
@@ -372,7 +361,7 @@
             pltpu.VMEM((8, TOK, HD), BF),
             pltpu.VMEM((sum(len(sources) for sources in kvs), 8, 2, HD, TOK), BF),
             pltpu.VMEM(sums, F32),
-            pltpu.SemaphoreType.DMA((19,)),
+            pltpu.SemaphoreType.DMA((18,)),
         ]
         + ([pltpu.VMEM((3,) + sums[1:], BF)] if last else []),
         compiler_params=pltpu.CompilerParams(vmem_limit_bytes=VMEM_LIMIT),
@@ -522,20 +511,23 @@
 
     packed = pack_q(queries, grad_out, attn_out, log_norm, doc_block)
     early = exchange(packed[0])
-    late, *_ = lax.optimization_barrier((packed[1], early, two_inner, three_inner))
+    late, *_ = lax.optimization_barrier((packed[1], early))
     late = exchange(late)
-    dq, dkv = attend(0, second, early, early, kvs, kdoc, None, None, False)
-    dq, own, others, three = attend(1, second, late, early, kvs, kdoc, dkv, dq, True)
-
+    dq_early, dkv = attend(0, second, early, early, kvs, kdoc, None, False)
+    dq_early, *_ = lax.optimization_barrier((dq_early, late))
+    dq_early = exchange(dq_early)
+    dq_late, own, others, far = attend(1, second, late, early, kvs, kdoc, dkv, True)
+
+    others, dq_early = lax.optimization_barrier((others, dq_early))
     theirs = move(others, inner_down)
-    dq = exchange(dq)
-    from_three = move(three, down[3])
+    dq_late = exchange(dq_late)
+    from_three = move(far, down[3])
     to_one, to_two = join(others, theirs)
     from_one, from_two = move(to_one, down[1]), move(to_two, down[2])
     pair = total(own, theirs, from_one, from_two, from_three)
-    pair, *_ = lax.optimization_barrier((pair, dq))
+    pair, *_ = lax.optimization_barrier((pair, dq_late))
     grad_keys, grad_values = unpack_kv(exchange(pair))
-    return unpack_q([dq]), grad_keys, grad_values
+    return unpack_q([dq_early, dq_late]), grad_keys, grad_values
 
 
 def solution(mesh):

time: 193 us -> 187 us (0.969)
  waiting for transfers between devices: 61.9 us -> 50.4 us
  starting transfers between devices: 48.7 us -> 55.9 us
    ppermute x9, waiting for transfers between devices: 53.1 us -> 42.4 us  [move(): return lax.ppermute(value, 'blk', pairs)]
    all_to_all x5 -> x6, starting transfers between devices: 23.7 us -> 29.8 us  [exchange(): return lax.all_to_all(value, 'uly', split_axis=0, concat_axis=0, tiled=True)]
    unnamed x23 -> x21, local copies, waits for them, and re-layouts: 5.68 us -> 4.97 us
    all_to_all x5 -> x6, waiting for transfers between devices: 8.72 us -> 8.01 us  [exchange(): return lax.all_to_all(value, 'uly', split_axis=0, concat_axis=0, tiled=True)]
  transfers between devices with their start and end apart: 14 -> 15, of which waited for: 6 -> 5; matrix products, arithmetic and copies ran while one was open for 2% -> 2% of each run, Pallas kernels for 21% -> 36%
where the time goes in v6:
time: 187 us; the launch traced here: 186 us
  Pallas kernels  70.4 us (38%)
  starting transfers between devices  55.9 us (30%)
  waiting for transfers between devices  50.4 us (27%)
  local copies, waits for them, and re-layouts  6.63 us (4%)
  other arithmetic  1.93 us (1%)
    pallas_call x2, Pallas kernels, attend(): pl.pallas_call(kernel, in_specs=[pl.BlockSpec(memory_space=pltpu.SMEM), *...  52.7 us
    ppermute x9, waiting for transfers between devices, move(): return lax.ppermute(value, 'blk', pairs)  42.4 us
    all_to_all x6, starting transfers between devices, exchange(): return lax.all_to_all(value, 'uly', split_axis=0, concat_axis=0, tiled=True)  29.8 us
    ppermute x9, starting transfers between devices, move(): return lax.ppermute(value, 'blk', pairs)  26.1 us
    all_to_all x6, waiting for transfers between devices, exchange(): return lax.all_to_all(value, 'uly', split_axis=0, concat_axis=0, tiled=True)  8.01 us
    pallas_call x1, Pallas kernels, pack_q(): pl.pallas_call(functools.partial(pack_q_kernel, per), grid=(8 // per,), i...  5.7 us
    unnamed x21, local copies, waits for them, and re-layouts  4.97 us
  transfers between devices with their start and end apart: 15, of which 5 were waited for; matrix products, arithmetic and copies ran while one was open for 2% of the time, Pallas kernels for 36%

profile of v6, /device:TPU:0, one launch (start us, length us, event | category | flops | bytes accessed | tf_op | source)
XLA Modules:
  0.0 186.1 jit_solution(18445514008496454647)
XLA Ops:
  0.6 2.0 %pack_kv.1 = bf16[8,2,128,128]{3,2,1,0:T(8,128)(2,1)} custom-call(bf16[128,1024]{1,0:T(8,128)(2,1)} %k_ref.1, bf16[128,1024]{1,0:T(8,128)(2,1)} %v_ref.1), custom_call_target="tpu_custom_call" | custom-call | bytes 1048576 | tf_op jit(solution)/shard_map/pack_kv/pallas_call | solution.py:53
  2.7 5.7 %all-to-all-start.2 = ((bf16[8,2,128,128]{3,2,1,0:T(8,128)(2,1)}), bf16[8,2,128,128]{3,2,1,0:T(8,128)(2,1)S(1)}, u32[]{:S(2)}, u32[]{:S(2)}) async-start(bf16[8,2,128,128]{3,2,1,0:T(8,128)(2,1)} %pack_kv.1), calls=%async_computation.2 | async-start | bytes 1048576 | tf_op jit(solution)/shard_map/all_to_all | solution.py:471
  10.6 5.7 %pack_q.1 = (bf16[8,9,128,128]{3,2,1,0:T(8,128)(2,1)}, bf16[8,8,128,128]{3,2,1,0:T(8,128)(2,1)}) custom-call(bf16[128,8192]{1,0:T(8,128)(2,1)} %q_ref.1, bf16[128,8192]{1,0:T(8,128)(2,1)} %do_ref.1, bf16[128,8192]{1,0:T(8,128)(2,1)} %o_ref.1, f32[128,64]{1,0:T(8,128)} %copy.10.ln_ref, bf16[128,128]{1,0:T(8,128)(2,1)} %select_convert_fusion.1.doc_ref), custom_call_target="tpu_custom_call" | custom-call | bytes 11534336 | tf_op jit(solution)/shard_map/pack_q/pallas_call | solution.py:108
  16.3 2.2 %all-to-all-done.2.refs_3_ = bf16[8,2,128,128]{3,2,1,0:T(8,128)(2,1)S(1)} async-done(((bf16[8,2,128,128]{3,2,1,0:T(8,128)(2,1)}), bf16[8,2,128,128]{3,2,1,0:T(8,128)(2,1)S(1)}, u32[]{:S(2)}, u32[]{:S(2)}) %all-to-all-start.2) | async-done | bytes 524320 | tf_op jit(solution)/shard_map/all_to_all | solution.py:471
  18.5 3.6 %all-to-all-start = ((bf16[8,9,128,128]{3,2,1,0:T(8,128)(2,1)}), bf16[8,9,128,128]{3,2,1,0:T(8,128)(2,1)S(1)}, u32[]{:S(2)}, u32[]{:S(2)}) async-start(bf16[8,9,128,128]{3,2,1,0:T(8,128)(2,1)} %get-tuple-element.21), calls=%async_computation | async-start | bytes 4718592 | tf_op jit(solution)/shard_map/all_to_all | solution.py:471
  22.1 5.5 %collective-permute-start.1 = (bf16[8,2,128,128]{3,2,1,0:T(8,128)(2,1)S(1)}, bf16[8,2,128,128]{3,2,1,0:T(8,128)(2,1)}, u32[]{:S(2)}, u32[]{:S(2)}) collective-permute-start(bf16[8,2,128,128]{3,2,1,0:T(8,128)(2,1)S(1)} %all-to-all-done.2.refs_3_), channel_id=1, source_target_pairs={{112,0},{0,16},{16,32},{32,48},{48,64},{64,80},{80,96},{96,112},{1... | collective-permute-start | bytes 1572872 | tf_op jit(solution)/shard_map/ppermute | solution.py:467
  27.8 0.9 fusion
  28.7 1.3 collective-permute-start.3
  30.0 28.7 %collective-permute-done.1.refs_5_ = bf16[8,2,128,128]{3,2,1,0:T(8,128)(2,1)} collective-permute-done((bf16[8,2,128,128]{3,2,1,0:T(8,128)(2,1)S(1)}, bf16[8,2,128,128]{3,2,1,0:T(8,128)(2,1)}, u32[]{:S(2)}, u32[]{:S(2)}) %collective-permute-start.1) | collective-permute-done | bytes 524320 | tf_op jit(solution)/shard_map/ppermute | solution.py:467
  58.7 2.1 %collective-permute-start.4 = (bf16[8,2,128,128]{3,2,1,0:T(8,128)(2,1)}, bf16[8,2,128,128]{3,2,1,0:T(8,128)(2,1)}, u32[]{:S(2)}, u32[]{:S(2)}) collective-permute-start(bf16[8,2,128,128]{3,2,1,0:T(8,128)(2,1)} %collective-permute-done.1.refs_5_), channel_id=1, source_target_pairs={{0,8},{16,24},{32,40},{48,56},{64,72},{80,88},{96,104},{112,120},{... | collective-permute-start | bytes 1572872 | tf_op jit(solution)/shard_map/ppermute | solution.py:467
  60.8 2.1 %collective-permute-start.2 = (bf16[8,2,128,128]{3,2,1,0:T(8,128)(2,1)}, bf16[8,2,128,128]{3,2,1,0:T(8,128)(2,1)}, u32[]{:S(2)}, u32[]{:S(2)}) collective-permute-start(bf16[8,2,128,128]{3,2,1,0:T(8,128)(2,1)} %collective-permute-done.refs_4_), channel_id=1, source_target_pairs={{0,8},{16,24},{32,40},{48,56},{64,72},{80,88},{96,104},{112,120},{... | collective-permute-start | bytes 1572872 | tf_op jit(solution)/shard_map/ppermute | solution.py:467
  64.2 1.4 copy-done.2
  65.6 5.5 %all-to-all-start.1 = ((bf16[8,8,128,128]{3,2,1,0:T(8,128)(2,1)}), bf16[8,8,128,128]{3,2,1,0:T(8,128)(2,1)}, u32[]{:S(2)}, u32[]{:S(2)}) async-start(bf16[8,8,128,128]{3,2,1,0:T(8,128)(2,1)} %get-tuple-element.22), calls=%async_computation.1 | async-start | bytes 4194304 | tf_op jit(solution)/shard_map/all_to_all | solution.py:471
  71.1 25.9 %attend.2 = (bf16[8,4,128,128]{3,2,1,0:T(8,128)(2,1)}, f32[4,2,2,128,512]{4,3,2,1,0:T(8,128)}) custom-call(s32[4]{0:T(128)} %compare_select_fusion.refs_0_, bf16[8,9,128,128]{3,2,1,0:T(8,128)(2,1)} %copy-done.2, bf16[8,9,128,128]{3,2,1,0:T(8,128)(2,1)} %copy-done.2, bf16[8,2,128,128]{3,2,1,0:T(8,128)(2,1)} %copy-done.7, ...), custom_call_target="tpu_custom_call" | custom-call | flops 22817013760 | bytes 8388608 | tf_op jit(solution)/shard_map/attend/pallas_call | solution.py:342
  97.0 5.7 %all-to-all-start.3 = ((bf16[8,4,128,128]{3,2,1,0:T(8,128)(2,1)}), bf16[8,4,128,128]{3,2,1,0:T(8,128)(2,1)S(1)}, u32[]{:S(2)}, u32[]{:S(2)}) async-start(bf16[8,4,128,128]{3,2,1,0:T(8,128)(2,1)} %get-tuple-element.26), calls=%async_computation.3 | async-start | bytes 2097152 | tf_op jit(solution)/shard_map/all_to_all | solution.py:471
  102.7 26.8 %attend.3 = (bf16[8,4,128,128]{3,2,1,0:T(8,128)(2,1)}, f32[2,2,128,512]{3,2,1,0:T(8,128)}, bf16[3,2,2,128,512]{4,3,2,1,0:T(8,128)(2,1)}, bf16[2,2,128,512]{3,2,1,0:T(8,128)(2,1)}) custom-call(s32[4]{0:T(128)} %compare_select_fusion.refs_0_, bf16[8,8,128,128]{3,2,1,0:T(8,128)(2,1)} %all-to-all-done.1.refs_1_, bf16[8,9,128,128]{3,2,1,0:T(8,128)(2,1)} %copy-done.2, ...), custom_call_target="tpu_custom_call" | custom-call | flops 22817013760 | bytes 8388608 | tf_op jit(solution)/shard_map/attend/pallas_call | solution.py:342
  129.6 1.4 collective-permute-start.5
  131.0 5.7 %all-to-all-start.4 = ((bf16[8,4,128,128]{3,2,1,0:T(8,128)(2,1)}), bf16[8,4,128,128]{3,2,1,0:T(8,128)(2,1)}, u32[]{:S(2)}, u32[]{:S(2)}) async-start(bf16[8,4,128,128]{3,2,1,0:T(8,128)(2,1)} %get-tuple-element.28), calls=%async_computation.4 | async-start | bytes 2097152 | tf_op jit(solution)/shard_map/all_to_all | solution.py:471
  136.8 5.5 %collective-permute-start.8 = (bf16[2,2,128,512]{3,2,1,0:T(8,128)(2,1)S(1)}, bf16[2,2,128,512]{3,2,1,0:T(8,128)(2,1)S(1)}, u32[]{:S(2)}, u32[]{:S(2)}) collective-permute-start(bf16[2,2,128,512]{3,2,1,0:T(8,128)(2,1)S(1)} %copy-done.9), channel_id=1, source_target_pairs={{0,104},{16,120},{32,8},{48,24},{64,40},{80,56},{96,72},{112,88},{... | collective-permute-start | bytes 1572872 | tf_op jit(solution)/shard_map/ppermute | solution.py:467
  142.3 1.2 copy-done
  143.5 2.4 %join.1 = (bf16[2,2,128,512]{3,2,1,0:T(8,128)(2,1)}, bf16[2,2,128,512]{3,2,1,0:T(8,128)(2,1)}) custom-call(bf16[3,2,2,128,512]{4,3,2,1,0:T(8,128)(2,1)} %get-tuple-element.30.mine_ref, bf16[3,2,2,128,512]{4,3,2,1,0:T(8,128)(2,1)} %copy-done, bf16[3,2,2,128,512]{4,3,2,1,0:T(8,128)(2,1)} %copy-done), custom_call_target="tpu_custom_call" | custom-call | bytes 3145728 | tf_op jit(solution)/shard_map/join/pallas_call | solution.py:386
  145.9 5.4 %collective-permute-start.6 = (bf16[2,2,128,512]{3,2,1,0:T(8,128)(2,1)}, bf16[2,2,128,512]{3,2,1,0:T(8,128)(2,1)S(1)}, u32[]{:S(2)}, u32[]{:S(2)}) collective-permute-start(bf16[2,2,128,512]{3,2,1,0:T(8,128)(2,1)} %get-tuple-element.31), channel_id=1, source_target_pairs={{0,120},{16,8},{32,24},{48,40},{64,56},{80,72},{96,88},{112,104},{... | collective-permute-start | bytes 1572872 | tf_op jit(solution)/shard_map/ppermute | solution.py:467
  151.3 2.7 %collective-permute-start.7 = (bf16[2,2,128,512]{3,2,1,0:T(8,128)(2,1)}, bf16[2,2,128,512]{3,2,1,0:T(8,128)(2,1)S(1)}, u32[]{:S(2)}, u32[]{:S(2)}) collective-permute-start(bf16[2,2,128,512]{3,2,1,0:T(8,128)(2,1)} %get-tuple-element.32), channel_id=1, source_target_pairs={{0,112},{16,0},{32,16},{48,32},{64,48},{80,64},{96,80},{112,96},{1... | collective-permute-start | bytes 1572872 | tf_op jit(solution)/shard_map/ppermute | solution.py:467
  154.0 4.3 %collective-permute-done.6.refs_0_ = bf16[2,2,128,512]{3,2,1,0:T(8,128)(2,1)S(1)} collective-permute-done((bf16[2,2,128,512]{3,2,1,0:T(8,128)(2,1)}, bf16[2,2,128,512]{3,2,1,0:T(8,128)(2,1)S(1)}, u32[]{:S(2)}, u32[]{:S(2)}) %collective-permute-start.6) | collective-permute-done | bytes 524320 | tf_op jit(solution)/shard_map/ppermute | solution.py:467
  158.3 9.4 %collective-permute-done.7.refs_1_ = bf16[2,2,128,512]{3,2,1,0:T(8,128)(2,1)S(1)} collective-permute-done((bf16[2,2,128,512]{3,2,1,0:T(8,128)(2,1)}, bf16[2,2,128,512]{3,2,1,0:T(8,128)(2,1)S(1)}, u32[]{:S(2)}, u32[]{:S(2)}) %collective-permute-start.7) | collective-permute-done | bytes 524320 | tf_op jit(solution)/shard_map/ppermute | solution.py:467
  167.6 0.8 copy-done.6
  168.4 2.8 %total.1 = bf16[8,2,128,128]{3,2,1,0:T(8,128)(2,1)} custom-call(f32[2,2,128,512]{3,2,1,0:T(8,128)} %get-tuple-element.29.own_ref, bf16[3,2,2,128,512]{4,3,2,1,0:T(8,128)(2,1)} %copy-done, bf16[2,2,128,512]{3,2,1,0:T(8,128)(2,1)} %copy-done.5, bf16[2,2,128,512]{3,2,1,0:T(8,128)(2,1)} %copy-done.6, bf16[2,2,128,512]{3,2,1,0:T(8,128)(2,1)} %copy-done.4), custom_call_target="tpu_custom_call" | custom-call | bytes 4194304 | tf_op jit(solution)/shard_map/total/pallas_call | solution.py:410
  171.2 3.5 %all-to-all-start.5 = ((bf16[8,2,128,128]{3,2,1,0:T(8,128)(2,1)}), bf16[8,2,128,128]{3,2,1,0:T(8,128)(2,1)S(1)}, u32[]{:S(2)}, u32[]{:S(2)}) async-start(bf16[8,2,128,128]{3,2,1,0:T(8,128)(2,1)} %total.1), calls=%async_computation.5 | async-start | bytes 1048576 | tf_op jit(solution)/shard_map/all_to_all | solution.py:471
  174.7 2.8 %unpack_q.1 = bf16[128,8192]{1,0:T(8,128)(2,1)} custom-call(bf16[8,4,128,128]{3,2,1,0:T(8,128)(2,1)} %copy-done.1, bf16[8,4,128,128]{3,2,1,0:T(8,128)(2,1)} %all-to-all-done.4.refs_1_), custom_call_target="tpu_custom_call" | custom-call | bytes 4194304 | tf_op jit(solution)/shard_map/unpack_q/pallas_call | solution.py:438
  177.5 5.8 %all-to-all-done.5.pair_ref = bf16[8,2,128,128]{3,2,1,0:T(8,128)(2,1)S(1)} async-done(((bf16[8,2,128,128]{3,2,1,0:T(8,128)(2,1)}), bf16[8,2,128,128]{3,2,1,0:T(8,128)(2,1)S(1)}, u32[]{:S(2)}, u32[]{:S(2)}) %all-to-all-start.5) | async-done | bytes 524320 | tf_op jit(solution)/shard_map/all_to_all | solution.py:471
  183.3 0.8 copy-done.3
  184.1 2.0 %unpack_kv.1 = (bf16[128,1024]{1,0:T(8,128)(2,1)}, bf16[128,1024]{1,0:T(8,128)(2,1)}) custom-call(bf16[8,2,128,128]{3,2,1,0:T(8,128)(2,1)} %copy-done.3), custom_call_target="tpu_custom_call" | custom-call | tf_op jit(solution)/shard_map/unpack_kv/pallas_call | solution.py:458
  (37 shorter events, 3.6 us)
Async XLA Ops:
  0.6 7.8 %copy-start.8 = (f32[128,64]{0,1:T(8,128)S(1)}, f32[128,64]{0,1:T(8,128)}, u32[]{:S(2)}) copy-start(f32[128,64]{0,1:T(8,128)} %param.12) | copy-start | bytes 98308
  2.7 15.8 %all-to-all-start.2 = ((bf16[8,2,128,128]{3,2,1,0:T(8,128)(2,1)}), bf16[8,2,128,128]{3,2,1,0:T(8,128)(2,1)S(1)}, u32[]{:S(2)}, u32[]{:S(2)}) async-start(bf16[8,2,128,128]{3,2,1,0:T(8,128)(2,1)} %pack_kv.1), calls=%async_computation.2 | async-start | bytes 1048576 | tf_op jit(solution)/shard_map/all_to_all | solution.py:471
  18.5 10.2 %copy-start.7 = (bf16[8,2,128,128]{3,2,1,0:T(8,128)(2,1)}, bf16[8,2,128,128]{3,2,1,0:T(8,128)(2,1)S(1)}, u32[]{:S(2)}) copy-start(bf16[8,2,128,128]{3,2,1,0:T(8,128)(2,1)S(1)} %all-to-all-done.2.refs_3_) | copy-start | bytes 1572868
  18.5 45.7 %all-to-all-start = ((bf16[8,9,128,128]{3,2,1,0:T(8,128)(2,1)}), bf16[8,9,128,128]{3,2,1,0:T(8,128)(2,1)S(1)}, u32[]{:S(2)}, u32[]{:S(2)}) async-start(bf16[8,9,128,128]{3,2,1,0:T(8,128)(2,1)} %get-tuple-element.21), calls=%async_computation | async-start | bytes 4718592 | tf_op jit(solution)/shard_map/all_to_all | solution.py:471
  22.1 36.6 %collective-permute-start.1 = (bf16[8,2,128,128]{3,2,1,0:T(8,128)(2,1)S(1)}, bf16[8,2,128,128]{3,2,1,0:T(8,128)(2,1)}, u32[]{:S(2)}, u32[]{:S(2)}) collective-permute-start(bf16[8,2,128,128]{3,2,1,0:T(8,128)(2,1)S(1)} %all-to-all-done.2.refs_3_), channel_id=1, source_target_pairs={{112,0},{0,16},{16,32},{32,48},{48,64},{64,80},{80,96},{96,112},{1... | collective-permute-start | bytes 1572872 | tf_op jit(solution)/shard_map/ppermute | solution.py:467
  27.6 33.2 %collective-permute-start = (bf16[8,2,128,128]{3,2,1,0:T(8,128)(2,1)S(1)}, bf16[8,2,128,128]{3,2,1,0:T(8,128)(2,1)}, u32[]{:S(2)}, u32[]{:S(2)}) collective-permute-start(bf16[8,2,128,128]{3,2,1,0:T(8,128)(2,1)S(1)} %all-to-all-done.2.refs_3_), channel_id=1, source_target_pairs={{0,8},{8,16},{16,24},{24,32},{32,40},{40,48},{48,56},{56,64},{64,7... | collective-permute-start | bytes 1572872 | tf_op jit(solution)/shard_map/ppermute | solution.py:467
  28.7 42.4 %collective-permute-start.3 = (bf16[8,2,128,128]{3,2,1,0:T(8,128)(2,1)S(1)}, bf16[8,2,128,128]{3,2,1,0:T(8,128)(2,1)}, u32[]{:S(2)}, u32[]{:S(2)}) collective-permute-start(bf16[8,2,128,128]{3,2,1,0:T(8,128)(2,1)S(1)} %all-to-all-done.2.refs_3_), channel_id=1, source_target_pairs={{104,0},{120,16},{8,32},{24,48},{40,64},{56,80},{72,96},{88,112},{... | collective-permute-start | bytes 1572872 | tf_op jit(solution)/shard_map/ppermute | solution.py:467
  58.7 12.4 %collective-permute-start.4 = (bf16[8,2,128,128]{3,2,1,0:T(8,128)(2,1)}, bf16[8,2,128,128]{3,2,1,0:T(8,128)(2,1)}, u32[]{:S(2)}, u32[]{:S(2)}) collective-permute-start(bf16[8,2,128,128]{3,2,1,0:T(8,128)(2,1)} %collective-permute-done.1.refs_5_), channel_id=1, source_target_pairs={{0,8},{16,24},{32,40},{48,56},{64,72},{80,88},{96,104},{112,120},{... | collective-permute-start | bytes 1572872 | tf_op jit(solution)/shard_map/ppermute | solution.py:467
  60.8 10.3 %collective-permute-start.2 = (bf16[8,2,128,128]{3,2,1,0:T(8,128)(2,1)}, bf16[8,2,128,128]{3,2,1,0:T(8,128)(2,1)}, u32[]{:S(2)}, u32[]{:S(2)}) collective-permute-start(bf16[8,2,128,128]{3,2,1,0:T(8,128)(2,1)} %collective-permute-done.refs_4_), channel_id=1, source_target_pairs={{0,8},{16,24},{32,40},{48,56},{64,72},{80,88},{96,104},{112,120},{... | collective-permute-start | bytes 1572872 | tf_op jit(solution)/shard_map/ppermute | solution.py:467
  64.2 1.4 copy-start.2
  65.6 31.4 %all-to-all-start.1 = ((bf16[8,8,128,128]{3,2,1,0:T(8,128)(2,1)}), bf16[8,8,128,128]{3,2,1,0:T(8,128)(2,1)}, u32[]{:S(2)}, u32[]{:S(2)}) async-start(bf16[8,8,128,128]{3,2,1,0:T(8,128)(2,1)} %get-tuple-element.22), calls=%async_computation.1 | async-start | bytes 4194304 | tf_op jit(solution)/shard_map/all_to_all | solution.py:471
  97.0 32.6 %all-to-all-start.3 = ((bf16[8,4,128,128]{3,2,1,0:T(8,128)(2,1)}), bf16[8,4,128,128]{3,2,1,0:T(8,128)(2,1)S(1)}, u32[]{:S(2)}, u32[]{:S(2)}) async-start(bf16[8,4,128,128]{3,2,1,0:T(8,128)(2,1)} %get-tuple-element.26), calls=%async_computation.3 | async-start | bytes 2097152 | tf_op jit(solution)/shard_map/all_to_all | solution.py:471
  129.6 7.2 %copy-start.9 = (bf16[2,2,128,512]{3,2,1,0:T(8,128)(2,1)S(1)}, bf16[2,2,128,512]{3,2,1,0:T(8,128)(2,1)}, u32[]{:S(2)}) copy-start(bf16[2,2,128,512]{3,2,1,0:T(8,128)(2,1)} %get-tuple-element.33) | copy-start | bytes 1572868
  129.6 16.3 %copy-start.1 = (bf16[8,4,128,128]{3,2,1,0:T(8,128)(2,1)}, bf16[8,4,128,128]{3,2,1,0:T(8,128)(2,1)S(1)}, u32[]{:S(2)}) copy-start(bf16[8,4,128,128]{3,2,1,0:T(8,128)(2,1)S(1)} %all-to-all-done.3.refs_0_) | copy-start | bytes 3145732
  129.6 12.7 %collective-permute-start.5 = (bf16[3,2,2,128,512]{4,3,2,1,0:T(8,128)(2,1)}, bf16[3,2,2,128,512]{4,3,2,1,0:T(8,128)(2,1)S(1)}, u32[]{:S(2)}, u32[]{:S(2)}) collective-permute-start(bf16[3,2,2,128,512]{4,3,2,1,0:T(8,128)(2,1)} %get-tuple-element.30.mine_ref), channel_id=1, source_target_pairs={{8,0},{24,16},{40,32},{56,48},{72,64},{88,80},{104,96},{120,112},{... | collective-permute-start | bytes 4718600 | tf_op jit(solution)/shard_map/ppermute | solution.py:467
  131.0 40.2 %all-to-all-start.4 = ((bf16[8,4,128,128]{3,2,1,0:T(8,128)(2,1)}), bf16[8,4,128,128]{3,2,1,0:T(8,128)(2,1)}, u32[]{:S(2)}, u32[]{:S(2)}) async-start(bf16[8,4,128,128]{3,2,1,0:T(8,128)(2,1)} %get-tuple-element.28), calls=%async_computation.4 | async-start | bytes 2097152 | tf_op jit(solution)/shard_map/all_to_all | solution.py:471
  136.8 17.2 %collective-permute-start.8 = (bf16[2,2,128,512]{3,2,1,0:T(8,128)(2,1)S(1)}, bf16[2,2,128,512]{3,2,1,0:T(8,128)(2,1)S(1)}, u32[]{:S(2)}, u32[]{:S(2)}) collective-permute-start(bf16[2,2,128,512]{3,2,1,0:T(8,128)(2,1)S(1)} %copy-done.9), channel_id=1, source_target_pairs={{0,104},{16,120},{32,8},{48,24},{64,40},{80,56},{96,72},{112,88},{... | collective-permute-start | bytes 1572872 | tf_op jit(solution)/shard_map/ppermute | solution.py:467
  142.3 1.2 copy-start
  145.9 12.4 %collective-permute-start.6 = (bf16[2,2,128,512]{3,2,1,0:T(8,128)(2,1)}, bf16[2,2,128,512]{3,2,1,0:T(8,128)(2,1)S(1)}, u32[]{:S(2)}, u32[]{:S(2)}) collective-permute-start(bf16[2,2,128,512]{3,2,1,0:T(8,128)(2,1)} %get-tuple-element.31), channel_id=1, source_target_pairs={{0,120},{16,8},{32,24},{48,40},{64,56},{80,72},{96,88},{112,104},{... | collective-permute-start | bytes 1572872 | tf_op jit(solution)/shard_map/ppermute | solution.py:467
  151.3 16.3 %collective-permute-start.7 = (bf16[2,2,128,512]{3,2,1,0:T(8,128)(2,1)}, bf16[2,2,128,512]{3,2,1,0:T(8,128)(2,1)S(1)}, u32[]{:S(2)}, u32[]{:S(2)}) collective-permute-start(bf16[2,2,128,512]{3,2,1,0:T(8,128)(2,1)} %get-tuple-element.32), channel_id=1, source_target_pairs={{0,112},{16,0},{32,16},{48,32},{64,48},{80,64},{96,80},{112,96},{1... | collective-permute-start | bytes 1572872 | tf_op jit(solution)/shard_map/ppermute | solution.py:467
  154.0 13.6 %copy-start.4 = (bf16[2,2,128,512]{3,2,1,0:T(8,128)(2,1)}, bf16[2,2,128,512]{3,2,1,0:T(8,128)(2,1)S(1)}, u32[]{:S(2)}) copy-start(bf16[2,2,128,512]{3,2,1,0:T(8,128)(2,1)S(1)} %collective-permute-done.8.refs_2_) | copy-start | bytes 1572868
  158.3 9.4 %copy-start.5 = (bf16[2,2,128,512]{3,2,1,0:T(8,128)(2,1)}, bf16[2,2,128,512]{3,2,1,0:T(8,128)(2,1)S(1)}, u32[]{:S(2)}) copy-start(bf16[2,2,128,512]{3,2,1,0:T(8,128)(2,1)S(1)} %collective-permute-done.6.refs_0_) | copy-start | bytes 1572868
  167.6 0.8 copy-start.6
  171.2 12.1 %all-to-all-start.5 = ((bf16[8,2,128,128]{3,2,1,0:T(8,128)(2,1)}), bf16[8,2,128,128]{3,2,1,0:T(8,128)(2,1)S(1)}, u32[]{:S(2)}, u32[]{:S(2)}) async-start(bf16[8,2,128,128]{3,2,1,0:T(8,128)(2,1)} %total.1), calls=%async_computation.5 | async-start | bytes 1048576 | tf_op jit(solution)/shard_map/all_to_all | solution.py:471
  183.3 0.8 copy-start.3

commit v7 on v6

--- a/solution.py
+++ b/solution.py
@@ -24,11 +24,13 @@
 F32 = jnp.float32
 BM, BN, PIPE = 256, 256, True
 BM, BN = 256, 256
+GROUP = 4
 PACK_PER = 4
 VMEM_LIMIT = 60 * 1024 * 1024
 
 NN = (((1,), (0,)), ((), ()))
 NT = (((1,), (1,)), ((), ()))
+TN = (((0,), (0,)), ((), ()))
 
 
 def dot(a, b, dims=NN):
@@ -62,7 +64,9 @@
 def pack_q_kernel(per, q_ref, do_ref, o_ref, ln_ref, doc_ref, *refs):
     *qd_refs, pick_ref = refs
     step = pl.program_id(0)
-    heads = ln_ref.shape[1]
+    group, member = lax.axis_index("blk"), lax.axis_index("uly")
+    groups = lax.axis_size("blk")
+    heads = ln_ref.shape[0]
     width = HEADS_DEV * HD
 
     @pl.when(step == 0)
@@ -75,6 +79,16 @@
     head = lax.broadcasted_iota(jnp.int32, (heads, 128), 0)
     col = lax.broadcasted_iota(jnp.int32, (heads, 128), 1)
     lane = lax.broadcasted_iota(jnp.int32, (TOK, 128), 1)
+    quarters = HALF // TOK
+    low = group * quarters + member
+    high = (2 * groups - 1 - group) * quarters + member - quarters
+    spot = jnp.where(member < quarters, low, high)
+    docs = doc_ref[pl.ds(spot, 1), :].astype(F32)
+    row = lax.broadcasted_iota(jnp.int32, (TOK, 128), 0)
+    docs = jnp.where(row == lane, jnp.broadcast_to(docs, (TOK, 128)), 0.0).astype(BF)
+    docs = dot(docs, jnp.ones((128, 128), BF))
+    other = (lane < 48 + DOCS) & (docs != (lane - 48).astype(F32))
+    doc_block = jnp.where(other, FAR, 0.0).astype(BF)
     norm_parts = parts_of(ln_ref[...] * NORM_SCALE)
     for i in range(per):
         first = i * width
@@ -82,13 +96,13 @@
         for j, part in enumerate(norm_parts):
             mine = head == (step * per + i) * HEADS_DEV + col % HEADS_DEV
             pick = (col // HEADS_DEV == j) & mine
-            norm += dot(part, jnp.where(pick, 1.0, 0.0).astype(BF))
+            norm += dot(part, jnp.where(pick, 1.0, 0.0).astype(BF), TN)
         cols = slice(first, first + width)
         high, low, _ = parts_of(do_ref[:, cols].astype(F32) * o_ref[:, cols].astype(F32))
         delta = dot(high, pick_ref[...]) + dot(low, pick_ref[...])
         high, mid, low = parts_of(delta)
         delta = jnp.where(lane < 32, high, jnp.where(lane < 40, mid, low))
-        stats = jnp.where(lane < 24, norm.astype(BF), jnp.where(lane < 48, delta, doc_ref[...]))
+        stats = jnp.where(lane < 24, norm.astype(BF), jnp.where(lane < 48, delta, doc_block))
         h = 0
         for index, ref in enumerate(qd_refs):
             count = ref.shape[1] // 2
@@ -138,7 +152,7 @@
     (dkv_in,) = take(1) if has_dkv else (None,)
     (dq_ref,) = take(1)
     dkv_out = take(3 if last else 1)
-    qt_ref, dot_ref, sel_ref, kv_ref, p_ref, ds_ref, dqt_ref = take(7)
+    qt_ref, dot_ref, sel_ref, kv_ref, p_ref, ds_ref, dqt_ref, dst_ref = take(8)
     qd_ref, stat_ref, raw_ref, sum_ref, sems = take(5)
     (others_ref,) = take(1) if last else (None,)
 
@@ -254,35 +268,38 @@
             ki = lax.broadcasted_iota(jnp.int32, (bm, bn), 1) + k0
             prob = jnp.where(qi >= ki, prob, 0.0)
         rows = slice(q0, q0 + bm)
-        ds_ref[slot, rows, kcols] = (prob * dot(do_ext, v_ext)).astype(BF)
+        dscore = (prob * dot(do_ext, v_ext)).astype(BF)
+        ds_ref[slot, rows, kcols] = dscore
+        dst_ref[slot, kcols, rows] = dscore.T
         p_ref[slot, rows, kcols] = prob.astype(BF)
 
-    def grads(index, qhalf, khalf, h, slot, diagonal):
+    def grads(index, qhalf, khalf, heads, diagonal):
         for k0, kn, q0 in ((0, 256, 0), (256, 256, 256)) if diagonal else ((0, HALF, 0),):
             span = slice(q0, HALF)
             cols = slice(k0, k0 + kn)
-            sum_ref[index, 1, khalf, :, cols] += dot(dot_ref[qhalf, h, :, span], p_ref[slot, span, cols])
-            sum_ref[index, 0, khalf, :, cols] += dot(qt_ref[qhalf, h, :, span], ds_ref[slot, span, cols])
+            for pair, left_ref, right_ref in ((1, dot_ref, p_ref), (0, qt_ref, ds_ref)):
+                left = jnp.concatenate([left_ref[qhalf, h, :, span] for h in heads], axis=1)
+                right = jnp.concatenate([right_ref[h, span, cols] for h in heads], axis=0)
+                sum_ref[index, pair, khalf, :, cols] += dot(left, right)
         for q0, qn, kn in ((0, 256, 256), (256, 256, 512)) if diagonal else ((0, HALF, HALF),):
             span = slice(q0, q0 + qn)
-            dqt_ref[qhalf, h, :, span] += dot(kv_ref[index, 0, khalf, :, :kn], ds_ref[slot, span, :kn], NT)
+            for h in heads:
+                dqt_ref[qhalf, h, :, span] += dot(
+                    kv_ref[index, 0, khalf, :, :kn], dst_ref[h, :kn, span]
+                )
 
     def tile(index, qhalf, khalf, diagonal):
-        for h in range(count):
-            for k0 in range(0, HALF, BN):
-                for q0 in range(0, HALF, BM):
-                    if diagonal and q0 + BM <= k0:
-                        if q0 >= k0 // 256 * 256:
-                            ds_ref[h % 2, q0 : q0 + BM, k0 : k0 + BN] = jnp.zeros((BM, BN), BF)
-                            p_ref[h % 2, q0 : q0 + BM, k0 : k0 + BN] = jnp.zeros((BM, BN), BF)
-                        continue
-                    scores(index, qhalf, khalf, h, h % 2, q0, k0, BM, BN, diagonal and q0 < k0 + BN)
-            if PIPE and h > 0:
-                grads(index, qhalf, khalf, h - 1, (h - 1) % 2, diagonal)
-            if not PIPE:
-                grads(index, qhalf, khalf, h, h % 2, diagonal)
-        if PIPE:
-            grads(index, qhalf, khalf, count - 1, (count - 1) % 2, diagonal)
+        groups = [range(h, min(h + GROUP, count)) for h in range(0, count, GROUP)]
+        for turn, heads in enumerate(groups):
+            for h in heads:
+                for k0 in range(0, HALF, BN):
+                    for q0 in range(0, HALF, BM):
+                        if diagonal and q0 + BM <= k0:
+                            continue
+                        scores(index, qhalf, khalf, h, h, q0, k0, BM, BN, diagonal and q0 < k0 + BN)
+            if turn:
+                grads(index, qhalf, khalf, groups[turn - 1], diagonal)
+        grads(index, qhalf, khalf, groups[-1], diagonal)
 
     stat_copy.wait()
     begin(0)
@@ -354,9 +371,10 @@
             pltpu.VMEM((2, count, HD, HALF), BF),
             pltpu.VMEM((2 * count, 48, HALF), BF),
             pltpu.VMEM(sums, BF),
-            pltpu.VMEM((2, HALF, HALF), BF),
-            pltpu.VMEM((2, HALF, HALF), BF),
+            pltpu.VMEM((count, HALF, HALF), BF),
+            pltpu.VMEM((count, HALF, HALF), BF),
             pltpu.VMEM((2, count, HD, HALF), F32),
+            pltpu.VMEM((count, HALF, HALF), BF),
             pltpu.VMEM((8, 2 * count, TOK, HD), BF),
             pltpu.VMEM((8, TOK, HD), BF),
             pltpu.VMEM((sum(len(sources) for sources in kvs), 8, 2, HD, TOK), BF),
@@ -447,17 +465,27 @@
     )(*parts)
 
 
-def unpack_kv_kernel(pair_ref, k_ref, v_ref):
+def unpack_kv_kernel(pair_ref, k_ref, v_ref, sems):
+    copies = []
     for u in range(8):
-        k_ref[:, u * HD : (u + 1) * HD] = pair_ref[u, 0]
-        v_ref[:, u * HD : (u + 1) * HD] = pair_ref[u, 1]
+        for i, ref in enumerate((k_ref, v_ref)):
+            target = ref.at[:, u * HD : (u + 1) * HD]
+            copies.append(pltpu.make_async_copy(pair_ref.at[u, i], target, sems.at[u, i]))
+    for copy in copies:
+        copy.start()
+    for copy in copies:
+        copy.wait()
 
 
 def unpack_kv(pair):
     shape = jax.ShapeDtypeStruct((TOK, 8 * HD), BF)
+    anywhere = pl.BlockSpec(memory_space=pl.ANY)
     return pl.pallas_call(
         unpack_kv_kernel,
+        in_specs=[anywhere],
+        out_specs=[anywhere, anywhere],
         out_shape=[shape, shape],
+        scratch_shapes=[pltpu.SemaphoreType.DMA((8, 2))],
         compiler_params=pltpu.CompilerParams(vmem_limit_bytes=VMEM_LIMIT),
         name="unpack_kv",
     )(pair)
@@ -474,17 +502,6 @@
 def local(queries, key_rows, value_rows, grad_out, attn_out, log_norm, doc_ids):
     groups = lax.axis_size("blk")
     group = lax.axis_index("blk")
-    member = lax.axis_index("uly")
-
-    first = jnp.where(
-        member < 4, group * HALF + member * TOK, (2 * groups - 1 - group) * HALF + (member - 4) * TOK
-    )
-    my_docs = lax.dynamic_slice_in_dim(doc_ids, first, TOK)
-    lane = jnp.arange(128, dtype=jnp.int32)[None, :]
-    doc_block = jnp.where(
-        (lane >= 48) & (lane < 48 + DOCS) & (my_docs[:, None] != lane - 48), FAR, 0.0
-    ).astype(BF)
-
     kdocs = []
     for step in range(STEPS):
         owner = (group - step) % groups
@@ -509,7 +526,7 @@
     two_inner, three_inner = (move(part, inner_up) for part in (one, two))
     kvs = [[kv], [one], [two, two_inner], [three, three_inner]]
 
-    packed = pack_q(queries, grad_out, attn_out, log_norm, doc_block)
+    packed = pack_q(queries, grad_out, attn_out, log_norm.T, doc_ids.reshape(-1, TOK))
     early = exchange(packed[0])
     late, *_ = lax.optimization_barrier((packed[1], early))
     late = exchange(late)

time: 187 us -> 196 us (1.048)
  Pallas kernels: 70.4 us -> 79.1 us
  waiting for transfers between devices: 50.4 us -> 54.2 us
    pallas_call x1, Pallas kernels: 1.97 us -> 17.1 us  [unpack_kv(): pl.pallas_call(unpack_kv_kernel, in_specs=[anywhere], out_specs=[anywhere...]
    pallas_call x2, Pallas kernels: 52.7 us -> 46.3 us  [attend(): pl.pallas_call(kernel, in_specs=[pl.BlockSpec(memory_space=pltpu.SMEM), *...]
    all_to_all x6, waiting for transfers between devices: 8.01 us -> 11.8 us  [exchange(): return lax.all_to_all(value, 'uly', split_axis=0, concat_axis=0, tiled=True)]
    unnamed x21 -> x18, local copies, waits for them, and re-layouts: 4.97 us -> 4.23 us
  transfers between devices with their start and end apart: 15 -> 15, of which waited for: 5 -> 6; matrix products, arithmetic and copies ran while one was open for 2% -> 1% of each run, Pallas kernels for 36% -> 31%
where the time goes in v7:
time: 196 us; the launch traced here: 195 us
  Pallas kernels  79.1 us (40%)
  starting transfers between devices  54.2 us (28%)
  waiting for transfers between devices  54.2 us (28%)
  local copies, waits for them, and re-layouts  5.13 us (3%)
    pallas_call x2, Pallas kernels, attend(): pl.pallas_call(kernel, in_specs=[pl.BlockSpec(memory_space=pltpu.SMEM), *...  46.3 us
    ppermute x9, waiting for transfers between devices, move(): return lax.ppermute(value, 'blk', pairs)  42.3 us
    all_to_all x6, starting transfers between devices, exchange(): return lax.all_to_all(value, 'uly', split_axis=0, concat_axis=0, tiled=True)  28.1 us
    ppermute x9, starting transfers between devices, move(): return lax.ppermute(value, 'blk', pairs)  26.1 us
    pallas_call x1, Pallas kernels, unpack_kv(): pl.pallas_call(unpack_kv_kernel, in_specs=[anywhere], out_specs=[anywhere...  17.1 us
    all_to_all x6, waiting for transfers between devices, exchange(): return lax.all_to_all(value, 'uly', split_axis=0, concat_axis=0, tiled=True)  11.8 us
    pallas_call x1, Pallas kernels, pack_q(): pl.pallas_call(functools.partial(pack_q_kernel, per), grid=(8 // per,), i...  5.78 us
    unnamed x18, local copies, waits for them, and re-layouts  4.23 us
  transfers between devices with their start and end apart: 15, of which 6 were waited for; matrix products, arithmetic and copies ran while one was open for 1% of the time, Pallas kernels for 31%

profile of v7, /device:TPU:0, one launch (start us, length us, event | category | flops | bytes accessed | tf_op | source)
XLA Modules:
  0.0 194.9 jit_solution(13753249535532138951)
XLA Ops:
  0.6 2.0 %pack_kv.1 = bf16[8,2,128,128]{3,2,1,0:T(8,128)(2,1)} custom-call(bf16[128,1024]{1,0:T(8,128)(2,1)} %k_ref.1, bf16[128,1024]{1,0:T(8,128)(2,1)} %v_ref.1), custom_call_target="tpu_custom_call" | custom-call | bytes 1048576 | tf_op jit(solution)/shard_map/pack_kv/pallas_call | solution.py:55
  2.6 5.7 %all-to-all-start.2 = ((bf16[8,2,128,128]{3,2,1,0:T(8,128)(2,1)}), bf16[8,2,128,128]{3,2,1,0:T(8,128)(2,1)S(1)}, u32[]{:S(2)}, u32[]{:S(2)}) async-start(bf16[8,2,128,128]{3,2,1,0:T(8,128)(2,1)} %pack_kv.1), calls=%async_computation.2 | async-start | bytes 1048576 | tf_op jit(solution)/shard_map/all_to_all | solution.py:499
  8.4 5.8 %pack_q.1 = (bf16[8,9,128,128]{3,2,1,0:T(8,128)(2,1)}, bf16[8,8,128,128]{3,2,1,0:T(8,128)(2,1)}) custom-call(bf16[128,8192]{1,0:T(8,128)(2,1)} %q_ref.1, bf16[128,8192]{1,0:T(8,128)(2,1)} %do_ref.1, bf16[128,8192]{1,0:T(8,128)(2,1)} %o_ref.1, f32[64,128]{1,0:T(8,128)} %bitcast.19, s32[128,128]{1,0:T(8,128)} %bitcast.18), custom_call_target="tpu_custom_call" | custom-call | bytes 11534336 | tf_op jit(solution)/shard_map/pack_q/pallas_call | solution.py:122
  14.2 4.3 %all-to-all-done.2.refs_3_ = bf16[8,2,128,128]{3,2,1,0:T(8,128)(2,1)S(1)} async-done(((bf16[8,2,128,128]{3,2,1,0:T(8,128)(2,1)}), bf16[8,2,128,128]{3,2,1,0:T(8,128)(2,1)S(1)}, u32[]{:S(2)}, u32[]{:S(2)}) %all-to-all-start.2) | async-done | bytes 524320 | tf_op jit(solution)/shard_map/all_to_all | solution.py:499
  18.5 3.6 %all-to-all-start = ((bf16[8,9,128,128]{3,2,1,0:T(8,128)(2,1)}), bf16[8,9,128,128]{3,2,1,0:T(8,128)(2,1)S(1)}, u32[]{:S(2)}, u32[]{:S(2)}) async-start(bf16[8,9,128,128]{3,2,1,0:T(8,128)(2,1)} %get-tuple-element.21), calls=%async_computation | async-start | bytes 4718592 | tf_op jit(solution)/shard_map/all_to_all | solution.py:499
  22.1 5.5 %collective-permute-start.1 = (bf16[8,2,128,128]{3,2,1,0:T(8,128)(2,1)S(1)}, bf16[8,2,128,128]{3,2,1,0:T(8,128)(2,1)}, u32[]{:S(2)}, u32[]{:S(2)}) collective-permute-start(bf16[8,2,128,128]{3,2,1,0:T(8,128)(2,1)S(1)} %all-to-all-done.2.refs_3_), channel_id=1, source_target_pairs={{112,0},{0,16},{16,32},{32,48},{48,64},{64,80},{80,96},{96,112},{1... | collective-permute-start | bytes 1572872 | tf_op jit(solution)/shard_map/ppermute | solution.py:495
  27.8 0.9 fusion
  28.7 1.3 collective-permute-start.3
  30.0 28.7 %collective-permute-done.1.refs_5_ = bf16[8,2,128,128]{3,2,1,0:T(8,128)(2,1)} collective-permute-done((bf16[8,2,128,128]{3,2,1,0:T(8,128)(2,1)S(1)}, bf16[8,2,128,128]{3,2,1,0:T(8,128)(2,1)}, u32[]{:S(2)}, u32[]{:S(2)}) %collective-permute-start.1) | collective-permute-done | bytes 524320 | tf_op jit(solution)/shard_map/ppermute | solution.py:495
  58.7 2.1 %collective-permute-start.4 = (bf16[8,2,128,128]{3,2,1,0:T(8,128)(2,1)}, bf16[8,2,128,128]{3,2,1,0:T(8,128)(2,1)}, u32[]{:S(2)}, u32[]{:S(2)}) collective-permute-start(bf16[8,2,128,128]{3,2,1,0:T(8,128)(2,1)} %collective-permute-done.1.refs_5_), channel_id=1, source_target_pairs={{0,8},{16,24},{32,40},{48,56},{64,72},{80,88},{96,104},{112,120},{... | collective-permute-start | bytes 1572872 | tf_op jit(solution)/shard_map/ppermute | solution.py:495
  60.8 2.1 %collective-permute-start.2 = (bf16[8,2,128,128]{3,2,1,0:T(8,128)(2,1)}, bf16[8,2,128,128]{3,2,1,0:T(8,128)(2,1)}, u32[]{:S(2)}, u32[]{:S(2)}) collective-permute-start(bf16[8,2,128,128]{3,2,1,0:T(8,128)(2,1)} %collective-permute-done.refs_4_), channel_id=1, source_target_pairs={{0,8},{16,24},{32,40},{48,56},{64,72},{80,88},{96,104},{112,120},{... | collective-permute-start | bytes 1572872 | tf_op jit(solution)/shard_map/ppermute | solution.py:495
  64.1 1.4 copy-done.2
  65.6 5.5 %all-to-all-start.1 = ((bf16[8,8,128,128]{3,2,1,0:T(8,128)(2,1)}), bf16[8,8,128,128]{3,2,1,0:T(8,128)(2,1)}, u32[]{:S(2)}, u32[]{:S(2)}) async-start(bf16[8,8,128,128]{3,2,1,0:T(8,128)(2,1)} %get-tuple-element.22), calls=%async_computation.1 | async-start | bytes 4194304 | tf_op jit(solution)/shard_map/all_to_all | solution.py:499
  71.1 22.6 %attend.2 = (bf16[8,4,128,128]{3,2,1,0:T(8,128)(2,1)}, f32[4,2,2,128,512]{4,3,2,1,0:T(8,128)}) custom-call(s32[4]{0:T(128)} %compare_select_fusion.refs_0_, bf16[8,9,128,128]{3,2,1,0:T(8,128)(2,1)} %copy-done.2, bf16[8,9,128,128]{3,2,1,0:T(8,128)(2,1)} %copy-done.2, bf16[8,2,128,128]{3,2,1,0:T(8,128)(2,1)} %copy-done.7, ...), custom_call_target="tpu_custom_call" | custom-call | flops 22817013760 | bytes 8388608 | tf_op jit(solution)/shard_map/attend/pallas_call | solution.py:359
  93.7 1.7 all-to-all-done.1.refs_1_
  95.4 4.0 %all-to-all-start.3 = ((bf16[8,4,128,128]{3,2,1,0:T(8,128)(2,1)}), bf16[8,4,128,128]{3,2,1,0:T(8,128)(2,1)S(1)}, u32[]{:S(2)}, u32[]{:S(2)}) async-start(bf16[8,4,128,128]{3,2,1,0:T(8,128)(2,1)} %get-tuple-element.26), calls=%async_computation.3 | async-start | bytes 2097152 | tf_op jit(solution)/shard_map/all_to_all | solution.py:499
  99.4 23.7 %attend.3 = (bf16[8,4,128,128]{3,2,1,0:T(8,128)(2,1)}, f32[2,2,128,512]{3,2,1,0:T(8,128)}, bf16[3,2,2,128,512]{4,3,2,1,0:T(8,128)(2,1)}, bf16[2,2,128,512]{3,2,1,0:T(8,128)(2,1)}) custom-call(s32[4]{0:T(128)} %compare_select_fusion.refs_0_, bf16[8,8,128,128]{3,2,1,0:T(8,128)(2,1)} %all-to-all-done.1.refs_1_, bf16[8,9,128,128]{3,2,1,0:T(8,128)(2,1)} %copy-done.2, ...), custom_call_target="tpu_custom_call" | custom-call | flops 22817013760 | bytes 8388608 | tf_op jit(solution)/shard_map/attend/pallas_call | solution.py:359
  123.2 1.4 collective-permute-start.5
  124.6 5.7 %all-to-all-start.4 = ((bf16[8,4,128,128]{3,2,1,0:T(8,128)(2,1)}), bf16[8,4,128,128]{3,2,1,0:T(8,128)(2,1)}, u32[]{:S(2)}, u32[]{:S(2)}) async-start(bf16[8,4,128,128]{3,2,1,0:T(8,128)(2,1)} %get-tuple-element.28), calls=%async_computation.4 | async-start | bytes 2097152 | tf_op jit(solution)/shard_map/all_to_all | solution.py:499
  130.3 5.5 %collective-permute-start.8 = (bf16[2,2,128,512]{3,2,1,0:T(8,128)(2,1)S(1)}, bf16[2,2,128,512]{3,2,1,0:T(8,128)(2,1)S(1)}, u32[]{:S(2)}, u32[]{:S(2)}) collective-permute-start(bf16[2,2,128,512]{3,2,1,0:T(8,128)(2,1)S(1)} %copy-done.8), channel_id=1, source_target_pairs={{0,104},{16,120},{32,8},{48,24},{64,40},{80,56},{96,72},{112,88},{... | collective-permute-start | bytes 1572872 | tf_op jit(solution)/shard_map/ppermute | solution.py:495
  135.9 1.2 copy-done
  137.0 2.4 %join.1 = (bf16[2,2,128,512]{3,2,1,0:T(8,128)(2,1)}, bf16[2,2,128,512]{3,2,1,0:T(8,128)(2,1)}) custom-call(bf16[3,2,2,128,512]{4,3,2,1,0:T(8,128)(2,1)} %get-tuple-element.30.mine_ref, bf16[3,2,2,128,512]{4,3,2,1,0:T(8,128)(2,1)} %copy-done, bf16[3,2,2,128,512]{4,3,2,1,0:T(8,128)(2,1)} %copy-done), custom_call_target="tpu_custom_call" | custom-call | bytes 3145728 | tf_op jit(solution)/shard_map/join/pallas_call | solution.py:404
  139.4 5.4 %collective-permute-start.6 = (bf16[2,2,128,512]{3,2,1,0:T(8,128)(2,1)}, bf16[2,2,128,512]{3,2,1,0:T(8,128)(2,1)S(1)}, u32[]{:S(2)}, u32[]{:S(2)}) collective-permute-start(bf16[2,2,128,512]{3,2,1,0:T(8,128)(2,1)} %get-tuple-element.31), channel_id=1, source_target_pairs={{0,120},{16,8},{32,24},{48,40},{64,56},{80,72},{96,88},{112,104},{... | collective-permute-start | bytes 1572872 | tf_op jit(solution)/shard_map/ppermute | solution.py:495
  144.8 2.7 %collective-permute-start.7 = (bf16[2,2,128,512]{3,2,1,0:T(8,128)(2,1)}, bf16[2,2,128,512]{3,2,1,0:T(8,128)(2,1)S(1)}, u32[]{:S(2)}, u32[]{:S(2)}) collective-permute-start(bf16[2,2,128,512]{3,2,1,0:T(8,128)(2,1)} %get-tuple-element.32), channel_id=1, source_target_pairs={{0,112},{16,0},{32,16},{48,32},{64,48},{80,64},{96,80},{112,96},{1... | collective-permute-start | bytes 1572872 | tf_op jit(solution)/shard_map/ppermute | solution.py:495
  147.6 4.3 %collective-permute-done.6.refs_0_ = bf16[2,2,128,512]{3,2,1,0:T(8,128)(2,1)S(1)} collective-permute-done((bf16[2,2,128,512]{3,2,1,0:T(8,128)(2,1)}, bf16[2,2,128,512]{3,2,1,0:T(8,128)(2,1)S(1)}, u32[]{:S(2)}, u32[]{:S(2)}) %collective-permute-start.6) | collective-permute-done | bytes 524320 | tf_op jit(solution)/shard_map/ppermute | solution.py:495
  151.8 9.4 %collective-permute-done.7.refs_1_ = bf16[2,2,128,512]{3,2,1,0:T(8,128)(2,1)S(1)} collective-permute-done((bf16[2,2,128,512]{3,2,1,0:T(8,128)(2,1)}, bf16[2,2,128,512]{3,2,1,0:T(8,128)(2,1)S(1)}, u32[]{:S(2)}, u32[]{:S(2)}) %collective-permute-start.7) | collective-permute-done | bytes 524320 | tf_op jit(solution)/shard_map/ppermute | solution.py:495
  161.2 0.8 copy-done.6
  162.0 2.7 %total.1 = bf16[8,2,128,128]{3,2,1,0:T(8,128)(2,1)} custom-call(f32[2,2,128,512]{3,2,1,0:T(8,128)} %get-tuple-element.29.own_ref, bf16[3,2,2,128,512]{4,3,2,1,0:T(8,128)(2,1)} %copy-done, bf16[2,2,128,512]{3,2,1,0:T(8,128)(2,1)} %copy-done.5, bf16[2,2,128,512]{3,2,1,0:T(8,128)(2,1)} %copy-done.6, bf16[2,2,128,512]{3,2,1,0:T(8,128)(2,1)} %copy-done.4), custom_call_target="tpu_custom_call" | custom-call | bytes 4194304 | tf_op jit(solution)/shard_map/total/pallas_call | solution.py:428
  164.7 3.5 %all-to-all-start.5 = ((bf16[8,2,128,128]{3,2,1,0:T(8,128)(2,1)}), bf16[8,2,128,128]{3,2,1,0:T(8,128)(2,1)S(1)}, u32[]{:S(2)}, u32[]{:S(2)}) async-start(bf16[8,2,128,128]{3,2,1,0:T(8,128)(2,1)} %total.1), calls=%async_computation.5 | async-start | bytes 1048576 | tf_op jit(solution)/shard_map/all_to_all | solution.py:499
  168.2 2.8 %unpack_q.1 = bf16[128,8192]{1,0:T(8,128)(2,1)} custom-call(bf16[8,4,128,128]{3,2,1,0:T(8,128)(2,1)} %copy-done.1, bf16[8,4,128,128]{3,2,1,0:T(8,128)(2,1)} %all-to-all-done.4.refs_1_), custom_call_target="tpu_custom_call" | custom-call | bytes 4194304 | tf_op jit(solution)/shard_map/unpack_q/pallas_call | solution.py:456
  171.0 5.8 %all-to-all-done.5.pair_ref = bf16[8,2,128,128]{3,2,1,0:T(8,128)(2,1)S(1)} async-done(((bf16[8,2,128,128]{3,2,1,0:T(8,128)(2,1)}), bf16[8,2,128,128]{3,2,1,0:T(8,128)(2,1)S(1)}, u32[]{:S(2)}, u32[]{:S(2)}) %all-to-all-start.5) | async-done | bytes 524320 | tf_op jit(solution)/shard_map/all_to_all | solution.py:499
  177.6 17.1 %unpack_kv.1 = (bf16[128,1024]{1,0:T(8,128)(2,1)}, bf16[128,1024]{1,0:T(8,128)(2,1)}) custom-call(bf16[8,2,128,128]{3,2,1,0:T(8,128)(2,1)} %copy-done.3), custom_call_target="tpu_custom_call" | custom-call | tf_op jit(solution)/shard_map/unpack_kv/pallas_call | solution.py:483
  (30 shorter events, 2.1 us)
Async XLA Ops:
  2.6 15.8 %all-to-all-start.2 = ((bf16[8,2,128,128]{3,2,1,0:T(8,128)(2,1)}), bf16[8,2,128,128]{3,2,1,0:T(8,128)(2,1)S(1)}, u32[]{:S(2)}, u32[]{:S(2)}) async-start(bf16[8,2,128,128]{3,2,1,0:T(8,128)(2,1)} %pack_kv.1), calls=%async_computation.2 | async-start | bytes 1048576 | tf_op jit(solution)/shard_map/all_to_all | solution.py:499
  18.5 10.2 %copy-start.7 = (bf16[8,2,128,128]{3,2,1,0:T(8,128)(2,1)}, bf16[8,2,128,128]{3,2,1,0:T(8,128)(2,1)S(1)}, u32[]{:S(2)}) copy-start(bf16[8,2,128,128]{3,2,1,0:T(8,128)(2,1)S(1)} %all-to-all-done.2.refs_3_) | copy-start | bytes 1572868
  18.5 45.7 %all-to-all-start = ((bf16[8,9,128,128]{3,2,1,0:T(8,128)(2,1)}), bf16[8,9,128,128]{3,2,1,0:T(8,128)(2,1)S(1)}, u32[]{:S(2)}, u32[]{:S(2)}) async-start(bf16[8,9,128,128]{3,2,1,0:T(8,128)(2,1)} %get-tuple-element.21), calls=%async_computation | async-start | bytes 4718592 | tf_op jit(solution)/shard_map/all_to_all | solution.py:499
  22.1 36.6 %collective-permute-start.1 = (bf16[8,2,128,128]{3,2,1,0:T(8,128)(2,1)S(1)}, bf16[8,2,128,128]{3,2,1,0:T(8,128)(2,1)}, u32[]{:S(2)}, u32[]{:S(2)}) collective-permute-start(bf16[8,2,128,128]{3,2,1,0:T(8,128)(2,1)S(1)} %all-to-all-done.2.refs_3_), channel_id=1, source_target_pairs={{112,0},{0,16},{16,32},{32,48},{48,64},{64,80},{80,96},{96,112},{1... | collective-permute-start | bytes 1572872 | tf_op jit(solution)/shard_map/ppermute | solution.py:495
  27.6 33.2 %collective-permute-start = (bf16[8,2,128,128]{3,2,1,0:T(8,128)(2,1)S(1)}, bf16[8,2,128,128]{3,2,1,0:T(8,128)(2,1)}, u32[]{:S(2)}, u32[]{:S(2)}) collective-permute-start(bf16[8,2,128,128]{3,2,1,0:T(8,128)(2,1)S(1)} %all-to-all-done.2.refs_3_), channel_id=1, source_target_pairs={{0,8},{8,16},{16,24},{24,32},{32,40},{40,48},{48,56},{56,64},{64,7... | collective-permute-start | bytes 1572872 | tf_op jit(solution)/shard_map/ppermute | solution.py:495
  28.7 42.4 %collective-permute-start.3 = (bf16[8,2,128,128]{3,2,1,0:T(8,128)(2,1)S(1)}, bf16[8,2,128,128]{3,2,1,0:T(8,128)(2,1)}, u32[]{:S(2)}, u32[]{:S(2)}) collective-permute-start(bf16[8,2,128,128]{3,2,1,0:T(8,128)(2,1)S(1)} %all-to-all-done.2.refs_3_), channel_id=1, source_target_pairs={{104,0},{120,16},{8,32},{24,48},{40,64},{56,80},{72,96},{88,112},{... | collective-permute-start | bytes 1572872 | tf_op jit(solution)/shard_map/ppermute | solution.py:495
  58.7 12.4 %collective-permute-start.4 = (bf16[8,2,128,128]{3,2,1,0:T(8,128)(2,1)}, bf16[8,2,128,128]{3,2,1,0:T(8,128)(2,1)}, u32[]{:S(2)}, u32[]{:S(2)}) collective-permute-start(bf16[8,2,128,128]{3,2,1,0:T(8,128)(2,1)} %collective-permute-done.1.refs_5_), channel_id=1, source_target_pairs={{0,8},{16,24},{32,40},{48,56},{64,72},{80,88},{96,104},{112,120},{... | collective-permute-start | bytes 1572872 | tf_op jit(solution)/shard_map/ppermute | solution.py:495
  60.8 10.3 %collective-permute-start.2 = (bf16[8,2,128,128]{3,2,1,0:T(8,128)(2,1)}, bf16[8,2,128,128]{3,2,1,0:T(8,128)(2,1)}, u32[]{:S(2)}, u32[]{:S(2)}) collective-permute-start(bf16[8,2,128,128]{3,2,1,0:T(8,128)(2,1)} %collective-permute-done.refs_4_), channel_id=1, source_target_pairs={{0,8},{16,24},{32,40},{48,56},{64,72},{80,88},{96,104},{112,120},{... | collective-permute-start | bytes 1572872 | tf_op jit(solution)/shard_map/ppermute | solution.py:495
  64.1 1.4 copy-start.2
  65.6 29.8 %all-to-all-start.1 = ((bf16[8,8,128,128]{3,2,1,0:T(8,128)(2,1)}), bf16[8,8,128,128]{3,2,1,0:T(8,128)(2,1)}, u32[]{:S(2)}, u32[]{:S(2)}) async-start(bf16[8,8,128,128]{3,2,1,0:T(8,128)(2,1)} %get-tuple-element.22), calls=%async_computation.1 | async-start | bytes 4194304 | tf_op jit(solution)/shard_map/all_to_all | solution.py:499
  95.4 27.8 %all-to-all-start.3 = ((bf16[8,4,128,128]{3,2,1,0:T(8,128)(2,1)}), bf16[8,4,128,128]{3,2,1,0:T(8,128)(2,1)S(1)}, u32[]{:S(2)}, u32[]{:S(2)}) async-start(bf16[8,4,128,128]{3,2,1,0:T(8,128)(2,1)} %get-tuple-element.26), calls=%async_computation.3 | async-start | bytes 2097152 | tf_op jit(solution)/shard_map/all_to_all | solution.py:499
  123.1 7.2 %copy-start.8 = (bf16[2,2,128,512]{3,2,1,0:T(8,128)(2,1)S(1)}, bf16[2,2,128,512]{3,2,1,0:T(8,128)(2,1)}, u32[]{:S(2)}) copy-start(bf16[2,2,128,512]{3,2,1,0:T(8,128)(2,1)} %get-tuple-element.33) | copy-start | bytes 1572868
  123.2 16.3 %copy-start.1 = (bf16[8,4,128,128]{3,2,1,0:T(8,128)(2,1)}, bf16[8,4,128,128]{3,2,1,0:T(8,128)(2,1)S(1)}, u32[]{:S(2)}) copy-start(bf16[8,4,128,128]{3,2,1,0:T(8,128)(2,1)S(1)} %all-to-all-done.3.refs_0_) | copy-start | bytes 3145732
  123.2 12.7 %collective-permute-start.5 = (bf16[3,2,2,128,512]{4,3,2,1,0:T(8,128)(2,1)}, bf16[3,2,2,128,512]{4,3,2,1,0:T(8,128)(2,1)S(1)}, u32[]{:S(2)}, u32[]{:S(2)}) collective-permute-start(bf16[3,2,2,128,512]{4,3,2,1,0:T(8,128)(2,1)} %get-tuple-element.30.mine_ref), channel_id=1, source_target_pairs={{8,0},{24,16},{40,32},{56,48},{72,64},{88,80},{104,96},{120,112},{... | collective-permute-start | bytes 4718600 | tf_op jit(solution)/shard_map/ppermute | solution.py:495
  124.6 40.1 %all-to-all-start.4 = ((bf16[8,4,128,128]{3,2,1,0:T(8,128)(2,1)}), bf16[8,4,128,128]{3,2,1,0:T(8,128)(2,1)}, u32[]{:S(2)}, u32[]{:S(2)}) async-start(bf16[8,4,128,128]{3,2,1,0:T(8,128)(2,1)} %get-tuple-element.28), calls=%async_computation.4 | async-start | bytes 2097152 | tf_op jit(solution)/shard_map/all_to_all | solution.py:499
  130.3 17.2 %collective-permute-start.8 = (bf16[2,2,128,512]{3,2,1,0:T(8,128)(2,1)S(1)}, bf16[2,2,128,512]{3,2,1,0:T(8,128)(2,1)S(1)}, u32[]{:S(2)}, u32[]{:S(2)}) collective-permute-start(bf16[2,2,128,512]{3,2,1,0:T(8,128)(2,1)S(1)} %copy-done.8), channel_id=1, source_target_pairs={{0,104},{16,120},{32,8},{48,24},{64,40},{80,56},{96,72},{112,88},{... | collective-permute-start | bytes 1572872 | tf_op jit(solution)/shard_map/ppermute | solution.py:495
  135.8 1.2 copy-start
  139.4 12.4 %collective-permute-start.6 = (bf16[2,2,128,512]{3,2,1,0:T(8,128)(2,1)}, bf16[2,2,128,512]{3,2,1,0:T(8,128)(2,1)S(1)}, u32[]{:S(2)}, u32[]{:S(2)}) collective-permute-start(bf16[2,2,128,512]{3,2,1,0:T(8,128)(2,1)} %get-tuple-element.31), channel_id=1, source_target_pairs={{0,120},{16,8},{32,24},{48,40},{64,56},{80,72},{96,88},{112,104},{... | collective-permute-start | bytes 1572872 | tf_op jit(solution)/shard_map/ppermute | solution.py:495
  144.8 16.3 %collective-permute-start.7 = (bf16[2,2,128,512]{3,2,1,0:T(8,128)(2,1)}, bf16[2,2,128,512]{3,2,1,0:T(8,128)(2,1)S(1)}, u32[]{:S(2)}, u32[]{:S(2)}) collective-permute-start(bf16[2,2,128,512]{3,2,1,0:T(8,128)(2,1)} %get-tuple-element.32), channel_id=1, source_target_pairs={{0,112},{16,0},{32,16},{48,32},{64,48},{80,64},{96,80},{112,96},{1... | collective-permute-start | bytes 1572872 | tf_op jit(solution)/shard_map/ppermute | solution.py:495
  147.5 13.6 %copy-start.4 = (bf16[2,2,128,512]{3,2,1,0:T(8,128)(2,1)}, bf16[2,2,128,512]{3,2,1,0:T(8,128)(2,1)S(1)}, u32[]{:S(2)}) copy-start(bf16[2,2,128,512]{3,2,1,0:T(8,128)(2,1)S(1)} %collective-permute-done.8.refs_2_) | copy-start | bytes 1572868
  151.8 9.4 %copy-start.5 = (bf16[2,2,128,512]{3,2,1,0:T(8,128)(2,1)}, bf16[2,2,128,512]{3,2,1,0:T(8,128)(2,1)S(1)}, u32[]{:S(2)}) copy-start(bf16[2,2,128,512]{3,2,1,0:T(8,128)(2,1)S(1)} %collective-permute-done.6.refs_0_) | copy-start | bytes 1572868
  161.2 0.8 copy-start.6
  164.7 12.1 %all-to-all-start.5 = ((bf16[8,2,128,128]{3,2,1,0:T(8,128)(2,1)}), bf16[8,2,128,128]{3,2,1,0:T(8,128)(2,1)S(1)}, u32[]{:S(2)}, u32[]{:S(2)}) async-start(bf16[8,2,128,128]{3,2,1,0:T(8,128)(2,1)} %total.1), calls=%async_computation.5 | async-start | bytes 1048576 | tf_op jit(solution)/shard_map/all_to_all | solution.py:499
  176.8 0.8 copy-start.3

commit v8 on v7

--- a/solution.py
+++ b/solution.py
@@ -465,27 +465,17 @@
     )(*parts)
 
 
-def unpack_kv_kernel(pair_ref, k_ref, v_ref, sems):
-    copies = []
+def unpack_kv_kernel(pair_ref, k_ref, v_ref):
     for u in range(8):
-        for i, ref in enumerate((k_ref, v_ref)):
-            target = ref.at[:, u * HD : (u + 1) * HD]
-            copies.append(pltpu.make_async_copy(pair_ref.at[u, i], target, sems.at[u, i]))
-    for copy in copies:
-        copy.start()
-    for copy in copies:
-        copy.wait()
+        k_ref[:, u * HD : (u + 1) * HD] = pair_ref[u, 0]
+        v_ref[:, u * HD : (u + 1) * HD] = pair_ref[u, 1]
 
 
 def unpack_kv(pair):
     shape = jax.ShapeDtypeStruct((TOK, 8 * HD), BF)
-    anywhere = pl.BlockSpec(memory_space=pl.ANY)
     return pl.pallas_call(
         unpack_kv_kernel,
-        in_specs=[anywhere],
-        out_specs=[anywhere, anywhere],
         out_shape=[shape, shape],
-        scratch_shapes=[pltpu.SemaphoreType.DMA((8, 2))],
         compiler_params=pltpu.CompilerParams(vmem_limit_bytes=VMEM_LIMIT),
         name="unpack_kv",
     )(pair)

time: 196 us -> 181 us (0.923)
  Pallas kernels: 79.1 us -> 64 us
    pallas_call x1, Pallas kernels: 17.1 us -> 1.97 us  [unpack_kv(): pl.pallas_call(unpack_kv_kernel, out_shape=[shape, shape], compiler_param...]
  transfers between devices with their start and end apart: 15 -> 15, of which waited for: 6 -> 6; matrix products, arithmetic and copies ran while one was open for 1% -> 1% of each run, Pallas kernels for 31% -> 33%
where the time goes in v8:
time: 181 us; the launch traced here: 180 us
  Pallas kernels  64 us (35%)
  starting transfers between devices  54.2 us (30%)
  waiting for transfers between devices  54.2 us (30%)
  local copies, waits for them, and re-layouts  5.13 us (3%)
    pallas_call x2, Pallas kernels, attend(): pl.pallas_call(kernel, in_specs=[pl.BlockSpec(memory_space=pltpu.SMEM), *...  46.3 us
    ppermute x9, waiting for transfers between devices, move(): return lax.ppermute(value, 'blk', pairs)  42.4 us
    all_to_all x6, starting transfers between devices, exchange(): return lax.all_to_all(value, 'uly', split_axis=0, concat_axis=0, tiled=True)  28.1 us
    ppermute x9, starting transfers between devices, move(): return lax.ppermute(value, 'blk', pairs)  26.1 us
    all_to_all x6, waiting for transfers between devices, exchange(): return lax.all_to_all(value, 'uly', split_axis=0, concat_axis=0, tiled=True)  11.8 us
    pallas_call x1, Pallas kernels, pack_q(): pl.pallas_call(functools.partial(pack_q_kernel, per), grid=(8 // per,), i...  5.78 us
    unnamed x18, local copies, waits for them, and re-layouts  4.23 us
  transfers between devices with their start and end apart: 15, of which 6 were waited for; matrix products, arithmetic and copies ran while one was open for 1% of the time, Pallas kernels for 33%

profile of v8, /device:TPU:0, one launch (start us, length us, event | category | flops | bytes accessed | tf_op | source)
XLA Modules:
  0.0 179.6 jit_solution(13204768124519222530)
XLA Ops:
  0.6 2.0 %pack_kv.1 = bf16[8,2,128,128]{3,2,1,0:T(8,128)(2,1)} custom-call(bf16[128,1024]{1,0:T(8,128)(2,1)} %k_ref.1, bf16[128,1024]{1,0:T(8,128)(2,1)} %v_ref.1), custom_call_target="tpu_custom_call" | custom-call | bytes 1048576 | tf_op jit(solution)/shard_map/pack_kv/pallas_call | solution.py:55
  2.6 5.7 %all-to-all-start.2 = ((bf16[8,2,128,128]{3,2,1,0:T(8,128)(2,1)}), bf16[8,2,128,128]{3,2,1,0:T(8,128)(2,1)S(1)}, u32[]{:S(2)}, u32[]{:S(2)}) async-start(bf16[8,2,128,128]{3,2,1,0:T(8,128)(2,1)} %pack_kv.1), calls=%async_computation.2 | async-start | bytes 1048576 | tf_op jit(solution)/shard_map/all_to_all | solution.py:489
  8.4 5.8 %pack_q.1 = (bf16[8,9,128,128]{3,2,1,0:T(8,128)(2,1)}, bf16[8,8,128,128]{3,2,1,0:T(8,128)(2,1)}) custom-call(bf16[128,8192]{1,0:T(8,128)(2,1)} %q_ref.1, bf16[128,8192]{1,0:T(8,128)(2,1)} %do_ref.1, bf16[128,8192]{1,0:T(8,128)(2,1)} %o_ref.1, f32[64,128]{1,0:T(8,128)} %bitcast.19, s32[128,128]{1,0:T(8,128)} %bitcast.18), custom_call_target="tpu_custom_call" | custom-call | bytes 11534336 | tf_op jit(solution)/shard_map/pack_q/pallas_call | solution.py:122
  14.2 4.3 %all-to-all-done.2.refs_3_ = bf16[8,2,128,128]{3,2,1,0:T(8,128)(2,1)S(1)} async-done(((bf16[8,2,128,128]{3,2,1,0:T(8,128)(2,1)}), bf16[8,2,128,128]{3,2,1,0:T(8,128)(2,1)S(1)}, u32[]{:S(2)}, u32[]{:S(2)}) %all-to-all-start.2) | async-done | bytes 524320 | tf_op jit(solution)/shard_map/all_to_all | solution.py:489
  18.5 3.6 %all-to-all-start = ((bf16[8,9,128,128]{3,2,1,0:T(8,128)(2,1)}), bf16[8,9,128,128]{3,2,1,0:T(8,128)(2,1)S(1)}, u32[]{:S(2)}, u32[]{:S(2)}) async-start(bf16[8,9,128,128]{3,2,1,0:T(8,128)(2,1)} %get-tuple-element.21), calls=%async_computation | async-start | bytes 4718592 | tf_op jit(solution)/shard_map/all_to_all | solution.py:489
  22.1 5.5 %collective-permute-start.1 = (bf16[8,2,128,128]{3,2,1,0:T(8,128)(2,1)S(1)}, bf16[8,2,128,128]{3,2,1,0:T(8,128)(2,1)}, u32[]{:S(2)}, u32[]{:S(2)}) collective-permute-start(bf16[8,2,128,128]{3,2,1,0:T(8,128)(2,1)S(1)} %all-to-all-done.2.refs_3_), channel_id=1, source_target_pairs={{112,0},{0,16},{16,32},{32,48},{48,64},{64,80},{80,96},{96,112},{1... | collective-permute-start | bytes 1572872 | tf_op jit(solution)/shard_map/ppermute | solution.py:485
  27.8 0.9 fusion
  28.7 1.3 collective-permute-start.3
  30.0 28.7 %collective-permute-done.1.refs_5_ = bf16[8,2,128,128]{3,2,1,0:T(8,128)(2,1)} collective-permute-done((bf16[8,2,128,128]{3,2,1,0:T(8,128)(2,1)S(1)}, bf16[8,2,128,128]{3,2,1,0:T(8,128)(2,1)}, u32[]{:S(2)}, u32[]{:S(2)}) %collective-permute-start.1) | collective-permute-done | bytes 524320 | tf_op jit(solution)/shard_map/ppermute | solution.py:485
  58.7 2.1 %collective-permute-start.4 = (bf16[8,2,128,128]{3,2,1,0:T(8,128)(2,1)}, bf16[8,2,128,128]{3,2,1,0:T(8,128)(2,1)}, u32[]{:S(2)}, u32[]{:S(2)}) collective-permute-start(bf16[8,2,128,128]{3,2,1,0:T(8,128)(2,1)} %collective-permute-done.1.refs_5_), channel_id=1, source_target_pairs={{0,8},{16,24},{32,40},{48,56},{64,72},{80,88},{96,104},{112,120},{... | collective-permute-start | bytes 1572872 | tf_op jit(solution)/shard_map/ppermute | solution.py:485
  60.8 2.1 %collective-permute-start.2 = (bf16[8,2,128,128]{3,2,1,0:T(8,128)(2,1)}, bf16[8,2,128,128]{3,2,1,0:T(8,128)(2,1)}, u32[]{:S(2)}, u32[]{:S(2)}) collective-permute-start(bf16[8,2,128,128]{3,2,1,0:T(8,128)(2,1)} %collective-permute-done.refs_4_), channel_id=1, source_target_pairs={{0,8},{16,24},{32,40},{48,56},{64,72},{80,88},{96,104},{112,120},{... | collective-permute-start | bytes 1572872 | tf_op jit(solution)/shard_map/ppermute | solution.py:485
  64.1 1.4 copy-done.2
  65.6 5.5 %all-to-all-start.1 = ((bf16[8,8,128,128]{3,2,1,0:T(8,128)(2,1)}), bf16[8,8,128,128]{3,2,1,0:T(8,128)(2,1)}, u32[]{:S(2)}, u32[]{:S(2)}) async-start(bf16[8,8,128,128]{3,2,1,0:T(8,128)(2,1)} %get-tuple-element.22), calls=%async_computation.1 | async-start | bytes 4194304 | tf_op jit(solution)/shard_map/all_to_all | solution.py:489
  71.1 22.6 %attend.2 = (bf16[8,4,128,128]{3,2,1,0:T(8,128)(2,1)}, f32[4,2,2,128,512]{4,3,2,1,0:T(8,128)}) custom-call(s32[4]{0:T(128)} %compare_select_fusion.refs_0_, bf16[8,9,128,128]{3,2,1,0:T(8,128)(2,1)} %copy-done.2, bf16[8,9,128,128]{3,2,1,0:T(8,128)(2,1)} %copy-done.2, bf16[8,2,128,128]{3,2,1,0:T(8,128)(2,1)} %copy-done.7, ...), custom_call_target="tpu_custom_call" | custom-call | flops 22817013760 | bytes 8388608 | tf_op jit(solution)/shard_map/attend/pallas_call | solution.py:359
  93.7 1.7 all-to-all-done.1.refs_1_
  95.4 4.0 %all-to-all-start.3 = ((bf16[8,4,128,128]{3,2,1,0:T(8,128)(2,1)}), bf16[8,4,128,128]{3,2,1,0:T(8,128)(2,1)S(1)}, u32[]{:S(2)}, u32[]{:S(2)}) async-start(bf16[8,4,128,128]{3,2,1,0:T(8,128)(2,1)} %get-tuple-element.26), calls=%async_computation.3 | async-start | bytes 2097152 | tf_op jit(solution)/shard_map/all_to_all | solution.py:489
  99.4 23.7 %attend.3 = (bf16[8,4,128,128]{3,2,1,0:T(8,128)(2,1)}, f32[2,2,128,512]{3,2,1,0:T(8,128)}, bf16[3,2,2,128,512]{4,3,2,1,0:T(8,128)(2,1)}, bf16[2,2,128,512]{3,2,1,0:T(8,128)(2,1)}) custom-call(s32[4]{0:T(128)} %compare_select_fusion.refs_0_, bf16[8,8,128,128]{3,2,1,0:T(8,128)(2,1)} %all-to-all-done.1.refs_1_, bf16[8,9,128,128]{3,2,1,0:T(8,128)(2,1)} %copy-done.2, ...), custom_call_target="tpu_custom_call" | custom-call | flops 22817013760 | bytes 8388608 | tf_op jit(solution)/shard_map/attend/pallas_call | solution.py:359
  123.2 1.4 collective-permute-start.5
  124.6 5.7 %all-to-all-start.4 = ((bf16[8,4,128,128]{3,2,1,0:T(8,128)(2,1)}), bf16[8,4,128,128]{3,2,1,0:T(8,128)(2,1)}, u32[]{:S(2)}, u32[]{:S(2)}) async-start(bf16[8,4,128,128]{3,2,1,0:T(8,128)(2,1)} %get-tuple-element.28), calls=%async_computation.4 | async-start | bytes 2097152 | tf_op jit(solution)/shard_map/all_to_all | solution.py:489
  130.3 5.5 %collective-permute-start.8 = (bf16[2,2,128,512]{3,2,1,0:T(8,128)(2,1)S(1)}, bf16[2,2,128,512]{3,2,1,0:T(8,128)(2,1)S(1)}, u32[]{:S(2)}, u32[]{:S(2)}) collective-permute-start(bf16[2,2,128,512]{3,2,1,0:T(8,128)(2,1)S(1)} %copy-done.8), channel_id=1, source_target_pairs={{0,104},{16,120},{32,8},{48,24},{64,40},{80,56},{96,72},{112,88},{... | collective-permute-start | bytes 1572872 | tf_op jit(solution)/shard_map/ppermute | solution.py:485
  135.9 1.2 copy-done
  137.0 2.4 %join.1 = (bf16[2,2,128,512]{3,2,1,0:T(8,128)(2,1)}, bf16[2,2,128,512]{3,2,1,0:T(8,128)(2,1)}) custom-call(bf16[3,2,2,128,512]{4,3,2,1,0:T(8,128)(2,1)} %get-tuple-element.30.mine_ref, bf16[3,2,2,128,512]{4,3,2,1,0:T(8,128)(2,1)} %copy-done, bf16[3,2,2,128,512]{4,3,2,1,0:T(8,128)(2,1)} %copy-done), custom_call_target="tpu_custom_call" | custom-call | bytes 3145728 | tf_op jit(solution)/shard_map/join/pallas_call | solution.py:404
  139.4 5.4 %collective-permute-start.6 = (bf16[2,2,128,512]{3,2,1,0:T(8,128)(2,1)}, bf16[2,2,128,512]{3,2,1,0:T(8,128)(2,1)S(1)}, u32[]{:S(2)}, u32[]{:S(2)}) collective-permute-start(bf16[2,2,128,512]{3,2,1,0:T(8,128)(2,1)} %get-tuple-element.31), channel_id=1, source_target_pairs={{0,120},{16,8},{32,24},{48,40},{64,56},{80,72},{96,88},{112,104},{... | collective-permute-start | bytes 1572872 | tf_op jit(solution)/shard_map/ppermute | solution.py:485
  144.8 2.7 %collective-permute-start.7 = (bf16[2,2,128,512]{3,2,1,0:T(8,128)(2,1)}, bf16[2,2,128,512]{3,2,1,0:T(8,128)(2,1)S(1)}, u32[]{:S(2)}, u32[]{:S(2)}) collective-permute-start(bf16[2,2,128,512]{3,2,1,0:T(8,128)(2,1)} %get-tuple-element.32), channel_id=1, source_target_pairs={{0,112},{16,0},{32,16},{48,32},{64,48},{80,64},{96,80},{112,96},{1... | collective-permute-start | bytes 1572872 | tf_op jit(solution)/shard_map/ppermute | solution.py:485
  147.6 4.3 %collective-permute-done.6.refs_0_ = bf16[2,2,128,512]{3,2,1,0:T(8,128)(2,1)S(1)} collective-permute-done((bf16[2,2,128,512]{3,2,1,0:T(8,128)(2,1)}, bf16[2,2,128,512]{3,2,1,0:T(8,128)(2,1)S(1)}, u32[]{:S(2)}, u32[]{:S(2)}) %collective-permute-start.6) | collective-permute-done | bytes 524320 | tf_op jit(solution)/shard_map/ppermute | solution.py:485
  151.8 9.4 %collective-permute-done.7.refs_1_ = bf16[2,2,128,512]{3,2,1,0:T(8,128)(2,1)S(1)} collective-permute-done((bf16[2,2,128,512]{3,2,1,0:T(8,128)(2,1)}, bf16[2,2,128,512]{3,2,1,0:T(8,128)(2,1)S(1)}, u32[]{:S(2)}, u32[]{:S(2)}) %collective-permute-start.7) | collective-permute-done | bytes 524320 | tf_op jit(solution)/shard_map/ppermute | solution.py:485
  161.2 0.8 copy-done.6
  162.0 2.7 %total.1 = bf16[8,2,128,128]{3,2,1,0:T(8,128)(2,1)} custom-call(f32[2,2,128,512]{3,2,1,0:T(8,128)} %get-tuple-element.29.own_ref, bf16[3,2,2,128,512]{4,3,2,1,0:T(8,128)(2,1)} %copy-done, bf16[2,2,128,512]{3,2,1,0:T(8,128)(2,1)} %copy-done.5, bf16[2,2,128,512]{3,2,1,0:T(8,128)(2,1)} %copy-done.6, bf16[2,2,128,512]{3,2,1,0:T(8,128)(2,1)} %copy-done.4), custom_call_target="tpu_custom_call" | custom-call | bytes 4194304 | tf_op jit(solution)/shard_map/total/pallas_call | solution.py:428
  164.7 3.5 %all-to-all-start.5 = ((bf16[8,2,128,128]{3,2,1,0:T(8,128)(2,1)}), bf16[8,2,128,128]{3,2,1,0:T(8,128)(2,1)S(1)}, u32[]{:S(2)}, u32[]{:S(2)}) async-start(bf16[8,2,128,128]{3,2,1,0:T(8,128)(2,1)} %total.1), calls=%async_computation.5 | async-start | bytes 1048576 | tf_op jit(solution)/shard_map/all_to_all | solution.py:489
  168.2 2.8 %unpack_q.1 = bf16[128,8192]{1,0:T(8,128)(2,1)} custom-call(bf16[8,4,128,128]{3,2,1,0:T(8,128)(2,1)} %copy-done.1, bf16[8,4,128,128]{3,2,1,0:T(8,128)(2,1)} %all-to-all-done.4.refs_1_), custom_call_target="tpu_custom_call" | custom-call | bytes 4194304 | tf_op jit(solution)/shard_map/unpack_q/pallas_call | solution.py:456
  171.0 5.8 %all-to-all-done.5.pair_ref = bf16[8,2,128,128]{3,2,1,0:T(8,128)(2,1)S(1)} async-done(((bf16[8,2,128,128]{3,2,1,0:T(8,128)(2,1)}), bf16[8,2,128,128]{3,2,1,0:T(8,128)(2,1)S(1)}, u32[]{:S(2)}, u32[]{:S(2)}) %all-to-all-start.5) | async-done | bytes 524320 | tf_op jit(solution)/shard_map/all_to_all | solution.py:489
  177.6 2.0 %unpack_kv.1 = (bf16[128,1024]{1,0:T(8,128)(2,1)}, bf16[128,1024]{1,0:T(8,128)(2,1)}) custom-call(bf16[8,2,128,128]{3,2,1,0:T(8,128)(2,1)} %copy-done.3), custom_call_target="tpu_custom_call" | custom-call | tf_op jit(solution)/shard_map/unpack_kv/pallas_call | solution.py:476
  (30 shorter events, 2.1 us)
Async XLA Ops:
  2.6 15.8 %all-to-all-start.2 = ((bf16[8,2,128,128]{3,2,1,0:T(8,128)(2,1)}), bf16[8,2,128,128]{3,2,1,0:T(8,128)(2,1)S(1)}, u32[]{:S(2)}, u32[]{:S(2)}) async-start(bf16[8,2,128,128]{3,2,1,0:T(8,128)(2,1)} %pack_kv.1), calls=%async_computation.2 | async-start | bytes 1048576 | tf_op jit(solution)/shard_map/all_to_all | solution.py:489
  18.5 10.2 %copy-start.7 = (bf16[8,2,128,128]{3,2,1,0:T(8,128)(2,1)}, bf16[8,2,128,128]{3,2,1,0:T(8,128)(2,1)S(1)}, u32[]{:S(2)}) copy-start(bf16[8,2,128,128]{3,2,1,0:T(8,128)(2,1)S(1)} %all-to-all-done.2.refs_3_) | copy-start | bytes 1572868
  18.5 45.7 %all-to-all-start = ((bf16[8,9,128,128]{3,2,1,0:T(8,128)(2,1)}), bf16[8,9,128,128]{3,2,1,0:T(8,128)(2,1)S(1)}, u32[]{:S(2)}, u32[]{:S(2)}) async-start(bf16[8,9,128,128]{3,2,1,0:T(8,128)(2,1)} %get-tuple-element.21), calls=%async_computation | async-start | bytes 4718592 | tf_op jit(solution)/shard_map/all_to_all | solution.py:489
  22.1 36.6 %collective-permute-start.1 = (bf16[8,2,128,128]{3,2,1,0:T(8,128)(2,1)S(1)}, bf16[8,2,128,128]{3,2,1,0:T(8,128)(2,1)}, u32[]{:S(2)}, u32[]{:S(2)}) collective-permute-start(bf16[8,2,128,128]{3,2,1,0:T(8,128)(2,1)S(1)} %all-to-all-done.2.refs_3_), channel_id=1, source_target_pairs={{112,0},{0,16},{16,32},{32,48},{48,64},{64,80},{80,96},{96,112},{1... | collective-permute-start | bytes 1572872 | tf_op jit(solution)/shard_map/ppermute | solution.py:485
  27.6 33.2 %collective-permute-start = (bf16[8,2,128,128]{3,2,1,0:T(8,128)(2,1)S(1)}, bf16[8,2,128,128]{3,2,1,0:T(8,128)(2,1)}, u32[]{:S(2)}, u32[]{:S(2)}) collective-permute-start(bf16[8,2,128,128]{3,2,1,0:T(8,128)(2,1)S(1)} %all-to-all-done.2.refs_3_), channel_id=1, source_target_pairs={{0,8},{8,16},{16,24},{24,32},{32,40},{40,48},{48,56},{56,64},{64,7... | collective-permute-start | bytes 1572872 | tf_op jit(solution)/shard_map/ppermute | solution.py:485
  28.7 42.4 %collective-permute-start.3 = (bf16[8,2,128,128]{3,2,1,0:T(8,128)(2,1)S(1)}, bf16[8,2,128,128]{3,2,1,0:T(8,128)(2,1)}, u32[]{:S(2)}, u32[]{:S(2)}) collective-permute-start(bf16[8,2,128,128]{3,2,1,0:T(8,128)(2,1)S(1)} %all-to-all-done.2.refs_3_), channel_id=1, source_target_pairs={{104,0},{120,16},{8,32},{24,48},{40,64},{56,80},{72,96},{88,112},{... | collective-permute-start | bytes 1572872 | tf_op jit(solution)/shard_map/ppermute | solution.py:485
  58.7 12.4 %collective-permute-start.4 = (bf16[8,2,128,128]{3,2,1,0:T(8,128)(2,1)}, bf16[8,2,128,128]{3,2,1,0:T(8,128)(2,1)}, u32[]{:S(2)}, u32[]{:S(2)}) collective-permute-start(bf16[8,2,128,128]{3,2,1,0:T(8,128)(2,1)} %collective-permute-done.1.refs_5_), channel_id=1, source_target_pairs={{0,8},{16,24},{32,40},{48,56},{64,72},{80,88},{96,104},{112,120},{... | collective-permute-start | bytes 1572872 | tf_op jit(solution)/shard_map/ppermute | solution.py:485
  60.8 10.3 %collective-permute-start.2 = (bf16[8,2,128,128]{3,2,1,0:T(8,128)(2,1)}, bf16[8,2,128,128]{3,2,1,0:T(8,128)(2,1)}, u32[]{:S(2)}, u32[]{:S(2)}) collective-permute-start(bf16[8,2,128,128]{3,2,1,0:T(8,128)(2,1)} %collective-permute-done.refs_4_), channel_id=1, source_target_pairs={{0,8},{16,24},{32,40},{48,56},{64,72},{80,88},{96,104},{112,120},{... | collective-permute-start | bytes 1572872 | tf_op jit(solution)/shard_map/ppermute | solution.py:485
  64.1 1.4 copy-start.2
  65.6 29.8 %all-to-all-start.1 = ((bf16[8,8,128,128]{3,2,1,0:T(8,128)(2,1)}), bf16[8,8,128,128]{3,2,1,0:T(8,128)(2,1)}, u32[]{:S(2)}, u32[]{:S(2)}) async-start(bf16[8,8,128,128]{3,2,1,0:T(8,128)(2,1)} %get-tuple-element.22), calls=%async_computation.1 | async-start | bytes 4194304 | tf_op jit(solution)/shard_map/all_to_all | solution.py:489
  95.4 27.8 %all-to-all-start.3 = ((bf16[8,4,128,128]{3,2,1,0:T(8,128)(2,1)}), bf16[8,4,128,128]{3,2,1,0:T(8,128)(2,1)S(1)}, u32[]{:S(2)}, u32[]{:S(2)}) async-start(bf16[8,4,128,128]{3,2,1,0:T(8,128)(2,1)} %get-tuple-element.26), calls=%async_computation.3 | async-start | bytes 2097152 | tf_op jit(solution)/shard_map/all_to_all | solution.py:489
  123.1 7.2 %copy-start.8 = (bf16[2,2,128,512]{3,2,1,0:T(8,128)(2,1)S(1)}, bf16[2,2,128,512]{3,2,1,0:T(8,128)(2,1)}, u32[]{:S(2)}) copy-start(bf16[2,2,128,512]{3,2,1,0:T(8,128)(2,1)} %get-tuple-element.33) | copy-start | bytes 1572868
  123.2 16.3 %copy-start.1 = (bf16[8,4,128,128]{3,2,1,0:T(8,128)(2,1)}, bf16[8,4,128,128]{3,2,1,0:T(8,128)(2,1)S(1)}, u32[]{:S(2)}) copy-start(bf16[8,4,128,128]{3,2,1,0:T(8,128)(2,1)S(1)} %all-to-all-done.3.refs_0_) | copy-start | bytes 3145732
  123.2 12.7 %collective-permute-start.5 = (bf16[3,2,2,128,512]{4,3,2,1,0:T(8,128)(2,1)}, bf16[3,2,2,128,512]{4,3,2,1,0:T(8,128)(2,1)S(1)}, u32[]{:S(2)}, u32[]{:S(2)}) collective-permute-start(bf16[3,2,2,128,512]{4,3,2,1,0:T(8,128)(2,1)} %get-tuple-element.30.mine_ref), channel_id=1, source_target_pairs={{8,0},{24,16},{40,32},{56,48},{72,64},{88,80},{104,96},{120,112},{... | collective-permute-start | bytes 4718600 | tf_op jit(solution)/shard_map/ppermute | solution.py:485
  124.6 40.1 %all-to-all-start.4 = ((bf16[8,4,128,128]{3,2,1,0:T(8,128)(2,1)}), bf16[8,4,128,128]{3,2,1,0:T(8,128)(2,1)}, u32[]{:S(2)}, u32[]{:S(2)}) async-start(bf16[8,4,128,128]{3,2,1,0:T(8,128)(2,1)} %get-tuple-element.28), calls=%async_computation.4 | async-start | bytes 2097152 | tf_op jit(solution)/shard_map/all_to_all | solution.py:489
  130.3 17.2 %collective-permute-start.8 = (bf16[2,2,128,512]{3,2,1,0:T(8,128)(2,1)S(1)}, bf16[2,2,128,512]{3,2,1,0:T(8,128)(2,1)S(1)}, u32[]{:S(2)}, u32[]{:S(2)}) collective-permute-start(bf16[2,2,128,512]{3,2,1,0:T(8,128)(2,1)S(1)} %copy-done.8), channel_id=1, source_target_pairs={{0,104},{16,120},{32,8},{48,24},{64,40},{80,56},{96,72},{112,88},{... | collective-permute-start | bytes 1572872 | tf_op jit(solution)/shard_map/ppermute | solution.py:485
  135.8 1.2 copy-start
  139.4 12.4 %collective-permute-start.6 = (bf16[2,2,128,512]{3,2,1,0:T(8,128)(2,1)}, bf16[2,2,128,512]{3,2,1,0:T(8,128)(2,1)S(1)}, u32[]{:S(2)}, u32[]{:S(2)}) collective-permute-start(bf16[2,2,128,512]{3,2,1,0:T(8,128)(2,1)} %get-tuple-element.31), channel_id=1, source_target_pairs={{0,120},{16,8},{32,24},{48,40},{64,56},{80,72},{96,88},{112,104},{... | collective-permute-start | bytes 1572872 | tf_op jit(solution)/shard_map/ppermute | solution.py:485
  144.8 16.3 %collective-permute-start.7 = (bf16[2,2,128,512]{3,2,1,0:T(8,128)(2,1)}, bf16[2,2,128,512]{3,2,1,0:T(8,128)(2,1)S(1)}, u32[]{:S(2)}, u32[]{:S(2)}) collective-permute-start(bf16[2,2,128,512]{3,2,1,0:T(8,128)(2,1)} %get-tuple-element.32), channel_id=1, source_target_pairs={{0,112},{16,0},{32,16},{48,32},{64,48},{80,64},{96,80},{112,96},{1... | collective-permute-start | bytes 1572872 | tf_op jit(solution)/shard_map/ppermute | solution.py:485
  147.5 13.6 %copy-start.4 = (bf16[2,2,128,512]{3,2,1,0:T(8,128)(2,1)}, bf16[2,2,128,512]{3,2,1,0:T(8,128)(2,1)S(1)}, u32[]{:S(2)}) copy-start(bf16[2,2,128,512]{3,2,1,0:T(8,128)(2,1)S(1)} %collective-permute-done.8.refs_2_) | copy-start | bytes 1572868
  151.8 9.4 %copy-start.5 = (bf16[2,2,128,512]{3,2,1,0:T(8,128)(2,1)}, bf16[2,2,128,512]{3,2,1,0:T(8,128)(2,1)S(1)}, u32[]{:S(2)}) copy-start(bf16[2,2,128,512]{3,2,1,0:T(8,128)(2,1)S(1)} %collective-permute-done.6.refs_0_) | copy-start | bytes 1572868
  161.2 0.8 copy-start.6
  164.7 12.1 %all-to-all-start.5 = ((bf16[8,2,128,128]{3,2,1,0:T(8,128)(2,1)}), bf16[8,2,128,128]{3,2,1,0:T(8,128)(2,1)S(1)}, u32[]{:S(2)}, u32[]{:S(2)}) async-start(bf16[8,2,128,128]{3,2,1,0:T(8,128)(2,1)} %total.1), calls=%async_computation.5 | async-start | bytes 1048576 | tf_op jit(solution)/shard_map/all_to_all | solution.py:489
  176.8 0.8 copy-start.3

commit v9 on v8

--- a/solution.py
+++ b/solution.py
@@ -527,9 +527,10 @@
 
     others, dq_early = lax.optimization_barrier((others, dq_early))
     theirs = move(others, inner_down)
-    dq_late = exchange(dq_late)
     from_three = move(far, down[3])
     to_one, to_two = join(others, theirs)
+    dq_late, to_one, to_two = lax.optimization_barrier((dq_late, to_one, to_two))
+    dq_late = exchange(dq_late)
     from_one, from_two = move(to_one, down[1]), move(to_two, down[2])
     pair = total(own, theirs, from_one, from_two, from_three)
     pair, *_ = lax.optimization_barrier((pair, dq_late))

time: 181 us -> 187 us (1.033)
  waiting for transfers between devices: 54.2 us -> 61.3 us
    ppermute x9, waiting for transfers between devices: 42.4 us -> 49.4 us  [move(): return lax.ppermute(value, 'blk', pairs)]
    unnamed x18 -> x20, local copies, waits for them, and re-layouts: 4.23 us -> 4.24 us
  transfers between devices with their start and end apart: 15 -> 15, of which waited for: 6 -> 7; matrix products, arithmetic and copies ran while one was open for 1% -> 1% of each run, Pallas kernels for 33% -> 31%
where the time goes in v9:
time: 187 us; the launch traced here: 186 us
  Pallas kernels  64 us (34%)
  waiting for transfers between devices  61.3 us (33%)
  starting transfers between devices  53.3 us (29%)
  local copies, waits for them, and re-layouts  5.14 us (3%)
    ppermute x9, waiting for transfers between devices, move(): return lax.ppermute(value, 'blk', pairs)  49.4 us
    pallas_call x2, Pallas kernels, attend(): pl.pallas_call(kernel, in_specs=[pl.BlockSpec(memory_space=pltpu.SMEM), *...  46.3 us
    all_to_all x6, starting transfers between devices, exchange(): return lax.all_to_all(value, 'uly', split_axis=0, concat_axis=0, tiled=True)  28.6 us
    ppermute x9, starting transfers between devices, move(): return lax.ppermute(value, 'blk', pairs)  24.8 us
    all_to_all x6, waiting for transfers between devices, exchange(): return lax.all_to_all(value, 'uly', split_axis=0, concat_axis=0, tiled=True)  11.9 us
    pallas_call x1, Pallas kernels, pack_q(): pl.pallas_call(functools.partial(pack_q_kernel, per), grid=(8 // per,), i...  5.78 us
    unnamed x20, local copies, waits for them, and re-layouts  4.24 us
  transfers between devices with their start and end apart: 15, of which 7 were waited for; matrix products, arithmetic and copies ran while one was open for 1% of the time, Pallas kernels for 31%

profile of v9, /device:TPU:0, one launch (start us, length us, event | category | flops | bytes accessed | tf_op | source)
XLA Modules:
  0.0 185.9 jit_solution(874324802123219385)
XLA Ops:
  0.6 2.0 %pack_kv.1 = bf16[8,2,128,128]{3,2,1,0:T(8,128)(2,1)} custom-call(bf16[128,1024]{1,0:T(8,128)(2,1)} %k_ref.1, bf16[128,1024]{1,0:T(8,128)(2,1)} %v_ref.1), custom_call_target="tpu_custom_call" | custom-call | bytes 1048576 | tf_op jit(solution)/shard_map/pack_kv/pallas_call | solution.py:55
  2.7 5.7 %all-to-all-start.2 = ((bf16[8,2,128,128]{3,2,1,0:T(8,128)(2,1)}), bf16[8,2,128,128]{3,2,1,0:T(8,128)(2,1)S(1)}, u32[]{:S(2)}, u32[]{:S(2)}) async-start(bf16[8,2,128,128]{3,2,1,0:T(8,128)(2,1)} %pack_kv.1), calls=%async_computation.2 | async-start | bytes 1048576 | tf_op jit(solution)/shard_map/all_to_all | solution.py:489
  8.4 5.8 %pack_q.1 = (bf16[8,9,128,128]{3,2,1,0:T(8,128)(2,1)}, bf16[8,8,128,128]{3,2,1,0:T(8,128)(2,1)}) custom-call(bf16[128,8192]{1,0:T(8,128)(2,1)} %q_ref.1, bf16[128,8192]{1,0:T(8,128)(2,1)} %do_ref.1, bf16[128,8192]{1,0:T(8,128)(2,1)} %o_ref.1, f32[64,128]{1,0:T(8,128)} %bitcast.19, s32[128,128]{1,0:T(8,128)} %bitcast.18), custom_call_target="tpu_custom_call" | custom-call | bytes 11534336 | tf_op jit(solution)/shard_map/pack_q/pallas_call | solution.py:122
  14.2 4.3 %all-to-all-done.2.refs_3_ = bf16[8,2,128,128]{3,2,1,0:T(8,128)(2,1)S(1)} async-done(((bf16[8,2,128,128]{3,2,1,0:T(8,128)(2,1)}), bf16[8,2,128,128]{3,2,1,0:T(8,128)(2,1)S(1)}, u32[]{:S(2)}, u32[]{:S(2)}) %all-to-all-start.2) | async-done | bytes 524320 | tf_op jit(solution)/shard_map/all_to_all | solution.py:489
  18.5 3.6 %all-to-all-start = ((bf16[8,9,128,128]{3,2,1,0:T(8,128)(2,1)}), bf16[8,9,128,128]{3,2,1,0:T(8,128)(2,1)S(1)}, u32[]{:S(2)}, u32[]{:S(2)}) async-start(bf16[8,9,128,128]{3,2,1,0:T(8,128)(2,1)} %get-tuple-element.24), calls=%async_computation | async-start | bytes 4718592 | tf_op jit(solution)/shard_map/all_to_all | solution.py:489
  22.1 5.5 %collective-permute-start.1 = (bf16[8,2,128,128]{3,2,1,0:T(8,128)(2,1)S(1)}, bf16[8,2,128,128]{3,2,1,0:T(8,128)(2,1)S(1)}, u32[]{:S(2)}, u32[]{:S(2)}) collective-permute-start(bf16[8,2,128,128]{3,2,1,0:T(8,128)(2,1)S(1)} %all-to-all-done.2.refs_3_), channel_id=1, source_target_pairs={{112,0},{0,16},{16,32},{32,48},{48,64},{64,80},{80,96},{96,112},{1... | collective-permute-start | bytes 1572872 | tf_op jit(solution)/shard_map/ppermute | solution.py:485
  27.8 0.9 fusion
  28.7 1.3 collective-permute-start.3
  30.0 28.7 %collective-permute-done.1.refs_5_ = bf16[8,2,128,128]{3,2,1,0:T(8,128)(2,1)S(1)} collective-permute-done((bf16[8,2,128,128]{3,2,1,0:T(8,128)(2,1)S(1)}, bf16[8,2,128,128]{3,2,1,0:T(8,128)(2,1)S(1)}, u32[]{:S(2)}, u32[]{:S(2)}) %collective-permute-start.1) | collective-permute-done | bytes 524320 | tf_op jit(solution)/shard_map/ppermute | solution.py:485
  58.7 2.1 %collective-permute-start.4 = (bf16[8,2,128,128]{3,2,1,0:T(8,128)(2,1)S(1)}, bf16[8,2,128,128]{3,2,1,0:T(8,128)(2,1)}, u32[]{:S(2)}, u32[]{:S(2)}) collective-permute-start(bf16[8,2,128,128]{3,2,1,0:T(8,128)(2,1)S(1)} %collective-permute-done.1.refs_5_), channel_id=1, source_target_pairs={{0,8},{16,24},{32,40},{48,56},{64,72},{80,88},{96,104},{112,120},{... | collective-permute-start | bytes 1572872 | tf_op jit(solution)/shard_map/ppermute | solution.py:485
  60.8 2.1 %collective-permute-start.2 = (bf16[8,2,128,128]{3,2,1,0:T(8,128)(2,1)}, bf16[8,2,128,128]{3,2,1,0:T(8,128)(2,1)}, u32[]{:S(2)}, u32[]{:S(2)}) collective-permute-start(bf16[8,2,128,128]{3,2,1,0:T(8,128)(2,1)} %collective-permute-done.refs_4_), channel_id=1, source_target_pairs={{0,8},{16,24},{32,40},{48,56},{64,72},{80,88},{96,104},{112,120},{... | collective-permute-start | bytes 1572872 | tf_op jit(solution)/shard_map/ppermute | solution.py:485
  64.1 1.4 copy-done.3
  65.6 5.5 %all-to-all-start.1 = ((bf16[8,8,128,128]{3,2,1,0:T(8,128)(2,1)}), bf16[8,8,128,128]{3,2,1,0:T(8,128)(2,1)}, u32[]{:S(2)}, u32[]{:S(2)}) async-start(bf16[8,8,128,128]{3,2,1,0:T(8,128)(2,1)} %get-tuple-element.25), calls=%async_computation.1 | async-start | bytes 4194304 | tf_op jit(solution)/shard_map/all_to_all | solution.py:489
  71.1 22.6 %attend.2 = (bf16[8,4,128,128]{3,2,1,0:T(8,128)(2,1)}, f32[4,2,2,128,512]{4,3,2,1,0:T(8,128)}) custom-call(s32[4]{0:T(128)} %compare_select_fusion.refs_0_, bf16[8,9,128,128]{3,2,1,0:T(8,128)(2,1)} %copy-done.3, bf16[8,9,128,128]{3,2,1,0:T(8,128)(2,1)} %copy-done.3, bf16[8,2,128,128]{3,2,1,0:T(8,128)(2,1)} %copy-done.8, ...), custom_call_target="tpu_custom_call" | custom-call | flops 22817013760 | bytes 8388608 | tf_op jit(solution)/shard_map/attend/pallas_call | solution.py:359
  93.7 1.7 all-to-all-done.1.refs_1_
  95.4 4.0 %all-to-all-start.3 = ((bf16[8,4,128,128]{3,2,1,0:T(8,128)(2,1)}), bf16[8,4,128,128]{3,2,1,0:T(8,128)(2,1)S(1)}, u32[]{:S(2)}, u32[]{:S(2)}) async-start(bf16[8,4,128,128]{3,2,1,0:T(8,128)(2,1)} %get-tuple-element.29), calls=%async_computation.3 | async-start | bytes 2097152 | tf_op jit(solution)/shard_map/all_to_all | solution.py:489
  99.4 23.7 %attend.3 = (bf16[8,4,128,128]{3,2,1,0:T(8,128)(2,1)}, f32[2,2,128,512]{3,2,1,0:T(8,128)}, bf16[3,2,2,128,512]{4,3,2,1,0:T(8,128)(2,1)}, bf16[2,2,128,512]{3,2,1,0:T(8,128)(2,1)}) custom-call(s32[4]{0:T(128)} %compare_select_fusion.refs_0_, bf16[8,8,128,128]{3,2,1,0:T(8,128)(2,1)} %all-to-all-done.1.refs_1_, bf16[8,9,128,128]{3,2,1,0:T(8,128)(2,1)} %copy-done.3, ...), custom_call_target="tpu_custom_call" | custom-call | flops 22817013760 | bytes 8388608 | tf_op jit(solution)/shard_map/attend/pallas_call | solution.py:359
  123.2 1.3 collective-permute-start.5
  124.5 4.2 %collective-permute-done.5.inner_two_ref.inner_three_ref.theirs_ref = bf16[3,2,2,128,512]{4,3,2,1,0:T(8,128)(2,1)S(1)} collective-permute-done((bf16[3,2,2,128,512]{4,3,2,1,0:T(8,128)(2,1)}, bf16[3,2,2,128,512]{4,3,2,1,0:T(8,128)(2,1)S(1)}, u32[]{:S(2)}, u32[]{:S(2)}) %collective-permute-start.5) | collective-permute-done | bytes 1572896 | tf_op jit(solution)/shard_map/ppermute | solution.py:485
  128.7 1.2 copy-done
  129.9 2.4 %join.1 = (bf16[2,2,128,512]{3,2,1,0:T(8,128)(2,1)}, bf16[2,2,128,512]{3,2,1,0:T(8,128)(2,1)}) custom-call(bf16[3,2,2,128,512]{4,3,2,1,0:T(8,128)(2,1)} %get-tuple-element.32.mine_ref, bf16[3,2,2,128,512]{4,3,2,1,0:T(8,128)(2,1)} %copy-done, bf16[3,2,2,128,512]{4,3,2,1,0:T(8,128)(2,1)} %copy-done), custom_call_target="tpu_custom_call" | custom-call | bytes 3145728 | tf_op jit(solution)/shard_map/join/pallas_call | solution.py:404
  132.2 5.7 %all-to-all-start.4 = ((bf16[8,4,128,128]{3,2,1,0:T(8,128)(2,1)}), bf16[8,4,128,128]{3,2,1,0:T(8,128)(2,1)S(1)}, u32[]{:S(2)}, u32[]{:S(2)}) async-start(bf16[8,4,128,128]{3,2,1,0:T(8,128)(2,1)} %get-tuple-element.35), calls=%async_computation.4 | async-start | bytes 2097152 | tf_op jit(solution)/shard_map/all_to_all | solution.py:489
  137.9 4.4 %collective-permute-start.8 = (bf16[2,2,128,512]{3,2,1,0:T(8,128)(2,1)}, bf16[2,2,128,512]{3,2,1,0:T(8,128)(2,1)S(1)}, u32[]{:S(2)}, u32[]{:S(2)}) collective-permute-start(bf16[2,2,128,512]{3,2,1,0:T(8,128)(2,1)} %get-tuple-element.39), channel_id=1, source_target_pairs={{0,104},{16,120},{32,8},{48,24},{64,40},{80,56},{96,72},{112,88},{... | collective-permute-start | bytes 1572872 | tf_op jit(solution)/shard_map/ppermute | solution.py:485
  142.4 5.3 %collective-permute-start.6 = (bf16[2,2,128,512]{3,2,1,0:T(8,128)(2,1)}, bf16[2,2,128,512]{3,2,1,0:T(8,128)(2,1)S(1)}, u32[]{:S(2)}, u32[]{:S(2)}) collective-permute-start(bf16[2,2,128,512]{3,2,1,0:T(8,128)(2,1)} %get-tuple-element.37), channel_id=1, source_target_pairs={{0,120},{16,8},{32,24},{48,40},{64,56},{80,72},{96,88},{112,104},{... | collective-permute-start | bytes 1572872 | tf_op jit(solution)/shard_map/ppermute | solution.py:485
  147.7 2.7 %collective-permute-start.7 = (bf16[2,2,128,512]{3,2,1,0:T(8,128)(2,1)}, bf16[2,2,128,512]{3,2,1,0:T(8,128)(2,1)S(1)}, u32[]{:S(2)}, u32[]{:S(2)}) collective-permute-start(bf16[2,2,128,512]{3,2,1,0:T(8,128)(2,1)} %get-tuple-element.38), channel_id=1, source_target_pairs={{0,112},{16,0},{32,16},{48,32},{64,48},{80,64},{96,80},{112,96},{1... | collective-permute-start | bytes 1572872 | tf_op jit(solution)/shard_map/ppermute | solution.py:485
  150.4 7.3 %collective-permute-done.6.refs_0_ = bf16[2,2,128,512]{3,2,1,0:T(8,128)(2,1)S(1)} collective-permute-done((bf16[2,2,128,512]{3,2,1,0:T(8,128)(2,1)}, bf16[2,2,128,512]{3,2,1,0:T(8,128)(2,1)S(1)}, u32[]{:S(2)}, u32[]{:S(2)}) %collective-permute-start.6) | collective-permute-done | bytes 524320 | tf_op jit(solution)/shard_map/ppermute | solution.py:485
  157.7 9.2 %collective-permute-done.7.refs_1_ = bf16[2,2,128,512]{3,2,1,0:T(8,128)(2,1)S(1)} collective-permute-done((bf16[2,2,128,512]{3,2,1,0:T(8,128)(2,1)}, bf16[2,2,128,512]{3,2,1,0:T(8,128)(2,1)S(1)}, u32[]{:S(2)}, u32[]{:S(2)}) %collective-permute-start.7) | collective-permute-done | bytes 524320 | tf_op jit(solution)/shard_map/ppermute | solution.py:485
  167.7 2.7 %total.1 = bf16[8,2,128,128]{3,2,1,0:T(8,128)(2,1)} custom-call(f32[2,2,128,512]{3,2,1,0:T(8,128)} %get-tuple-element.36.own_ref, bf16[3,2,2,128,512]{4,3,2,1,0:T(8,128)(2,1)} %copy-done, bf16[2,2,128,512]{3,2,1,0:T(8,128)(2,1)} %copy-done.6, bf16[2,2,128,512]{3,2,1,0:T(8,128)(2,1)} %copy-done.7, bf16[2,2,128,512]{3,2,1,0:T(8,128)(2,1)} %copy-done.5), custom_call_target="tpu_custom_call" | custom-call | bytes 4194304 | tf_op jit(solution)/shard_map/total/pallas_call | solution.py:428
  170.5 3.9 %all-to-all-start.5 = ((bf16[8,2,128,128]{3,2,1,0:T(8,128)(2,1)}), bf16[8,2,128,128]{3,2,1,0:T(8,128)(2,1)S(1)}, u32[]{:S(2)}, u32[]{:S(2)}) async-start(bf16[8,2,128,128]{3,2,1,0:T(8,128)(2,1)} %total.1), calls=%async_computation.5 | async-start | bytes 1048576 | tf_op jit(solution)/shard_map/all_to_all | solution.py:489
  174.4 2.8 %unpack_q.1 = bf16[128,8192]{1,0:T(8,128)(2,1)} custom-call(bf16[8,4,128,128]{3,2,1,0:T(8,128)(2,1)} %copy-done.1, bf16[8,4,128,128]{3,2,1,0:T(8,128)(2,1)} %copy-done.2), custom_call_target="tpu_custom_call" | custom-call | bytes 4194304 | tf_op jit(solution)/shard_map/unpack_q/pallas_call | solution.py:456
  177.2 5.9 %all-to-all-done.5.pair_ref = bf16[8,2,128,128]{3,2,1,0:T(8,128)(2,1)S(1)} async-done(((bf16[8,2,128,128]{3,2,1,0:T(8,128)(2,1)}), bf16[8,2,128,128]{3,2,1,0:T(8,128)(2,1)S(1)}, u32[]{:S(2)}, u32[]{:S(2)}) %all-to-all-start.5) | async-done | bytes 524320 | tf_op jit(solution)/shard_map/all_to_all | solution.py:489
  183.9 2.0 %unpack_kv.1 = (bf16[128,1024]{1,0:T(8,128)(2,1)}, bf16[128,1024]{1,0:T(8,128)(2,1)}) custom-call(bf16[8,2,128,128]{3,2,1,0:T(8,128)(2,1)} %copy-done.4), custom_call_target="tpu_custom_call" | custom-call | tf_op jit(solution)/shard_map/unpack_kv/pallas_call | solution.py:476
  (32 shorter events, 2.9 us)
Async XLA Ops:
  2.7 15.8 %all-to-all-start.2 = ((bf16[8,2,128,128]{3,2,1,0:T(8,128)(2,1)}), bf16[8,2,128,128]{3,2,1,0:T(8,128)(2,1)S(1)}, u32[]{:S(2)}, u32[]{:S(2)}) async-start(bf16[8,2,128,128]{3,2,1,0:T(8,128)(2,1)} %pack_kv.1), calls=%async_computation.2 | async-start | bytes 1048576 | tf_op jit(solution)/shard_map/all_to_all | solution.py:489
  18.5 10.2 %copy-start.8 = (bf16[8,2,128,128]{3,2,1,0:T(8,128)(2,1)}, bf16[8,2,128,128]{3,2,1,0:T(8,128)(2,1)S(1)}, u32[]{:S(2)}) copy-start(bf16[8,2,128,128]{3,2,1,0:T(8,128)(2,1)S(1)} %all-to-all-done.2.refs_3_) | copy-start | bytes 1572868
  18.5 45.7 %all-to-all-start = ((bf16[8,9,128,128]{3,2,1,0:T(8,128)(2,1)}), bf16[8,9,128,128]{3,2,1,0:T(8,128)(2,1)S(1)}, u32[]{:S(2)}, u32[]{:S(2)}) async-start(bf16[8,9,128,128]{3,2,1,0:T(8,128)(2,1)} %get-tuple-element.24), calls=%async_computation | async-start | bytes 4718592 | tf_op jit(solution)/shard_map/all_to_all | solution.py:489
  22.1 36.6 %collective-permute-start.1 = (bf16[8,2,128,128]{3,2,1,0:T(8,128)(2,1)S(1)}, bf16[8,2,128,128]{3,2,1,0:T(8,128)(2,1)S(1)}, u32[]{:S(2)}, u32[]{:S(2)}) collective-permute-start(bf16[8,2,128,128]{3,2,1,0:T(8,128)(2,1)S(1)} %all-to-all-done.2.refs_3_), channel_id=1, source_target_pairs={{112,0},{0,16},{16,32},{32,48},{48,64},{64,80},{80,96},{96,112},{1... | collective-permute-start | bytes 1572872 | tf_op jit(solution)/shard_map/ppermute | solution.py:485
  27.6 33.2 %collective-permute-start = (bf16[8,2,128,128]{3,2,1,0:T(8,128)(2,1)S(1)}, bf16[8,2,128,128]{3,2,1,0:T(8,128)(2,1)}, u32[]{:S(2)}, u32[]{:S(2)}) collective-permute-start(bf16[8,2,128,128]{3,2,1,0:T(8,128)(2,1)S(1)} %all-to-all-done.2.refs_3_), channel_id=1, source_target_pairs={{0,8},{8,16},{16,24},{24,32},{32,40},{40,48},{48,56},{56,64},{64,7... | collective-permute-start | bytes 1572872 | tf_op jit(solution)/shard_map/ppermute | solution.py:485
  28.7 42.4 %collective-permute-start.3 = (bf16[8,2,128,128]{3,2,1,0:T(8,128)(2,1)S(1)}, bf16[8,2,128,128]{3,2,1,0:T(8,128)(2,1)}, u32[]{:S(2)}, u32[]{:S(2)}) collective-permute-start(bf16[8,2,128,128]{3,2,1,0:T(8,128)(2,1)S(1)} %all-to-all-done.2.refs_3_), channel_id=1, source_target_pairs={{104,0},{120,16},{8,32},{24,48},{40,64},{56,80},{72,96},{88,112},{... | collective-permute-start | bytes 1572872 | tf_op jit(solution)/shard_map/ppermute | solution.py:485
  58.7 5.4 %copy-start.9 = (bf16[8,2,128,128]{3,2,1,0:T(8,128)(2,1)}, bf16[8,2,128,128]{3,2,1,0:T(8,128)(2,1)S(1)}, u32[]{:S(2)}) copy-start(bf16[8,2,128,128]{3,2,1,0:T(8,128)(2,1)S(1)} %collective-permute-done.1.refs_5_) | copy-start | bytes 1572868
  58.7 12.4 %collective-permute-start.4 = (bf16[8,2,128,128]{3,2,1,0:T(8,128)(2,1)S(1)}, bf16[8,2,128,128]{3,2,1,0:T(8,128)(2,1)}, u32[]{:S(2)}, u32[]{:S(2)}) collective-permute-start(bf16[8,2,128,128]{3,2,1,0:T(8,128)(2,1)S(1)} %collective-permute-done.1.refs_5_), channel_id=1, source_target_pairs={{0,8},{16,24},{32,40},{48,56},{64,72},{80,88},{96,104},{112,120},{... | collective-permute-start | bytes 1572872 | tf_op jit(solution)/shard_map/ppermute | solution.py:485
  60.8 10.3 %collective-permute-start.2 = (bf16[8,2,128,128]{3,2,1,0:T(8,128)(2,1)}, bf16[8,2,128,128]{3,2,1,0:T(8,128)(2,1)}, u32[]{:S(2)}, u32[]{:S(2)}) collective-permute-start(bf16[8,2,128,128]{3,2,1,0:T(8,128)(2,1)} %collective-permute-done.refs_4_), channel_id=1, source_target_pairs={{0,8},{16,24},{32,40},{48,56},{64,72},{80,88},{96,104},{112,120},{... | collective-permute-start | bytes 1572872 | tf_op jit(solution)/shard_map/ppermute | solution.py:485
  64.1 1.4 copy-start.3
  65.6 29.8 %all-to-all-start.1 = ((bf16[8,8,128,128]{3,2,1,0:T(8,128)(2,1)}), bf16[8,8,128,128]{3,2,1,0:T(8,128)(2,1)}, u32[]{:S(2)}, u32[]{:S(2)}) async-start(bf16[8,8,128,128]{3,2,1,0:T(8,128)(2,1)} %get-tuple-element.25), calls=%async_computation.1 | async-start | bytes 4194304 | tf_op jit(solution)/shard_map/all_to_all | solution.py:489
  95.4 27.8 %all-to-all-start.3 = ((bf16[8,4,128,128]{3,2,1,0:T(8,128)(2,1)}), bf16[8,4,128,128]{3,2,1,0:T(8,128)(2,1)S(1)}, u32[]{:S(2)}, u32[]{:S(2)}) async-start(bf16[8,4,128,128]{3,2,1,0:T(8,128)(2,1)} %get-tuple-element.29), calls=%async_computation.3 | async-start | bytes 2097152 | tf_op jit(solution)/shard_map/all_to_all | solution.py:489
  123.2 47.3 %copy-start.1 = (bf16[8,4,128,128]{3,2,1,0:T(8,128)(2,1)}, bf16[8,4,128,128]{3,2,1,0:T(8,128)(2,1)S(1)}, u32[]{:S(2)}) copy-start(bf16[8,4,128,128]{3,2,1,0:T(8,128)(2,1)S(1)} %all-to-all-done.3.refs_0_) | copy-start | bytes 3145732
  123.2 5.5 %collective-permute-start.5 = (bf16[3,2,2,128,512]{4,3,2,1,0:T(8,128)(2,1)}, bf16[3,2,2,128,512]{4,3,2,1,0:T(8,128)(2,1)S(1)}, u32[]{:S(2)}, u32[]{:S(2)}) collective-permute-start(bf16[3,2,2,128,512]{4,3,2,1,0:T(8,128)(2,1)} %get-tuple-element.32.mine_ref), channel_id=1, source_target_pairs={{8,0},{24,16},{40,32},{56,48},{72,64},{88,80},{104,96},{120,112},{... | collective-permute-start | bytes 4718600 | tf_op jit(solution)/shard_map/ppermute | solution.py:485
  128.7 1.2 copy-start
  132.2 38.2 %all-to-all-start.4 = ((bf16[8,4,128,128]{3,2,1,0:T(8,128)(2,1)}), bf16[8,4,128,128]{3,2,1,0:T(8,128)(2,1)S(1)}, u32[]{:S(2)}, u32[]{:S(2)}) async-start(bf16[8,4,128,128]{3,2,1,0:T(8,128)(2,1)} %get-tuple-element.35), calls=%async_computation.4 | async-start | bytes 2097152 | tf_op jit(solution)/shard_map/all_to_all | solution.py:489
  137.9 12.4 %collective-permute-start.8 = (bf16[2,2,128,512]{3,2,1,0:T(8,128)(2,1)}, bf16[2,2,128,512]{3,2,1,0:T(8,128)(2,1)S(1)}, u32[]{:S(2)}, u32[]{:S(2)}) collective-permute-start(bf16[2,2,128,512]{3,2,1,0:T(8,128)(2,1)} %get-tuple-element.39), channel_id=1, source_target_pairs={{0,104},{16,120},{32,8},{48,24},{64,40},{80,56},{96,72},{112,88},{... | collective-permute-start | bytes 1572872 | tf_op jit(solution)/shard_map/ppermute | solution.py:485
  142.4 15.3 %collective-permute-start.6 = (bf16[2,2,128,512]{3,2,1,0:T(8,128)(2,1)}, bf16[2,2,128,512]{3,2,1,0:T(8,128)(2,1)S(1)}, u32[]{:S(2)}, u32[]{:S(2)}) collective-permute-start(bf16[2,2,128,512]{3,2,1,0:T(8,128)(2,1)} %get-tuple-element.37), channel_id=1, source_target_pairs={{0,120},{16,8},{32,24},{48,40},{64,56},{80,72},{96,88},{112,104},{... | collective-permute-start | bytes 1572872 | tf_op jit(solution)/shard_map/ppermute | solution.py:485
  147.7 19.2 %collective-permute-start.7 = (bf16[2,2,128,512]{3,2,1,0:T(8,128)(2,1)}, bf16[2,2,128,512]{3,2,1,0:T(8,128)(2,1)S(1)}, u32[]{:S(2)}, u32[]{:S(2)}) collective-permute-start(bf16[2,2,128,512]{3,2,1,0:T(8,128)(2,1)} %get-tuple-element.38), channel_id=1, source_target_pairs={{0,112},{16,0},{32,16},{48,32},{64,48},{80,64},{96,80},{112,96},{1... | collective-permute-start | bytes 1572872 | tf_op jit(solution)/shard_map/ppermute | solution.py:485
  150.4 16.5 %copy-start.5 = (bf16[2,2,128,512]{3,2,1,0:T(8,128)(2,1)}, bf16[2,2,128,512]{3,2,1,0:T(8,128)(2,1)S(1)}, u32[]{:S(2)}) copy-start(bf16[2,2,128,512]{3,2,1,0:T(8,128)(2,1)S(1)} %collective-permute-done.8.refs_2_) | copy-start | bytes 1572868
  157.7 9.2 %copy-start.6 = (bf16[2,2,128,512]{3,2,1,0:T(8,128)(2,1)}, bf16[2,2,128,512]{3,2,1,0:T(8,128)(2,1)S(1)}, u32[]{:S(2)}) copy-start(bf16[2,2,128,512]{3,2,1,0:T(8,128)(2,1)S(1)} %collective-permute-done.6.refs_0_) | copy-start | bytes 1572868
  166.9 0.8 copy-start.7
  170.4 4.0 %copy-start.2 = (bf16[8,4,128,128]{3,2,1,0:T(8,128)(2,1)}, bf16[8,4,128,128]{3,2,1,0:T(8,128)(2,1)S(1)}, u32[]{:S(2)}) copy-start(bf16[8,4,128,128]{3,2,1,0:T(8,128)(2,1)S(1)} %all-to-all-done.4.refs_1_) | copy-start | bytes 3145732
  170.5 12.6 %all-to-all-start.5 = ((bf16[8,2,128,128]{3,2,1,0:T(8,128)(2,1)}), bf16[8,2,128,128]{3,2,1,0:T(8,128)(2,1)S(1)}, u32[]{:S(2)}, u32[]{:S(2)}) async-start(bf16[8,2,128,128]{3,2,1,0:T(8,128)(2,1)} %total.1), calls=%async_computation.5 | async-start | bytes 1048576 | tf_op jit(solution)/shard_map/all_to_all | solution.py:489
  183.1 0.8 copy-start.4
